TPU v7x, 512 devices: a whole 4x8x8 slice. The times are simulated.
512 devices in a mesh: user: 16 (over y, core), dev: 32 (over z, x).
Axes of the slice: x: 4, y: 8, z: 8, core: 2. Of those that a mesh axis runs over, the one named last changes fastest.
Arguments:
- queries: bfloat16 [16384, 2048], P(('user', 'dev')), parts along dimension 0, may hold values from -9 to 9
- keys: bfloat16 [64, 256, 2048], P('user', 'dev'), parts along dimension 0, may hold values from -9 to 9
- values: bfloat16 [64, 256, 2048], P('user', 'dev'), parts along dimension 0, may hold values from -24 to 24
- kv_count: int32 [64, 32], P('user'), parts along dimension 0, may hold values from 1 to 8, 192 in all within a row
- beam_user: int32 [512], P('user'), parts along dimension 0, may hold values from 0 to 3, as said below
- routes: int32 [16384, 2], P(('user', 'dev')), parts along dimension 0, may hold values from 0 to 31, as said below
- route_gate: float32 [16384, 2], P(('user', 'dev')), parts along dimension 0, may hold values from 0.2 to 1
- norm_gain: float32 [2048], replicated, may hold values from 0.1 to 1.9
- w_up: bfloat16 [2048, 16384], P(None, 'dev'), may hold values from -0.125 to 0.125
- w_down: bfloat16 [16384, 2048], P('dev'), may hold values from -0.0625 to 0.0625
Outputs:
- context: bfloat16 [16384, 2048], P(('user', 'dev')), parts along dimension 0
- routed: bfloat16 [16384, 2048], P(('user', 'dev')), parts along dimension 0
There are 16 independent parts, one for each index of `user`. A program takes and returns all parts, laid end to end along the dimension named above; an argument that names none is the same for every part. Nothing has to cross between parts.
Inputs may be any that keep to these rules, and one draw needn't show every extreme that they name: `beam_user`: each user owns the beams of exactly 8 devices. `routes`: each row names two different experts. On the rows of one device each expert 0 to 1 is named at most 16 times, and on every device one of them exactly 16 times.
All inputs are finite; a program needn't handle non-finite values.
Results may differ from a plain program's by a relative error of at most 0.012.
Values may be sent and summed in bfloat16 or wider, within the bound.
No kernel may reach another device: no remote copies, remote signals or barrier semaphores. Data moves between devices by JAX's collectives and lax.ppermute only.
A program may use at most 64 MiB of HBM per device.

v0:
```python
import jax
import jax.numpy as jnp
from jax import lax
from jax.sharding import PartitionSpec as P

HEAD = 128
EXPF = 2
TOPK = 2
CAP = 16


def on_device(
    queries, keys, values, kv_count, beam_user, routes, route_gate, norm_gain, w_up, w_down
):
    count = lax.axis_size("dev")
    myself = lax.axis_index("dev")
    beams = queries.shape[0]
    width = queries.shape[1]
    heads = width // HEAD
    shard_len = keys.shape[1]
    outgoing_keys = jnp.take(keys, beam_user, axis=0)
    outgoing_values = jnp.take(values, beam_user, axis=0)
    got_keys, got_values = (
        lax.all_to_all(outgoing_keys, "dev", split_axis=0, concat_axis=0, tiled=True),
        lax.all_to_all(outgoing_values, "dev", split_axis=0, concat_axis=0, tiled=True),
    )
    owner_user = beam_user[myself]
    counts_row = kv_count[owner_user]
    valid = (jnp.arange(shard_len)[None, :] < counts_row[:, None]).reshape(-1)
    user_keys = got_keys.reshape(count * shard_len, heads, HEAD)
    user_values = got_values.reshape(count * shard_len, heads, HEAD)
    query_rows = queries.reshape(beams, heads, HEAD)
    scores = jnp.einsum(
        "bhd,lhd->hbl", query_rows, user_keys, preferred_element_type=jnp.float32
    ) * HEAD ** (-0.5)
    scores = jnp.where(valid[None, None, :], scores, -1e30)
    top = jnp.max(scores, axis=-1, keepdims=True)
    expo = jnp.exp(scores - top)
    total = jnp.sum(expo, axis=-1, keepdims=True)
    weights = (expo / total).astype(jnp.bfloat16)
    mixed = jnp.einsum("hbl,lhd->bhd", weights, user_values, preferred_element_type=jnp.float32)
    context = mixed.reshape(beams, width).astype(jnp.bfloat16)
    rows_f = queries.astype(jnp.float32)
    mean_sq = jnp.mean(rows_f * rows_f, axis=-1, keepdims=True)
    normed = (rows_f * lax.rsqrt(mean_sq + 1e-06) * norm_gain[None, :]).astype(jnp.bfloat16)
    flat_routes = routes.reshape(-1)
    flat_gate = route_gate.reshape(-1)
    hits = flat_routes[None, :] == jnp.arange(EXPF)[:, None]
    slot_of = jnp.cumsum(hits.astype(jnp.int32), axis=1) - 1
    placed = hits[:, None, :] & (slot_of[:, None, :] == jnp.arange(CAP)[None, :, None])
    placed_f = placed.astype(jnp.float32).reshape(EXPF, CAP, beams, TOPK)
    picker = jnp.sum(placed_f, axis=-1).reshape(EXPF * CAP, beams).astype(jnp.bfloat16)
    packed = jnp.dot(picker, normed, preferred_element_type=jnp.float32).astype(jnp.bfloat16)
    packed = packed.reshape(EXPF, CAP, width)
    group = count // EXPF
    outgoing = jnp.repeat(packed, group, axis=0)
    hidden = jax.nn.silu(
        jnp.einsum(
            "scd,dh->sch",
            lax.all_to_all(outgoing, "dev", split_axis=0, concat_axis=0, tiled=True),
            w_up,
            preferred_element_type=jnp.float32,
        )
    ).astype(jnp.bfloat16)
    partial_out = jnp.einsum("sch,hd->scd", hidden, w_down, preferred_element_type=jnp.float32)
    returned = lax.all_to_all(
        partial_out.astype(jnp.bfloat16), "dev", split_axis=0, concat_axis=0, tiled=True
    ).astype(partial_out.dtype)
    summed = jnp.sum(returned.reshape(EXPF, group, CAP, width), axis=1)
    gate_pick = jnp.einsum(
        "ecrk,rk->rec", placed_f, flat_gate.reshape(beams, TOPK), precision=lax.Precision.HIGHEST
    )
    routed = jnp.dot(
        gate_pick.reshape(beams, EXPF * CAP),
        summed.reshape(EXPF * CAP, width),
        precision=lax.Precision.HIGHEST,
    )
    return (context, routed.astype(jnp.bfloat16))


def solution(mesh):
    return jax.shard_map(
        on_device,
        mesh=mesh,
        in_specs=(
            P(("user", "dev"), None),
            P("user", "dev", None),
            P("user", "dev", None),
            P("user", None),
            P("user"),
            P(("user", "dev"), None),
            P(("user", "dev"), None),
            P(),
            P(None, "dev"),
            P("dev", None),
        ),
        out_specs=(P(("user", "dev"), None), P(("user", "dev"), None)),
        check_vma=False,
    )
```

profile of v0, /device:TPU:36, one launch (start us, length us, event | category | flops | bytes accessed | tf_op | source)
XLA Modules:
  0.0 193.9 jit_solution(4303290667410414005)
XLA Ops:
  0.7 0.8 compare_select_fusion
  1.5 0.7 compare_and_fusion
  2.2 1.5 gather_fusion
  3.7 1.6 gather_fusion.1
  5.3 2.8 %broadcast_select_fusion = (bf16[32,8,2048]{2,1,0:T(8,128)(2,1)}, bf16[32,8,2048]{2,1,0:T(8,128)(2,1)}) fusion(bf16[32,8,2048]{2,1,0:T(8,128)(2,1)} %gather_fusion.1, pred[32]{0:T(512)(128)(4,1)S(1)} %compare_and_fusion, bf16[32,8,2048]{2,1,0:T(8,128)(2,1)S(1)} %gather_fusion), kind=kLoop, calls=%fused_computation.21 | loop fusion | flops 1048576 | bytes 4194336 | tf_op jit(solution)/shard_map/jit(_take)/select_n | solution.py:21
  8.1 13.6 %all-to-all-start.1 = ((bf16[32,8,2048]{2,1,0:T(8,128)(2,1)}), bf16[32,8,2048]{2,1,0:T(8,128)(2,1)S(1)}, u32[]{:S(2)}, u32[]{:S(2)}) async-start(bf16[32,8,2048]{2,1,0:T(8,128)(2,1)} %get-tuple-element.3), calls=%async_computation.1 | async-start | bytes 2097152 | tf_op jit(solution)/shard_map/all_to_all | solution.py:24
  21.9 0.5 reduce_window_sum.11
  23.0 26.7 %all-to-all-done.1 = bf16[32,8,2048]{2,1,0:T(8,128)(2,1)S(1)} async-done(((bf16[32,8,2048]{2,1,0:T(8,128)(2,1)}), bf16[32,8,2048]{2,1,0:T(8,128)(2,1)S(1)}, u32[]{:S(2)}, u32[]{:S(2)}) %all-to-all-start.1) | async-done | bytes 1048608 | tf_op jit(solution)/shard_map/all_to_all | solution.py:24
  49.7 0.2 broadcast_in_dim.35
  50.0 54.9 %all_to_all.20 = bf16[32,16,2048]{2,1,0:T(8,128)(2,1)} all-to-all(bf16[32,16,2048]{2,1,0:T(8,128)(2,1)S(1)} %bitcast.54), channel_id=1, replica_groups=mesh['user'=16,'dev'=32] {'dev'}, dimensions={0} | all-to-all | bytes 4194304 | tf_op jit(solution)/shard_map/all_to_all | solution.py:60
  104.9 5.6 %all-to-all-start = ((bf16[32,8,2048]{2,1,0:T(8,128)(2,1)}), bf16[32,8,2048]{2,1,0:T(8,128)(2,1)}, u32[]{:S(2)}, u32[]{:S(2)}) async-start(bf16[32,8,2048]{2,1,0:T(8,128)(2,1)} %get-tuple-element.4), calls=%async_computation | async-start | bytes 2097152 | tf_op jit(solution)/shard_map/all_to_all | solution.py:25
  110.5 6.1 %convolution_convert_fusion = bf16[32,16,2048]{2,1,0:T(8,128)(2,1)} fusion(bf16[512,2048]{1,0:T(8,128)(2,1)S(1)} %copy-done, bf16[32,16,2048]{2,1,0:T(8,128)(2,1)} %all_to_all.20, bf16[2048,512]{1,0:T(8,128)(2,1)} %param.20), kind=kOutput, calls=%fused_computation.4 | convolution fusion | flops 2149842944 | bytes 8388608 | tf_op jit(solution)/shard_map/sch,hd->scd/dot_general | solution.py:65
  116.6 20.5 %all-to-all-done = bf16[32,8,2048]{2,1,0:T(8,128)(2,1)} async-done(((bf16[32,8,2048]{2,1,0:T(8,128)(2,1)}), bf16[32,8,2048]{2,1,0:T(8,128)(2,1)}, u32[]{:S(2)}, u32[]{:S(2)}) %all-to-all-start) | async-done | bytes 1048608 | tf_op jit(solution)/shard_map/all_to_all | solution.py:25
  137.1 5.6 %all-to-all-start.3 = ((bf16[32,16,2048]{2,1,0:T(8,128)(2,1)}), bf16[32,16,2048]{2,1,0:T(8,128)(2,1)}, u32[]{:S(2)}, u32[]{:S(2)}) async-start(bf16[32,16,2048]{2,1,0:T(8,128)(2,1)} %convolution_convert_fusion), calls=%async_computation.3 | async-start | bytes 4194304 | tf_op jit(solution)/shard_map/all_to_all | solution.py:66
  142.8 0.6 dynamic_slice.6
  145.3 0.7 dynamic-slice_bitcast_fusion
  146.4 1.5 copy.36
  147.9 0.5 fusion.7
  148.4 0.8 copy-done.2
  149.4 2.2 %fusion.9 = bf16[16,4,8,128]{3,2,1,0:T(8,128)(2,1)S(1)} fusion(bf16[256,16,128]{2,1,0:T(8,128)(2,1)S(1)} %bitcast.56, f32[16,32]{1,0:T(8,128)S(1)} %fusion.30, f32[16,32,256]{2,1,0:T(8,128)} %copy-done.2), kind=kOutput, calls=%fused_computation.17 | convolution fusion | flops 34013952 | bytes 1705984 | tf_op jit(solution)/shard_map/hbl,lhd->bhd/dot_general | solution.py:41
  151.6 0.7 copy.46
  152.3 38.6 %all-to-all-done.3 = bf16[32,16,2048]{2,1,0:T(8,128)(2,1)} async-done(((bf16[32,16,2048]{2,1,0:T(8,128)(2,1)}), bf16[32,16,2048]{2,1,0:T(8,128)(2,1)}, u32[]{:S(2)}, u32[]{:S(2)}) %all-to-all-start.3) | async-done | bytes 2097184 | tf_op jit(solution)/shard_map/all_to_all | solution.py:66
  190.9 2.0 %convert_reduce_fusion = f32[2,16,2048]{2,1,0:T(8,128)S(1)} fusion(bf16[32,16,2048]{2,1,0:T(8,128)(2,1)} %all-to-all-done.3), kind=kLoop, calls=%fused_computation.3 | loop fusion | flops 2031616 | bytes 2359296 | tf_op jit(solution)/shard_map/reduce_sum | solution.py:69
  192.8 1.1 fusion.1
  (32 shorter events, 1.5 us)
Async XLA Ops:
  0.6 109.9 %copy-start = (bf16[512,2048]{1,0:T(8,128)(2,1)S(1)}, bf16[512,2048]{1,0:T(8,128)(2,1)}, u32[]{:S(2)}) copy-start(bf16[512,2048]{1,0:T(8,128)(2,1)} %param.21) | copy-start | bytes 6291460
  0.6 3.0 %copy-start.1 = (bf16[4,8,2048]{2,1,0:T(8,128)(2,1)S(1)}, bf16[4,8,2048]{2,1,0:T(8,128)(2,1)}, u32[]{:S(2)}) copy-start(bf16[4,8,2048]{2,1,0:T(8,128)(2,1)} %param.13) | copy-start | bytes 393220
  8.1 13.6 %copy-start.5 = (s32[32,2]{0,1:T(2,128)S(1)}, s32[32,2]{0,1:T(2,128)}, u32[]{:S(2)}) copy-start(s32[32,2]{0,1:T(2,128)} %param.17) | copy-start | bytes 772
  8.1 14.5 %copy-start.3 = (bf16[32,2048]{1,0:T(8,128)(2,1)S(1)}, bf16[32,2048]{1,0:T(8,128)(2,1)}, u32[]{:S(2)}) copy-start(bf16[32,2048]{1,0:T(8,128)(2,1)} %param.12) | copy-start | bytes 393220
  8.1 14.7 %copy-start.4 = (f32[2048]{0:T(1024)S(1)}, f32[2048]{0:T(1024)}, u32[]{:S(2)}) copy-start(f32[2048]{0:T(1024)} %param.19) | copy-start | bytes 24580
  8.1 41.6 %all-to-all-start.1 = ((bf16[32,8,2048]{2,1,0:T(8,128)(2,1)}), bf16[32,8,2048]{2,1,0:T(8,128)(2,1)S(1)}, u32[]{:S(2)}, u32[]{:S(2)}) async-start(bf16[32,8,2048]{2,1,0:T(8,128)(2,1)} %get-tuple-element.3), calls=%async_computation.1 | async-start | bytes 2097152 | tf_op jit(solution)/shard_map/all_to_all | solution.py:24
  104.9 32.2 %all-to-all-start = ((bf16[32,8,2048]{2,1,0:T(8,128)(2,1)}), bf16[32,8,2048]{2,1,0:T(8,128)(2,1)}, u32[]{:S(2)}, u32[]{:S(2)}) async-start(bf16[32,8,2048]{2,1,0:T(8,128)(2,1)} %get-tuple-element.4), calls=%async_computation | async-start | bytes 2097152 | tf_op jit(solution)/shard_map/all_to_all | solution.py:25
  116.6 26.2 %copy-start.7 = (s32[32]{0:T(128)S(1)}, s32[32]{0:T(128)}, u32[]{:S(2)}) copy-start(s32[32]{0:T(128)} %param.16) | copy-start | bytes 388
  116.6 29.6 %copy-start.6 = (f32[32,2]{0,1:T(2,128)S(1)}, f32[32,2]{0,1:T(2,128)}, u32[]{:S(2)}) copy-start(f32[32,2]{0,1:T(2,128)} %param.18) | copy-start | bytes 772
  137.1 53.7 %all-to-all-start.3 = ((bf16[32,16,2048]{2,1,0:T(8,128)(2,1)}), bf16[32,16,2048]{2,1,0:T(8,128)(2,1)}, u32[]{:S(2)}, u32[]{:S(2)}) async-start(bf16[32,16,2048]{2,1,0:T(8,128)(2,1)} %convolution_convert_fusion), calls=%async_computation.3 | async-start | bytes 4194304 | tf_op jit(solution)/shard_map/all_to_all | solution.py:66
  148.4 0.8 copy-start.2
where the time goes:
time: 195 us; the launch traced here: 194 us
  waiting for transfers between devices  85.8 us (44%)
  blocking collectives  54.9 us (28%)
  starting transfers between devices  24.8 us (13%)
  matrix products  10 us (5%)
  local copies, waits for them, and re-layouts  8.29 us (4%)
  other arithmetic  7.24 us (4%)
  between operations  2.8 us (1%)
    all_to_all x1, blocking collectives, on_device(): lax.all_to_all(outgoing, 'dev', split_axis=0, concat_axis=0, tiled=True)  54.9 us
    all_to_all x1, waiting for transfers between devices, on_device(): lax.all_to_all(partial_out.astype(jnp.bfloat16), 'dev', split_axis=0, con...  38.6 us
    all_to_all x1, waiting for transfers between devices, on_device(): lax.all_to_all(outgoing_keys, 'dev', split_axis=0, concat_axis=0, tiled=T...  26.7 us
    all_to_all x1, waiting for transfers between devices, on_device(): lax.all_to_all(outgoing_values, 'dev', split_axis=0, concat_axis=0, tiled...  20.5 us
    all_to_all x1, starting transfers between devices, on_device(): lax.all_to_all(outgoing_keys, 'dev', split_axis=0, concat_axis=0, tiled=T...  13.6 us
    dot_general x1, matrix products, on_device(): jnp.einsum('sch,hd->scd', hidden, w_down, preferred_element_type=jnp.floa...  6.06 us
    all_to_all x1, starting transfers between devices, on_device(): lax.all_to_all(partial_out.astype(jnp.bfloat16), 'dev', split_axis=0, con...  5.62 us
    all_to_all x1, starting transfers between devices, on_device(): lax.all_to_all(outgoing_values, 'dev', split_axis=0, concat_axis=0, tiled...  5.62 us
  transfers between devices with their start and end apart: 3, of which 3 were waited for; matrix products, arithmetic and copies ran while one was open for 7% of the time, Pallas kernels for 0%

commit v1 on v0

v1 whole, which is shorter than its diff:
```python
import functools

import jax
import jax.numpy as jnp
from jax import lax
from jax.experimental import pallas as pl
from jax.experimental.pallas import tpu as pltpu
from jax.sharding import PartitionSpec as P

HEAD = 128
EXPF = 2
CAP = 16
NX = 4
NZ = 8
HALF = NZ // EXPF
BF = jnp.bfloat16
F32 = jnp.float32

Z_RINGS = [[z * NX + x for z in range(NZ)] for x in range(NX)]
RIGHT = [(z * NX + x, z * NX + (x + 1) % NX) for z in range(NZ) for x in range(NX)]
LEFT = [(z * NX + x, z * NX + (x - 1) % NX) for z in range(NZ) for x in range(NX)]


def to_right(a):
    return lax.ppermute(a, "dev", RIGHT)


def to_left(a):
    return lax.ppermute(a, "dev", LEFT)


def along_z(a):
    return lax.all_to_all(
        a, "dev", split_axis=0, concat_axis=0, axis_index_groups=Z_RINGS, tiled=True
    )


def slot_columns(routes, expert):
    beams = routes.shape[0]
    chosen = jnp.sum((routes == expert).astype(F32), axis=1, keepdims=True)
    row = lax.broadcasted_iota(jnp.int32, (beams, beams), 0)
    col = lax.broadcasted_iota(jnp.int32, (beams, beams), 1)
    return chosen, row, col


def pack_rows_kernel(queries_ref, routes_ref, gain_ref, out_ref):
    rows = queries_ref[...].astype(F32)
    mean_sq = jnp.mean(rows * rows, axis=-1, keepdims=True)
    normed = (rows * lax.rsqrt(mean_sq + 1e-06) * gain_ref[...]).astype(BF)
    routes = routes_ref[...]
    beams = rows.shape[0]
    for expert in range(EXPF):
        chosen, row, col = slot_columns(routes, expert)
        slot = jnp.sum(jnp.where(row < col, chosen, 0.0), axis=0, keepdims=True)
        mine = jnp.sum(jnp.where(row == col, chosen, 0.0), axis=0, keepdims=True)
        place = lax.broadcasted_iota(jnp.int32, (CAP, beams), 0).astype(F32)
        picker = jnp.where((place == slot) & (mine > 0.5), 1.0, 0.0).astype(BF)
        packed = jnp.dot(picker, normed, preferred_element_type=F32).astype(BF)
        for z in range(HALF):
            out_ref[expert * HALF + z] = packed


def pack_rows(queries, routes, gain):
    width = queries.shape[1]
    return pl.pallas_call(
        pack_rows_kernel,
        out_shape=jax.ShapeDtypeStruct((NZ, CAP, width), BF),
        cost_estimate=pl.CostEstimate(
            flops=4_000_000, bytes_accessed=700_000, transcendentals=32
        ),
        name="pack_rows",
    )(queries, routes, gain.reshape(1, width))


def combine_kernel(ret_ref, routes_ref, gate_ref, out_ref):
    routes = routes_ref[...]
    gate = gate_ref[...]
    beams = routes.shape[0]
    total = None
    for expert in range(EXPF):
        summed = ret_ref[expert * HALF].astype(F32)
        for z in range(1, HALF):
            summed = summed + ret_ref[expert * HALF + z].astype(F32)
        chosen, row, col = slot_columns(routes, expert)
        mine = jnp.sum(jnp.where(row == col, chosen, 0.0), axis=0, keepdims=True)
        slot = jnp.sum(jnp.where(col < row, mine, 0.0), axis=1, keepdims=True)
        weight = jnp.sum(jnp.where(routes == expert, gate, 0.0), axis=1, keepdims=True)
        place = lax.broadcasted_iota(jnp.int32, (beams, CAP), 1).astype(F32)
        spread = jnp.where((place == slot) & (chosen > 0.5), weight, 0.0)
        part = jnp.dot(
            spread, summed, precision=lax.Precision.HIGHEST, preferred_element_type=F32
        )
        total = part if total is None else total + part
    out_ref[...] = total.astype(BF)


def combine(ret, routes, gate):
    beams = routes.shape[0]
    width = ret.shape[-1]
    return pl.pallas_call(
        combine_kernel,
        out_shape=jax.ShapeDtypeStruct((beams, width), BF),
        cost_estimate=pl.CostEstimate(
            flops=25_000_000, bytes_accessed=700_000, transcendentals=0
        ),
        name="combine",
    )(ret, routes, gate)


def pack_heads_kernel(q_ref, own_ref, left_ref, right_ref, kfar_ref, vfar_ref, out_ref):
    rows = q_ref.shape[0]
    shard = kfar_ref.shape[0]
    span = out_ref.shape[2]
    for z in range(NZ):
        cols = slice(z * span, (z + 1) * span)
        at = 0
        for which, far in ((0, kfar_ref), (1, vfar_ref)):
            for ref in (own_ref, left_ref, right_ref):
                out_ref[z, at : at + shard, :] = ref[which, :, cols]
                at += shard
            out_ref[z, at : at + shard, :] = far[:, cols]
            at += shard
        out_ref[z, at : at + rows, :] = q_ref[:, cols]


def pack_heads(queries, own, left, right, k_far, v_far):
    rows, width = queries.shape
    shard = k_far.shape[0]
    return pl.pallas_call(
        pack_heads_kernel,
        out_shape=jax.ShapeDtypeStruct((NZ, 2 * NX * shard + rows, width // NZ), BF),
        cost_estimate=pl.CostEstimate(
            flops=0, bytes_accessed=2_400_000, transcendentals=0
        ),
        name="pack_heads",
    )(queries, own, left, right, k_far, v_far)


def attend_kernel(beams, got_ref, bias_ref, out_ref):
    span = got_ref.shape[2]
    memory = (got_ref.shape[1] - beams) // 2
    count = NZ * memory
    for head in range(span // HEAD):
        cols = slice(head * HEAD, (head + 1) * HEAD)
        keys = got_ref[:, 0:memory, cols].reshape(count, HEAD)
        values = got_ref[:, memory : 2 * memory, cols].reshape(count, HEAD)
        for src in range(0, NZ, 2):
            rows = got_ref[src : src + 2, 2 * memory : 2 * memory + beams, cols]
            rows = rows.reshape(2 * beams, HEAD)
            scores = lax.dot_general(
                rows, keys, (((1,), (1,)), ((), ())), preferred_element_type=F32
            )
            scores = scores * HEAD ** (-0.5)
            scores = scores.reshape(2, beams, count) + bias_ref[src : src + 2][:, None, :]
            top = jnp.max(scores, axis=-1, keepdims=True)
            expo = jnp.exp(scores - top)
            total = jnp.sum(expo, axis=-1, keepdims=True)
            weights = (expo / total).astype(BF).reshape(2 * beams, count)
            mixed = jnp.dot(weights, values, preferred_element_type=F32).astype(BF)
            out_ref[src : src + 2, :, cols] = mixed.reshape(2, beams, HEAD)


def attend(got, bias, beams):
    span = got.shape[2]
    return pl.pallas_call(
        functools.partial(attend_kernel, beams),
        out_shape=jax.ShapeDtypeStruct((NZ, beams, span), BF),
        cost_estimate=pl.CostEstimate(
            flops=300_000_000, bytes_accessed=1_400_000, transcendentals=600_000
        ),
        compiler_params=pltpu.CompilerParams(vmem_limit_bytes=24 * 2**20),
        name="attend",
    )(got, bias)


def experts_kernel(count, *refs):
    ins, (up_ref, down_ref), outs = refs[:count], refs[count : count + 2], refs[count + 2 : -1]
    acc = refs[-1]
    step = pl.program_id(0)
    at = 0
    for rows_ref in ins:
        size = rows_ref.shape[0]
        hidden = jnp.dot(rows_ref[...], up_ref[...], preferred_element_type=F32)
        hidden = (hidden / (1.0 + jnp.exp(-hidden))).astype(BF)
        part = jnp.dot(hidden, down_ref[...], preferred_element_type=F32)
        span = slice(at, at + size)

        @pl.when(step == 0)
        def _(part=part, span=span):
            acc[span, :] = part

        @pl.when(step != 0)
        def _(part=part, span=span):
            acc[span, :] += part

        at += size

    @pl.when(step == pl.num_programs(0) - 1)
    def _():
        at = 0
        for out_ref in outs:
            size = out_ref.shape[0]
            out_ref[...] = acc[at : at + size, :].astype(out_ref.dtype)
            at += size


def experts(blocks, up, down, tile=256):
    width, hidden = up.shape
    total = sum(b.shape[0] for b in blocks)
    whole = [pl.BlockSpec(b.shape, lambda j: (0, 0)) for b in blocks]
    return pl.pallas_call(
        functools.partial(experts_kernel, len(blocks)),
        grid=(hidden // tile,),
        in_specs=whole
        + [
            pl.BlockSpec((width, tile), lambda j: (0, j)),
            pl.BlockSpec((tile, width), lambda j: (j, 0)),
        ],
        out_specs=list(whole),
        out_shape=[jax.ShapeDtypeStruct(b.shape, BF) for b in blocks],
        scratch_shapes=[pltpu.VMEM((total, width), F32)],
        cost_estimate=pl.CostEstimate(
            flops=4 * total * width * hidden,
            bytes_accessed=4 * width * hidden + 4 * total * width,
            transcendentals=total * hidden,
        ),
        compiler_params=pltpu.CompilerParams(vmem_limit_bytes=32 * 2**20),
        name="experts",
    )(*blocks, up, down)


def on_device(
    queries, keys, values, kv_count, beam_user, routes, route_gate, norm_gain, w_up, w_down
):
    beams, width = queries.shape
    users, shard_len, _ = keys.shape
    shard = users * shard_len
    x = lax.rem(lax.axis_index("dev"), NX)

    own = jnp.stack([keys.reshape(shard, width), values.reshape(shard, width)])
    left, right = to_right(own), to_left(own)
    k_far, v_far = to_right(left[0]), to_left(right[1])

    block = along_z(pack_rows(queries, routes, norm_gain))
    size = NZ * CAP
    block = block.reshape(size, width)
    block_l, block_r = to_right(block), to_left(block)
    far_a, far_b = to_right(block_l[: size // 2]), to_left(block_r[size // 2 :])

    (part,) = experts([block], w_up, w_down)
    part_l, part_r = experts([block_l, block_r], w_up, w_down)
    part_fa, part_fb = experts([far_a, far_b], w_up, w_down)

    got = along_z(pack_heads(queries, own, left, right, k_far, v_far))
    order = jnp.stack([x, lax.rem(x + NX - 1, NX), lax.rem(x + 1, NX), lax.rem(x + 2, NX)])
    counts = jnp.take(kv_count.reshape(users, NZ, NX), order, axis=2)
    counts = counts.transpose(1, 2, 0)[None, :, :, :, None]
    column_users = beam_user.reshape(NZ, NX)[:, x]
    offset = jnp.arange(shard_len)[None, None, None, None, :]
    same = column_users[:, None, None, None, None] == jnp.arange(users)[None, None, None, :, None]
    bias = jnp.where(same & (offset < counts), 0.0, -1e30).astype(F32)
    mixed = along_z(attend(got, bias.reshape(NZ, NZ * NX * shard), beams))
    context = mixed.transpose(1, 0, 2).reshape(beams, width)

    half = size // 2
    more_r = to_right(part_fa)
    more_l = to_left(part_fb)
    part_r = jnp.concatenate(
        [(part_r[:half].astype(F32) + more_r.astype(F32)).astype(BF), part_r[half:]]
    )
    part_l = jnp.concatenate(
        [part_l[:half], (part_l[half:].astype(F32) + more_l.astype(F32)).astype(BF)]
    )
    from_l, from_r = to_right(part_r), to_left(part_l)
    total = (part.astype(F32) + from_l.astype(F32) + from_r.astype(F32)).astype(BF)
    ret = along_z(total.reshape(NZ, CAP, width))
    routed = combine(ret, routes, route_gate)
    return (context, routed)


def solution(mesh):
    return jax.shard_map(
        on_device,
        mesh=mesh,
        in_specs=(
            P(("user", "dev"), None),
            P("user", "dev", None),
            P("user", "dev", None),
            P("user", None),
            P("user"),
            P(("user", "dev"), None),
            P(("user", "dev"), None),
            P(),
            P(None, "dev"),
            P("dev", None),
        ),
        out_specs=(P(("user", "dev"), None), P(("user", "dev"), None)),
        check_vma=False,
    )
```

time: 195 us -> 157 us (0.81)
  the two profiles are of different devices: /device:TPU:36 before, /device:TPU:32 now
where the time goes in v1:
time: 157 us; the launch traced here: 155 us
  starting transfers between devices  64.6 us (41%)
  waiting for transfers between devices  41.2 us (26%)
  Pallas kernels  21.8 us (14%)
  local copies, waits for them, and re-layouts  20.5 us (13%)
  other arithmetic  6.27 us (4%)
    all_to_all x4, waiting for transfers between devices, along_z(): lax.all_to_all(a, 'dev', split_axis=0, concat_axis=0, axis_index_groups=Z...  27.1 us
    ppermute x6, starting transfers between devices, to_left(): return lax.ppermute(a, 'dev', LEFT)  25.1 us
    all_to_all x4, starting transfers between devices, along_z(): lax.all_to_all(a, 'dev', split_axis=0, concat_axis=0, axis_index_groups=Z...  24.5 us
    ppermute x6, starting transfers between devices, to_right(): return lax.ppermute(a, 'dev', RIGHT)  15 us
    unnamed x44, local copies, waits for them, and re-layouts  14.5 us
    pallas_call x3, Pallas kernels, experts(): pl.pallas_call(functools.partial(experts_kernel, len(blocks)), grid=(hidd...  10.8 us
    ppermute x6, waiting for transfers between devices, to_right(): return lax.ppermute(a, 'dev', RIGHT)  8.52 us
    ppermute x6, waiting for transfers between devices, to_left(): return lax.ppermute(a, 'dev', LEFT)  5.66 us
  transfers between devices with their start and end apart: 16, of which 6 were waited for; matrix products, arithmetic and copies ran while one was open for 8% of the time, Pallas kernels for 11%

profile of v1, /device:TPU:32, one launch (start us, length us, event | category | flops | bytes accessed | tf_op | source)
XLA Modules:
  0.0 155.4 jit_solution(5938180076968769462)
XLA Ops:
  4.0 10.3 %all-to-all-start.2 = ((bf16[8,16,2048]{2,1,0:T(8,128)(2,1)}), bf16[8,16,2048]{2,1,0:T(8,128)(2,1)S(1)}, u32[]{:S(2)}, u32[]{:S(2)}) async-start(bf16[8,16,2048]{2,1,0:T(8,128)(2,1)} %pack_rows.1), calls=%async_computation.2 | async-start | bytes 1048576 | tf_op jit(solution)/shard_map/all_to_all | solution.py:33
  15.3 3.4 %collective-permute-start = (bf16[2,32,2048]{2,1,0:T(8,128)(2,1)S(1)}, bf16[2,32,2048]{2,1,0:T(8,128)(2,1)S(1)}, u32[]{:S(2)}, u32[]{:S(2)}) collective-permute-start(bf16[2,32,2048]{2,1,0:T(8,128)(2,1)S(1)} %pad_maximum_fusion.2.own_ref), channel_id=1, source_target_pairs={{0,1},{1,2},{2,3},{3,0},{4,5},{5,6},{6,7},{7,4},{8,9},{9,10},{10,1... | collective-permute-start | bytes 786440 | tf_op jit(solution)/shard_map/ppermute | solution.py:25
  18.7 3.7 %collective-permute-start.1 = (bf16[2,32,2048]{2,1,0:T(8,128)(2,1)S(1)}, bf16[2,32,2048]{2,1,0:T(8,128)(2,1)S(1)}, u32[]{:S(2)}, u32[]{:S(2)}) collective-permute-start(bf16[2,32,2048]{2,1,0:T(8,128)(2,1)S(1)} %pad_maximum_fusion.2.own_ref), channel_id=1, source_target_pairs={{0,3},{1,0},{2,1},{3,2},{4,7},{5,4},{6,5},{7,6},{8,11},{9,8},{10,9... | collective-permute-start | bytes 786440 | tf_op jit(solution)/shard_map/ppermute | solution.py:29
  23.3 8.6 %all-to-all-done.2 = bf16[8,16,2048]{2,1,0:T(8,128)(2,1)S(1)} async-done(((bf16[8,16,2048]{2,1,0:T(8,128)(2,1)}), bf16[8,16,2048]{2,1,0:T(8,128)(2,1)S(1)}, u32[]{:S(2)}, u32[]{:S(2)}) %all-to-all-start.2) | async-done | bytes 524320 | tf_op jit(solution)/shard_map/all_to_all | solution.py:33
  31.8 3.4 %collective-permute-start.4 = (bf16[128,2048]{1,0:T(8,128)(2,1)S(1)}, bf16[128,2048]{1,0:T(8,128)(2,1)S(1)}, u32[]{:S(2)}, u32[]{:S(2)}) collective-permute-start(bf16[128,2048]{1,0:T(8,128)(2,1)S(1)} %bitcast.24), channel_id=1, source_target_pairs={{0,1},{1,2},{2,3},{3,0},{4,5},{5,6},{6,7},{7,4},{8,9},{9,10},{10,1... | collective-permute-start | bytes 1572872 | tf_op jit(solution)/shard_map/ppermute | solution.py:25
  35.2 3.7 %collective-permute-start.5 = (bf16[128,2048]{1,0:T(8,128)(2,1)S(1)}, bf16[128,2048]{1,0:T(8,128)(2,1)S(1)}, u32[]{:S(2)}, u32[]{:S(2)}) collective-permute-start(bf16[128,2048]{1,0:T(8,128)(2,1)S(1)} %bitcast.25), channel_id=1, source_target_pairs={{0,3},{1,0},{2,1},{3,2},{4,7},{5,4},{6,5},{7,6},{8,11},{9,8},{10,9... | collective-permute-start | bytes 1572872 | tf_op jit(solution)/shard_map/ppermute | solution.py:29
  39.0 2.2 %collective-permute-start.2 = (bf16[32,2048]{1,0:T(8,128)(2,1)S(1)}, bf16[32,2048]{1,0:T(8,128)(2,1)S(1)}, u32[]{:S(2)}, u32[]{:S(2)}) collective-permute-start(bf16[32,2048]{1,0:T(8,128)(2,1)S(1)} %slice_bitcast_fusion.1), channel_id=1, source_target_pairs={{0,1},{1,2},{2,3},{3,0},{4,5},{5,6},{6,7},{7,4},{8,9},{9,10},{10,1... | collective-permute-start | bytes 393224 | tf_op jit(solution)/shard_map/ppermute | solution.py:25
  41.2 8.5 %collective-permute-done.4.refs_0_ = bf16[128,2048]{1,0:T(8,128)(2,1)S(1)} collective-permute-done((bf16[128,2048]{1,0:T(8,128)(2,1)S(1)}, bf16[128,2048]{1,0:T(8,128)(2,1)S(1)}, u32[]{:S(2)}, u32[]{:S(2)}) %collective-permute-start.4) | collective-permute-done | bytes 524320 | tf_op jit(solution)/shard_map/ppermute | solution.py:25
  54.9 4.9 %collective-permute-start.7 = (bf16[64,2048]{1,0:T(8,128)(2,1)}, bf16[64,2048]{1,0:T(8,128)(2,1)}, u32[]{:S(2)}, u32[]{:S(2)}) collective-permute-start(bf16[64,2048]{1,0:T(8,128)(2,1)} %slice.37), channel_id=1, source_target_pairs={{0,3},{1,0},{2,1},{3,2},{4,7},{5,4},{6,5},{7,6},{8,11},{9,8},{10,9... | collective-permute-start | bytes 786440 | tf_op jit(solution)/shard_map/ppermute | solution.py:29
  60.5 2.2 %collective-permute-start.3 = (bf16[32,2048]{1,0:T(8,128)(2,1)}, bf16[32,2048]{1,0:T(8,128)(2,1)S(1)}, u32[]{:S(2)}, u32[]{:S(2)}) collective-permute-start(bf16[32,2048]{1,0:T(8,128)(2,1)} %slice_bitcast_fusion), channel_id=1, source_target_pairs={{0,3},{1,0},{2,1},{3,2},{4,7},{5,4},{6,5},{7,6},{8,11},{9,8},{10,9... | collective-permute-start | bytes 393224 | tf_op jit(solution)/shard_map/ppermute | solution.py:29
  63.0 4.6 %collective-permute-done.3.vfar_ref = bf16[32,2048]{1,0:T(8,128)(2,1)S(1)} collective-permute-done((bf16[32,2048]{1,0:T(8,128)(2,1)}, bf16[32,2048]{1,0:T(8,128)(2,1)S(1)}, u32[]{:S(2)}, u32[]{:S(2)}) %collective-permute-start.3) | collective-permute-done | bytes 131104 | tf_op jit(solution)/shard_map/ppermute | solution.py:29
  68.3 2.3 %pack_heads.1 = bf16[8,288,256]{2,1,0:T(8,128)(2,1)} custom-call(bf16[32,2048]{1,0:T(8,128)(2,1)} %queries_ref.1, bf16[2,32,2048]{2,1,0:T(8,128)(2,1)} %copy-done.14, bf16[2,32,2048]{2,1,0:T(8,128)(2,1)} %copy-done.15, bf16[2,32,2048]{2,1,0:T(8,128)(2,1)} %copy-done.16, bf16[32,2048]{1,0:T(8,128)(2,1)} %copy-done.17, bf16[32,2048]{1,0:T(8,128)(2,1)} %copy-done.18), custom_call_target="tpu_custom_call" | custom-call | bytes 2400000 | tf_op jit(solution)/shard_map/pack_heads/pallas_call | solution.py:129
  70.6 3.6 %all-to-all-start = ((bf16[8,288,256]{2,1,0:T(8,128)(2,1)}), bf16[8,288,256]{2,1,0:T(8,128)(2,1)S(1)}, u32[]{:S(2)}, u32[]{:S(2)}) async-start(bf16[8,288,256]{2,1,0:T(8,128)(2,1)} %pack_heads.1), calls=%async_computation | async-start | bytes 2359296 | tf_op jit(solution)/shard_map/all_to_all | solution.py:33
  75.8 5.2 %experts.5 = (bf16[64,2048]{1,0:T(8,128)(2,1)}, bf16[64,2048]{1,0:T(8,128)(2,1)S(1)}) custom-call(bf16[64,2048]{1,0:T(8,128)(2,1)S(1)} %collective-permute-done.6.refs_0_, bf16[64,2048]{1,0:T(8,128)(2,1)} %collective-permute-done.7.refs_1_, bf16[2048,512]{1,0:T(8,128)(2,1)S(1)} %copy-done, bf16[512,2048]{1,0:T(8,128)(2,1)S(1)} %copy-done.1), custom_call_target="tpu_custom_call" | custom-call | flops 536870912 | bytes 5242880 | tf_op jit(solution)/shard_map/experts/pallas_call | solution.py:211
  89.7 3.7 %experts.4 = (bf16[128,2048]{1,0:T(8,128)(2,1)S(1)}, bf16[128,2048]{1,0:T(8,128)(2,1)S(1)}) custom-call(bf16[128,2048]{1,0:T(8,128)(2,1)S(1)} %copy-done.8, bf16[128,2048]{1,0:T(8,128)(2,1)S(1)} %copy-done.10, bf16[2048,512]{1,0:T(8,128)(2,1)S(1)} %copy-done, bf16[512,2048]{1,0:T(8,128)(2,1)S(1)} %copy-done.2), custom_call_target="tpu_custom_call" | custom-call | flops 1073741824 | bytes 6291456 | tf_op jit(solution)/shard_map/experts/pallas_call | solution.py:211
  93.5 5.1 %collective-permute-start.10 = (bf16[64,2048]{1,0:T(8,128)(2,1)S(1)}, bf16[64,2048]{1,0:T(8,128)(2,1)S(1)}, u32[]{:S(2)}, u32[]{:S(2)}) collective-permute-start(bf16[64,2048]{1,0:T(8,128)(2,1)S(1)} %copy-done.12), channel_id=1, source_target_pairs={{0,3},{1,0},{2,1},{3,2},{4,7},{5,4},{6,5},{7,6},{8,11},{9,8},{10,9... | collective-permute-start | bytes 786440 | tf_op jit(solution)/shard_map/ppermute | solution.py:29
  103.4 5.6 %collective-permute-start.11 = (bf16[128,2048]{1,0:T(8,128)(2,1)}, bf16[128,2048]{1,0:T(8,128)(2,1)}, u32[]{:S(2)}, u32[]{:S(2)}) collective-permute-start(bf16[128,2048]{1,0:T(8,128)(2,1)} %pad_maximum_fusion.1), channel_id=1, source_target_pairs={{0,3},{1,0},{2,1},{3,2},{4,7},{5,4},{6,5},{7,6},{8,11},{9,8},{10,9... | collective-permute-start | bytes 1572872 | tf_op jit(solution)/shard_map/ppermute | solution.py:29
  115.1 4.2 %attend.1 = bf16[8,32,256]{2,1,0:T(8,128)(2,1)} custom-call(bf16[8,288,256]{2,1,0:T(8,128)(2,1)S(1)} %all-to-all-done.got_ref, f32[8,1024]{1,0:T(8,128)S(1)} %and_select_fusion.bias_ref), custom_call_target="tpu_custom_call" | custom-call | flops 300000000 | bytes 1400000 | tf_op jit(solution)/shard_map/attend/pallas_call | solution.py:165
  119.3 7.1 %all-to-all-start.1 = ((bf16[8,32,256]{2,1,0:T(8,128)(2,1)}), bf16[8,32,256]{2,1,0:T(8,128)(2,1)S(1)}, u32[]{:S(2)}, u32[]{:S(2)}) async-start(bf16[8,32,256]{2,1,0:T(8,128)(2,1)} %attend.1), calls=%async_computation.1 | async-start | bytes 262144 | tf_op jit(solution)/shard_map/all_to_all | solution.py:33
  126.4 2.4 %add_convert_fusion = bf16[128,2048]{1,0:T(8,128)(2,1)} fusion(bf16[128,2048]{1,0:T(8,128)(2,1)} %collective-permute-done.11, bf16[128,2048]{1,0:T(8,128)(2,1)} %collective-permute-done.9, bf16[128,2048]{1,0:T(8,128)(2,1)} %copy-done.6), kind=kLoop, calls=%fused_computation.1 | loop fusion | flops 1572864 | bytes 2097152 | tf_op jit(solution)/shard_map/convert_element_type | solution.py:275
  128.8 6.7 %all-to-all-done.1 = bf16[8,32,256]{2,1,0:T(8,128)(2,1)S(1)} async-done(((bf16[8,32,256]{2,1,0:T(8,128)(2,1)}), bf16[8,32,256]{2,1,0:T(8,128)(2,1)S(1)}, u32[]{:S(2)}, u32[]{:S(2)}) %all-to-all-start.1) | async-done | bytes 131104 | tf_op jit(solution)/shard_map/all_to_all | solution.py:33
  135.5 3.5 %all-to-all-start.3 = ((bf16[8,16,2048]{2,1,0:T(8,128)(2,1)}), bf16[8,16,2048]{2,1,0:T(8,128)(2,1)S(1)}, u32[]{:S(2)}, u32[]{:S(2)}) async-start(bf16[8,16,2048]{2,1,0:T(8,128)(2,1)} %bitcast.17), calls=%async_computation.3 | async-start | bytes 1048576 | tf_op jit(solution)/shard_map/all_to_all | solution.py:33
  140.3 11.8 %all-to-all-done.3.ret_ref = bf16[8,16,2048]{2,1,0:T(8,128)(2,1)S(1)} async-done(((bf16[8,16,2048]{2,1,0:T(8,128)(2,1)}), bf16[8,16,2048]{2,1,0:T(8,128)(2,1)S(1)}, u32[]{:S(2)}, u32[]{:S(2)}) %all-to-all-start.3) | async-done | bytes 524320 | tf_op jit(solution)/shard_map/all_to_all | solution.py:33
  153.0 2.4 %combine.1 = bf16[32,2048]{1,0:T(8,128)(2,1)} custom-call(bf16[8,16,2048]{2,1,0:T(8,128)(2,1)} %copy-done.13, s32[32,2]{1,0:T(8,128)} %copy.19.routes_ref, f32[32,2]{1,0:T(8,128)} %copy.21.gate_ref), custom_call_target="tpu_custom_call" | custom-call | flops 25000000 | bytes 700000 | tf_op jit(solution)/shard_map/combine/pallas_call | solution.py:100
  (88 shorter events, 35.3 us)
Async XLA Ops:
  0.6 21.9 %copy-start.19 = (s32[4,32]{1,0:T(4,128)S(1)}, s32[4,32]{1,0:T(4,128)}, u32[]{:S(2)}) copy-start(s32[4,32]{1,0:T(4,128)} %param.13) | copy-start | bytes 1540
  4.0 27.8 %all-to-all-start.2 = ((bf16[8,16,2048]{2,1,0:T(8,128)(2,1)}), bf16[8,16,2048]{2,1,0:T(8,128)(2,1)S(1)}, u32[]{:S(2)}, u32[]{:S(2)}) async-start(bf16[8,16,2048]{2,1,0:T(8,128)(2,1)} %pack_rows.1), calls=%async_computation.2 | async-start | bytes 1048576 | tf_op jit(solution)/shard_map/all_to_all | solution.py:33
  15.3 52.3 %copy-start.14 = (bf16[2,32,2048]{2,1,0:T(8,128)(2,1)}, bf16[2,32,2048]{2,1,0:T(8,128)(2,1)S(1)}, u32[]{:S(2)}) copy-start(bf16[2,32,2048]{2,1,0:T(8,128)(2,1)S(1)} %pad_maximum_fusion.2.own_ref) | copy-start | bytes 786436
  15.3 23.6 %collective-permute-start = (bf16[2,32,2048]{2,1,0:T(8,128)(2,1)S(1)}, bf16[2,32,2048]{2,1,0:T(8,128)(2,1)S(1)}, u32[]{:S(2)}, u32[]{:S(2)}) collective-permute-start(bf16[2,32,2048]{2,1,0:T(8,128)(2,1)S(1)} %pad_maximum_fusion.2.own_ref), channel_id=1, source_target_pairs={{0,1},{1,2},{2,3},{3,0},{4,5},{5,6},{6,7},{7,4},{8,9},{9,10},{10,1... | collective-permute-start | bytes 786440 | tf_op jit(solution)/shard_map/ppermute | solution.py:25
  18.7 41.1 %collective-permute-start.1 = (bf16[2,32,2048]{2,1,0:T(8,128)(2,1)S(1)}, bf16[2,32,2048]{2,1,0:T(8,128)(2,1)S(1)}, u32[]{:S(2)}, u32[]{:S(2)}) collective-permute-start(bf16[2,32,2048]{2,1,0:T(8,128)(2,1)S(1)} %pad_maximum_fusion.2.own_ref), channel_id=1, source_target_pairs={{0,3},{1,0},{2,1},{3,2},{4,7},{5,4},{6,5},{7,6},{8,11},{9,8},{10,9... | collective-permute-start | bytes 786440 | tf_op jit(solution)/shard_map/ppermute | solution.py:29
  31.8 31.0 %copy-start.4 = (bf16[8,16,2048]{2,1,0:T(8,128)(2,1)}, bf16[8,16,2048]{2,1,0:T(8,128)(2,1)S(1)}, u32[]{:S(2)}) copy-start(bf16[8,16,2048]{2,1,0:T(8,128)(2,1)S(1)} %all-to-all-done.2) | copy-start | bytes 1572868
  31.8 17.9 %collective-permute-start.4 = (bf16[128,2048]{1,0:T(8,128)(2,1)S(1)}, bf16[128,2048]{1,0:T(8,128)(2,1)S(1)}, u32[]{:S(2)}, u32[]{:S(2)}) collective-permute-start(bf16[128,2048]{1,0:T(8,128)(2,1)S(1)} %bitcast.24), channel_id=1, source_target_pairs={{0,1},{1,2},{2,3},{3,0},{4,5},{5,6},{6,7},{7,4},{8,9},{9,10},{10,1... | collective-permute-start | bytes 1572872 | tf_op jit(solution)/shard_map/ppermute | solution.py:25
  35.2 18.2 %collective-permute-start.5 = (bf16[128,2048]{1,0:T(8,128)(2,1)S(1)}, bf16[128,2048]{1,0:T(8,128)(2,1)S(1)}, u32[]{:S(2)}, u32[]{:S(2)}) collective-permute-start(bf16[128,2048]{1,0:T(8,128)(2,1)S(1)} %bitcast.25), channel_id=1, source_target_pairs={{0,3},{1,0},{2,1},{3,2},{4,7},{5,4},{6,5},{7,6},{8,11},{9,8},{10,9... | collective-permute-start | bytes 1572872 | tf_op jit(solution)/shard_map/ppermute | solution.py:29
  39.0 28.6 %copy-start.15 = (bf16[2,32,2048]{2,1,0:T(8,128)(2,1)}, bf16[2,32,2048]{2,1,0:T(8,128)(2,1)S(1)}, u32[]{:S(2)}) copy-start(bf16[2,32,2048]{2,1,0:T(8,128)(2,1)S(1)} %collective-permute-done.left_ref) | copy-start | bytes 786436
  39.0 24.0 %collective-permute-start.2 = (bf16[32,2048]{1,0:T(8,128)(2,1)S(1)}, bf16[32,2048]{1,0:T(8,128)(2,1)S(1)}, u32[]{:S(2)}, u32[]{:S(2)}) collective-permute-start(bf16[32,2048]{1,0:T(8,128)(2,1)S(1)} %slice_bitcast_fusion.1), channel_id=1, source_target_pairs={{0,1},{1,2},{2,3},{3,0},{4,5},{5,6},{6,7},{7,4},{8,9},{9,10},{10,1... | collective-permute-start | bytes 393224 | tf_op jit(solution)/shard_map/ppermute | solution.py:25
  51.2 23.0 %collective-permute-start.6 = (bf16[64,2048]{1,0:T(8,128)(2,1)}, bf16[64,2048]{1,0:T(8,128)(2,1)S(1)}, u32[]{:S(2)}, u32[]{:S(2)}) collective-permute-start(bf16[64,2048]{1,0:T(8,128)(2,1)} %slice.36), channel_id=1, source_target_pairs={{0,1},{1,2},{2,3},{3,0},{4,5},{5,6},{6,7},{7,4},{8,9},{9,10},{10,1... | collective-permute-start | bytes 786440 | tf_op jit(solution)/shard_map/ppermute | solution.py:25
  54.9 19.3 %collective-permute-start.7 = (bf16[64,2048]{1,0:T(8,128)(2,1)}, bf16[64,2048]{1,0:T(8,128)(2,1)}, u32[]{:S(2)}, u32[]{:S(2)}) collective-permute-start(bf16[64,2048]{1,0:T(8,128)(2,1)} %slice.37), channel_id=1, source_target_pairs={{0,3},{1,0},{2,1},{3,2},{4,7},{5,4},{6,5},{7,6},{8,11},{9,8},{10,9... | collective-permute-start | bytes 786440 | tf_op jit(solution)/shard_map/ppermute | solution.py:29
  59.8 7.8 %copy-start.16 = (bf16[2,32,2048]{2,1,0:T(8,128)(2,1)}, bf16[2,32,2048]{2,1,0:T(8,128)(2,1)S(1)}, u32[]{:S(2)}) copy-start(bf16[2,32,2048]{2,1,0:T(8,128)(2,1)S(1)} %collective-permute-done.1.right_ref) | copy-start | bytes 786436
  60.5 7.1 %collective-permute-start.3 = (bf16[32,2048]{1,0:T(8,128)(2,1)}, bf16[32,2048]{1,0:T(8,128)(2,1)S(1)}, u32[]{:S(2)}, u32[]{:S(2)}) collective-permute-start(bf16[32,2048]{1,0:T(8,128)(2,1)} %slice_bitcast_fusion), channel_id=1, source_target_pairs={{0,3},{1,0},{2,1},{3,2},{4,7},{5,4},{6,5},{7,6},{8,11},{9,8},{10,9... | collective-permute-start | bytes 393224 | tf_op jit(solution)/shard_map/ppermute | solution.py:29
  63.0 11.3 %copy-start = (bf16[2048,512]{1,0:T(8,128)(2,1)S(1)}, bf16[2048,512]{1,0:T(8,128)(2,1)}, u32[]{:S(2)}) copy-start(bf16[2048,512]{1,0:T(8,128)(2,1)} %refs_2_.5) | copy-start | bytes 6291460
  63.0 4.6 %copy-start.17 = (bf16[32,2048]{1,0:T(8,128)(2,1)}, bf16[32,2048]{1,0:T(8,128)(2,1)S(1)}, u32[]{:S(2)}) copy-start(bf16[32,2048]{1,0:T(8,128)(2,1)S(1)} %collective-permute-done.2.kfar_ref) | copy-start | bytes 393220
  70.6 44.4 %all-to-all-start = ((bf16[8,288,256]{2,1,0:T(8,128)(2,1)}), bf16[8,288,256]{2,1,0:T(8,128)(2,1)S(1)}, u32[]{:S(2)}, u32[]{:S(2)}) async-start(bf16[8,288,256]{2,1,0:T(8,128)(2,1)} %pack_heads.1), calls=%async_computation | async-start | bytes 2359296 | tf_op jit(solution)/shard_map/all_to_all | solution.py:33
  81.7 17.0 %collective-permute-start.8 = (bf16[64,2048]{1,0:T(8,128)(2,1)}, bf16[64,2048]{1,0:T(8,128)(2,1)S(1)}, u32[]{:S(2)}, u32[]{:S(2)}) collective-permute-start(bf16[64,2048]{1,0:T(8,128)(2,1)} %get-tuple-element.7), channel_id=1, source_target_pairs={{0,1},{1,2},{2,3},{3,0},{4,5},{5,6},{6,7},{7,4},{8,9},{9,10},{10,1... | collective-permute-start | bytes 786440 | tf_op jit(solution)/shard_map/ppermute | solution.py:25
  93.5 9.0 %collective-permute-start.10 = (bf16[64,2048]{1,0:T(8,128)(2,1)S(1)}, bf16[64,2048]{1,0:T(8,128)(2,1)S(1)}, u32[]{:S(2)}, u32[]{:S(2)}) collective-permute-start(bf16[64,2048]{1,0:T(8,128)(2,1)S(1)} %copy-done.12), channel_id=1, source_target_pairs={{0,3},{1,0},{2,1},{3,2},{4,7},{5,4},{6,5},{7,6},{8,11},{9,8},{10,9... | collective-permute-start | bytes 786440 | tf_op jit(solution)/shard_map/ppermute | solution.py:29
  99.6 26.8 %collective-permute-start.9 = (bf16[128,2048]{1,0:T(8,128)(2,1)}, bf16[128,2048]{1,0:T(8,128)(2,1)}, u32[]{:S(2)}, u32[]{:S(2)}) collective-permute-start(bf16[128,2048]{1,0:T(8,128)(2,1)} %pad_maximum_fusion), channel_id=1, source_target_pairs={{0,1},{1,2},{2,3},{3,0},{4,5},{5,6},{6,7},{7,4},{8,9},{9,10},{10,1... | collective-permute-start | bytes 1572872 | tf_op jit(solution)/shard_map/ppermute | solution.py:25
  103.4 23.0 %collective-permute-start.11 = (bf16[128,2048]{1,0:T(8,128)(2,1)}, bf16[128,2048]{1,0:T(8,128)(2,1)}, u32[]{:S(2)}, u32[]{:S(2)}) collective-permute-start(bf16[128,2048]{1,0:T(8,128)(2,1)} %pad_maximum_fusion.1), channel_id=1, source_target_pairs={{0,3},{1,0},{2,1},{3,2},{4,7},{5,4},{6,5},{7,6},{8,11},{9,8},{10,9... | collective-permute-start | bytes 1572872 | tf_op jit(solution)/shard_map/ppermute | solution.py:29
  115.1 23.9 %copy-start.20 = (f32[32,2]{0,1:T(2,128)S(1)}, f32[32,2]{0,1:T(2,128)}, u32[]{:S(2)}) copy-start(f32[32,2]{0,1:T(2,128)} %param.16) | copy-start | bytes 772
  119.3 16.2 %all-to-all-start.1 = ((bf16[8,32,256]{2,1,0:T(8,128)(2,1)}), bf16[8,32,256]{2,1,0:T(8,128)(2,1)S(1)}, u32[]{:S(2)}, u32[]{:S(2)}) async-start(bf16[8,32,256]{2,1,0:T(8,128)(2,1)} %attend.1), calls=%async_computation.1 | async-start | bytes 262144 | tf_op jit(solution)/shard_map/all_to_all | solution.py:33
  135.5 16.7 %all-to-all-start.3 = ((bf16[8,16,2048]{2,1,0:T(8,128)(2,1)}), bf16[8,16,2048]{2,1,0:T(8,128)(2,1)S(1)}, u32[]{:S(2)}, u32[]{:S(2)}) async-start(bf16[8,16,2048]{2,1,0:T(8,128)(2,1)} %bitcast.17), calls=%async_computation.3 | async-start | bytes 1048576 | tf_op jit(solution)/shard_map/all_to_all | solution.py:33
  (13 other events, 16.3 us)

commit v2 on v1

v2 whole, which is shorter than its diff:
```python
import functools

import jax
import jax.numpy as jnp
from jax import lax
from jax.experimental import pallas as pl
from jax.experimental.pallas import tpu as pltpu
from jax.sharding import PartitionSpec as P

HEAD = 128
EXPF = 2
CAP = 16
NX = 4
NZ = 8
HALF = NZ // EXPF
BF = jnp.bfloat16
F32 = jnp.float32

Z_RINGS = [[z * NX + x for z in range(NZ)] for x in range(NX)]
RIGHT = [(z * NX + x, z * NX + (x + 1) % NX) for z in range(NZ) for x in range(NX)]
FAR = [(z * NX + x, z * NX + (x + 2) % NX) for z in range(NZ) for x in range(NX)]
LEFT = [(z * NX + x, z * NX + (x - 1) % NX) for z in range(NZ) for x in range(NX)]


def to_right(a):
    return lax.ppermute(a, "dev", RIGHT)


def to_left(a):
    return lax.ppermute(a, "dev", LEFT)


def to_far(a):
    return lax.ppermute(a, "dev", FAR)


def along_z(a):
    return lax.all_to_all(
        a, "dev", split_axis=0, concat_axis=0, axis_index_groups=Z_RINGS, tiled=True
    )


def in_hbm(*arrays):
    return [pltpu.with_memory_space_constraint(a, pltpu.HBM) for a in arrays]


def turn(row):
    n = row.shape[1]
    at = lax.broadcasted_iota(jnp.int32, (n, n), 0)
    to = lax.broadcasted_iota(jnp.int32, (n, n), 1)
    return jnp.sum(jnp.where(at == to, row, 0.0), axis=1, keepdims=True)


def pack_rows_kernel(
    queries_ref, routes_ref, gain_ref, keys_ref, values_ref, out_ref, both_ref, sems
):
    copies = [
        pltpu.make_async_copy(ref, both_ref.at[at], sems.at[at])
        for at, ref in enumerate((keys_ref, values_ref))
    ]
    for copy in copies:
        copy.start()
    rows = queries_ref[...].astype(F32)
    mean_sq = jnp.mean(rows * rows, axis=-1, keepdims=True)
    normed = (rows * lax.rsqrt(mean_sq + 1e-06) * gain_ref[...]).astype(BF)
    routes = routes_ref[...]
    beams = rows.shape[0]
    at = lax.broadcasted_iota(jnp.int32, (beams, beams), 0)
    to = lax.broadcasted_iota(jnp.int32, (beams, beams), 1)
    place = lax.broadcasted_iota(jnp.int32, (CAP, beams), 0).astype(F32)
    for expert in range(EXPF):
        mine = jnp.sum((routes == expert).astype(F32), axis=0, keepdims=True)
        slot = jnp.sum(jnp.where(at < to, turn(mine), 0.0), axis=0, keepdims=True)
        picker = jnp.where((place == slot) & (mine > 0.5), 1.0, 0.0).astype(BF)
        packed = jnp.dot(picker, normed, preferred_element_type=F32).astype(BF)
        for z in range(HALF):
            out_ref[expert * HALF + z] = packed
    for copy in copies:
        copy.wait()


def pack_rows(queries, routes, gain, keys, values):
    width = queries.shape[1]
    args = (queries, routes, gain.reshape(1, width), keys, values)
    args = in_hbm(*args)
    return pl.pallas_call(
        pack_rows_kernel,
        in_specs=[pl.BlockSpec(memory_space=pltpu.VMEM)] * 3
        + [pl.BlockSpec(memory_space=pl.ANY)] * 2,
        out_specs=[
            pl.BlockSpec(memory_space=pltpu.VMEM),
            pl.BlockSpec(memory_space=pl.ANY),
        ],
        out_shape=[
            jax.ShapeDtypeStruct((NZ, CAP, width), BF),
            jax.ShapeDtypeStruct((2, *keys.shape), BF),
        ],
        scratch_shapes=[pltpu.SemaphoreType.DMA((2,))],
        cost_estimate=pl.CostEstimate(
            flops=4_000_000, bytes_accessed=1_200_000, transcendentals=32
        ),
        compiler_params=pltpu.CompilerParams(vmem_limit_bytes=4 * 2**20),
        name="pack_rows",
    )(*args)


def finish_kernel(own_ref, left_ref, right_ref, far_ref, mixed_ref, out_ref):
    span = out_ref.shape[2]
    pieces = own_ref.shape[1] // span
    for piece in range(pieces):
        cols = slice(piece * span, (piece + 1) * span)
        total = own_ref[:, cols].astype(F32) + left_ref[:, cols].astype(F32)
        total = total + right_ref[:, cols].astype(F32) + far_ref[:, cols].astype(F32)
        out_ref[:, piece * CAP : (piece + 1) * CAP, :] = total.astype(BF).reshape(NZ, CAP, span)
    out_ref[:, pieces * CAP :, :] = mixed_ref[...]


def finish(own, left, right, far, mixed):
    beams, span = mixed.shape[1:]
    pieces = own.shape[1] // span
    return pl.pallas_call(
        finish_kernel,
        out_shape=jax.ShapeDtypeStruct((NZ, pieces * CAP + beams, span), BF),
        cost_estimate=pl.CostEstimate(
            flops=1_000_000, bytes_accessed=2_900_000, transcendentals=0
        ),
        compiler_params=pltpu.CompilerParams(vmem_limit_bytes=8 * 2**20),
        name="finish",
    )(own, left, right, far, mixed)


def combine_kernel(ret_ref, routes_ref, gate_ref, context_ref, routed_ref):
    routes = routes_ref[...]
    gate = gate_ref[...]
    beams = routes.shape[1]
    span = ret_ref.shape[2]
    pieces = routed_ref.shape[1] // span
    at = lax.broadcasted_iota(jnp.int32, (beams, beams), 0)
    to = lax.broadcasted_iota(jnp.int32, (beams, beams), 1)
    place = lax.broadcasted_iota(jnp.int32, (beams, CAP), 1).astype(F32)
    spread = []
    for expert in range(EXPF):
        mine = jnp.sum((routes == expert).astype(F32), axis=0, keepdims=True)
        slot = jnp.sum(jnp.where(to < at, mine, 0.0), axis=1, keepdims=True)
        weight = jnp.sum(jnp.where(routes == expert, gate, 0.0), axis=0, keepdims=True)
        spread.append(jnp.where((place == slot) & (turn(mine) > 0.5), turn(weight), 0.0))
    for piece in range(pieces):
        rows = slice(piece * CAP, (piece + 1) * CAP)
        total = None
        for expert in range(EXPF):
            summed = ret_ref[expert * HALF, rows, :].astype(F32)
            for z in range(1, HALF):
                summed = summed + ret_ref[expert * HALF + z, rows, :].astype(F32)
            part = jnp.dot(
                spread[expert],
                summed,
                precision=lax.Precision.HIGHEST,
                preferred_element_type=F32,
            )
            total = part if total is None else total + part
        routed_ref[:, piece * span : (piece + 1) * span] = total.astype(BF)
    for z in range(NZ):
        context_ref[:, z * span : (z + 1) * span] = ret_ref[z, pieces * CAP :, :]


def combine(ret, routes, gate, beams, width):
    shape = jax.ShapeDtypeStruct((beams, width), BF)
    return pl.pallas_call(
        combine_kernel,
        out_shape=[shape, shape],
        cost_estimate=pl.CostEstimate(
            flops=25_000_000, bytes_accessed=1_000_000, transcendentals=0
        ),
        compiler_params=pltpu.CompilerParams(vmem_limit_bytes=6 * 2**20),
        name="combine",
    )(ret, routes, gate)


def pack_heads_kernel(q_ref, own_ref, left_ref, right_ref, far_ref, out_ref):
    rows = q_ref.shape[0]
    shard = own_ref.shape[1]
    span = out_ref.shape[2]
    for z in range(NZ):
        cols = slice(z * span, (z + 1) * span)
        at = 0
        for which in (0, 1):
            for ref in (own_ref, left_ref, right_ref, far_ref):
                out_ref[z, at : at + shard, :] = ref[which, :, cols]
                at += shard
        out_ref[z, at : at + rows, :] = q_ref[:, cols]


def pack_heads(queries, own, left, right, far):
    rows, width = queries.shape
    shard = own.shape[1]
    return pl.pallas_call(
        pack_heads_kernel,
        out_shape=jax.ShapeDtypeStruct((NZ, 2 * NX * shard + rows, width // NZ), BF),
        cost_estimate=pl.CostEstimate(
            flops=20_000_000_000, bytes_accessed=2_400_000, transcendentals=0
        ),
        compiler_params=pltpu.CompilerParams(vmem_limit_bytes=8 * 2**20),
        name="pack_heads",
    )(queries, own, left, right, far)


def valid_positions(counts, shard):
    users, shards = counts.shape
    offsets = shard // users
    total = shards * shard
    at = lax.broadcasted_iota(jnp.int32, (shards, total), 1)
    shard_of = at // shard
    step = shard_of % NX
    step = jnp.where(step == 1, NX - 1, jnp.where(step == 2, 1, jnp.where(step == 3, 2, 0)))
    x = (lax.axis_index("dev") + step) % NX
    source = shard_of // NX * NX + x
    spread = (source == lax.broadcasted_iota(jnp.int32, (shards, total), 0)).astype(F32)
    found = jnp.dot(counts.astype(F32), spread, preferred_element_type=F32)
    at = at[:users]
    user = at // offsets % users
    mine = user == lax.broadcasted_iota(jnp.int32, (users, total), 0)
    limit = jnp.sum(jnp.where(mine, found, 0.0), axis=0, keepdims=True)
    return user[:1], (at[:1] % offsets).astype(F32) < limit - 0.5


def attend_kernel(owner_ref, got_ref, counts_ref, out_ref, *, beams, group):
    span = got_ref.shape[2]
    memory = (got_ref.shape[1] - beams) // 2
    count = NZ * memory
    user, valid = valid_positions(counts_ref[...], memory // NX)
    x = lax.axis_index("dev") % NX
    biases = []
    for src in range(NZ):
        mine = user == owner_ref[src * NX + x]
        biases.append(jnp.where(mine & valid, 0.0, -1e30))
    for head in range(span // HEAD):
        cols = slice(head * HEAD, (head + 1) * HEAD)
        keys = got_ref[:, 0:memory, cols].reshape(count, HEAD)
        values = got_ref[:, memory : 2 * memory, cols].reshape(count, HEAD)
        for src in range(0, NZ, group):
            own = slice(src, src + group)
            rows = got_ref[own, 2 * memory : 2 * memory + beams, cols]
            rows = rows.reshape(group * beams, HEAD)
            scores = lax.dot_general(
                rows, keys, (((1,), (1,)), ((), ())), preferred_element_type=F32
            )
            scores = jnp.concatenate(
                [
                    scores[at * beams : (at + 1) * beams] * HEAD ** (-0.5) + biases[src + at]
                    for at in range(group)
                ],
                axis=0,
            )
            top = jnp.max(scores, axis=-1, keepdims=True)
            expo = jnp.exp(scores - top)
            total = jnp.sum(expo, axis=-1, keepdims=True)
            weights = (expo * (1.0 / total)).astype(BF)
            mixed = jnp.dot(weights, values, preferred_element_type=F32).astype(BF)
            out_ref[own, :, cols] = mixed.reshape(group, beams, HEAD)


def attend(got, counts, owner, beams):
    span = got.shape[2]
    return pl.pallas_call(
        functools.partial(attend_kernel, beams=beams, group=2),
        in_specs=[
            pl.BlockSpec(memory_space=pltpu.SMEM),
            pl.BlockSpec(memory_space=pltpu.VMEM),
            pl.BlockSpec(memory_space=pltpu.VMEM),
        ],
        out_shape=jax.ShapeDtypeStruct((NZ, beams, span), BF),
        cost_estimate=pl.CostEstimate(
            flops=300_000_000, bytes_accessed=1_400_000, transcendentals=600_000
        ),
        compiler_params=pltpu.CompilerParams(vmem_limit_bytes=12 * 2**20),
        name="attend",
    )(owner, got, *in_hbm(counts))


def experts_kernel(rows_ref, up_ref, down_ref, out_ref, up, down, sems):
    copies = []
    for which, (source, target) in enumerate(((up_ref, up), (down_ref, down))):
        size = target.shape[0] // 2
        for half in range(2):
            own = slice(half * size, (half + 1) * size)
            copies.append(
                pltpu.make_async_copy(source.at[own], target.at[own], sems.at[which, half])
            )
            copies[-1].start()
    value = rows_ref[...]
    for which, weight in enumerate((up, down)):
        size = weight.shape[0] // 2
        total = None
        for half in range(2):
            own = slice(half * size, (half + 1) * size)
            copies[which * 2 + half].wait()
            part = jnp.dot(value[:, own], weight[own, :], preferred_element_type=F32)
            total = part if total is None else total + part
        if which == 0:
            value = (total / (1.0 + jnp.exp(-total))).astype(BF)
    out_ref[...] = total.astype(BF)


def experts(rows, up, down):
    size = rows.shape[0]
    width, hidden = up.shape
    return pl.pallas_call(
        experts_kernel,
        in_specs=[pl.BlockSpec(memory_space=pltpu.VMEM)]
        + [pl.BlockSpec(memory_space=pl.ANY)] * 2,
        out_shape=jax.ShapeDtypeStruct(rows.shape, BF),
        scratch_shapes=[
            pltpu.VMEM(up.shape, up.dtype),
            pltpu.VMEM(down.shape, down.dtype),
            pltpu.SemaphoreType.DMA((2, 2)),
        ],
        cost_estimate=pl.CostEstimate(
            flops=400 * size * width * hidden,
            bytes_accessed=4 * width * hidden + 4 * size * width,
            transcendentals=size * hidden,
        ),
        compiler_params=pltpu.CompilerParams(vmem_limit_bytes=10 * 2**20),
        name="experts",
    )(rows, *in_hbm(up, down))


def on_device(
    queries, keys, values, kv_count, beam_user, routes, route_gate, norm_gain, w_up, w_down
):
    beams, width = queries.shape
    users, shard_len, _ = keys.shape
    shard = users * shard_len
    x = lax.rem(lax.axis_index("dev"), NX)

    routes, route_gate = routes.T, route_gate.T

    size = NZ * CAP
    packed, own = pack_rows(
        queries, routes, norm_gain, keys.reshape(shard, width), values.reshape(shard, width)
    )
    left, right, far = to_right(own), to_left(own), to_far(own)
    block = along_z(packed).reshape(size, width)
    block, far = lax.optimization_barrier((block, far))
    block_f, block_l, block_r = to_far(block), to_right(block), to_left(block)
    part = experts(block, w_up, w_down)

    got = along_z(pack_heads(queries, own, left, right, far))
    mixed = attend(got, kv_count, beam_user, beams)

    part_l = experts(block_l, w_up, w_down)
    from_r = to_left(part_l)
    part_r = experts(block_r, w_up, w_down)
    from_l = to_right(part_r)
    part_f = experts(block_f, w_up, w_down)
    from_f = to_far(part_f)
    ret = along_z(finish(part, from_l, from_r, from_f, mixed))
    context, routed = combine(ret, routes, route_gate, beams, width)
    return (context, routed)


def solution(mesh):
    return jax.shard_map(
        on_device,
        mesh=mesh,
        in_specs=(
            P(("user", "dev"), None),
            P("user", "dev", None),
            P("user", "dev", None),
            P("user", None),
            P("user"),
            P(("user", "dev"), None),
            P(("user", "dev"), None),
            P(),
            P(None, "dev"),
            P("dev", None),
        ),
        out_specs=(P(("user", "dev"), None), P(("user", "dev"), None)),
        check_vma=False,
    )
```

time: 157 us -> 110 us (0.70)
  waiting for transfers between devices: 41.2 us -> 14.7 us
  blocking collectives: 0 us -> 21.5 us
  local copies, waits for them, and re-layouts: 20.5 us -> 0.92 us
  starting transfers between devices: 64.6 us -> 49 us
  other arithmetic: 6.27 us -> 0 us
    all_to_all x0 -> x1, blocking collectives: none -> 21.5 us  [along_z(): lax.all_to_all(a, 'dev', split_axis=0, concat_axis=0, axis_index_groups=Z...]
    ppermute x6 -> x3, starting transfers between devices: 25.1 us -> 10.2 us  [to_left(): return lax.ppermute(a, 'dev', LEFT)]
    all_to_all x4 -> x2, waiting for transfers between devices: 27.1 us -> 12.6 us  [along_z(): lax.all_to_all(a, 'dev', split_axis=0, concat_axis=0, axis_index_groups=Z...]
    unnamed x44 -> x8, local copies, waits for them, and re-layouts: 14.5 us -> 0.92 us
    ppermute x0 -> x3, starting transfers between devices: none -> 11.8 us  [to_far(): return lax.ppermute(a, 'dev', FAR)]
    ppermute x6 -> x3, waiting for transfers between devices: 8.52 us -> 1.74 us  [to_right(): return lax.ppermute(a, 'dev', RIGHT)]
    ppermute x6 -> x3, starting transfers between devices: 15 us -> 8.58 us  [to_right(): return lax.ppermute(a, 'dev', RIGHT)]
    all_to_all x4 -> x2, starting transfers between devices: 24.5 us -> 18.5 us  [along_z(): lax.all_to_all(a, 'dev', split_axis=0, concat_axis=0, axis_index_groups=Z...]
  transfers between devices with their start and end apart: 16 -> 11, of which waited for: 6 -> 4; matrix products, arithmetic and copies ran while one was open for 8% -> 0% of each run, Pallas kernels for 11% -> 16%
where the time goes in v2:
time: 110 us
  starting transfers between devices  49 us (45%)
  Pallas kernels  22.7 us (21%)
  blocking collectives  21.5 us (20%)
  waiting for transfers between devices  14.7 us (13%)
    all_to_all x1, blocking collectives, along_z(): lax.all_to_all(a, 'dev', split_axis=0, concat_axis=0, axis_index_groups=Z...  21.5 us
    all_to_all x2, starting transfers between devices, along_z(): lax.all_to_all(a, 'dev', split_axis=0, concat_axis=0, axis_index_groups=Z...  18.5 us
    all_to_all x2, waiting for transfers between devices, along_z(): lax.all_to_all(a, 'dev', split_axis=0, concat_axis=0, axis_index_groups=Z...  12.6 us
    ppermute x3, starting transfers between devices, to_far(): return lax.ppermute(a, 'dev', FAR)  11.8 us
    pallas_call x4, Pallas kernels, experts(): pl.pallas_call(experts_kernel, in_specs=[pl.BlockSpec(memory_space=pltpu....  11.4 us
    ppermute x3, starting transfers between devices, to_left(): return lax.ppermute(a, 'dev', LEFT)  10.2 us
    ppermute x3, starting transfers between devices, to_right(): return lax.ppermute(a, 'dev', RIGHT)  8.58 us
    pallas_call x1, Pallas kernels, attend(): pl.pallas_call(functools.partial(attend_kernel, beams=beams, group=2), in...  4.88 us
  transfers between devices with their start and end apart: 11, of which 4 were waited for; matrix products, arithmetic and copies ran while one was open for 0% of the time, Pallas kernels for 16%

profile of v2, /device:TPU:32, one launch (start us, length us, event | category | flops | bytes accessed | tf_op | source)
XLA Modules:
  0.0 109.7 jit_solution(4468189627734927201)
XLA Ops:
  0.6 2.7 %pack_rows.1 = (bf16[8,16,2048]{2,1,0:T(8,128)(2,1)}, bf16[2,32,2048]{2,1,0:T(8,128)(2,1)S(1)}) custom-call(bf16[32,2048]{1,0:T(8,128)(2,1)} %q_ref.1, s32[2,32]{1,0:T(2,128)} %bitcast.10, f32[1,2048]{1,0:T(1,128)} %bitcast.15, bf16[32,2048]{1,0:T(8,128)(2,1)} %bitcast.13, bf16[32,2048]{1,0:T(8,128)(2,1)} %bitcast.14), custom_call_target="tpu_custom_call" | custom-call | flops 4000000 | bytes 1200000 | tf_op jit(solution)/shard_map/pack_rows/pallas_call | solution.py:86
  3.3 10.3 %all-to-all-start = ((bf16[8,16,2048]{2,1,0:T(8,128)(2,1)}), bf16[8,16,2048]{2,1,0:T(8,128)(2,1)S(1)}, u32[]{:S(2)}, u32[]{:S(2)}) async-start(bf16[8,16,2048]{2,1,0:T(8,128)(2,1)} %get-tuple-element.6), calls=%async_computation | async-start | bytes 1048576 | tf_op jit(solution)/shard_map/all_to_all | solution.py:38
  13.7 4.9 %collective-permute-start = (bf16[2,32,2048]{2,1,0:T(8,128)(2,1)S(1)}, bf16[2,32,2048]{2,1,0:T(8,128)(2,1)S(1)}, u32[]{:S(2)}, u32[]{:S(2)}) collective-permute-start(bf16[2,32,2048]{2,1,0:T(8,128)(2,1)S(1)} %get-tuple-element.7.own_ref), channel_id=1, source_target_pairs={{0,2},{1,3},{2,0},{3,1},{4,6},{5,7},{6,4},{7,5},{8,10},{9,11},{10,... | collective-permute-start | bytes 786440 | tf_op jit(solution)/shard_map/ppermute | solution.py:34
  18.6 3.0 %collective-permute-start.8 = (bf16[2,32,2048]{2,1,0:T(8,128)(2,1)S(1)}, bf16[2,32,2048]{2,1,0:T(8,128)(2,1)S(1)}, u32[]{:S(2)}, u32[]{:S(2)}) collective-permute-start(bf16[2,32,2048]{2,1,0:T(8,128)(2,1)S(1)} %get-tuple-element.7.own_ref), channel_id=1, source_target_pairs={{0,3},{1,0},{2,1},{3,2},{4,7},{5,4},{6,5},{7,6},{8,11},{9,8},{10,9... | collective-permute-start | bytes 786440 | tf_op jit(solution)/shard_map/ppermute | solution.py:30
  21.6 2.8 %collective-permute-start.7 = (bf16[2,32,2048]{2,1,0:T(8,128)(2,1)S(1)}, bf16[2,32,2048]{2,1,0:T(8,128)(2,1)S(1)}, u32[]{:S(2)}, u32[]{:S(2)}) collective-permute-start(bf16[2,32,2048]{2,1,0:T(8,128)(2,1)S(1)} %get-tuple-element.7.own_ref), channel_id=1, source_target_pairs={{0,1},{1,2},{2,3},{3,0},{4,5},{5,6},{6,7},{7,4},{8,9},{9,10},{10,1... | collective-permute-start | bytes 786440 | tf_op jit(solution)/shard_map/ppermute | solution.py:26
  24.8 6.3 %all-to-all-done = bf16[8,16,2048]{2,1,0:T(8,128)(2,1)S(1)} async-done(((bf16[8,16,2048]{2,1,0:T(8,128)(2,1)}), bf16[8,16,2048]{2,1,0:T(8,128)(2,1)S(1)}, u32[]{:S(2)}, u32[]{:S(2)}) %all-to-all-start) | async-done | bytes 524320 | tf_op jit(solution)/shard_map/all_to_all | solution.py:38
  31.2 4.9 %collective-permute-start.5 = (bf16[128,2048]{1,0:T(8,128)(2,1)S(1)}, bf16[128,2048]{1,0:T(8,128)(2,1)S(1)}, u32[]{:S(2)}, u32[]{:S(2)}) collective-permute-start(bf16[128,2048]{1,0:T(8,128)(2,1)S(1)} %bitcast.6), channel_id=1, source_target_pairs={{0,2},{1,3},{2,0},{3,1},{4,6},{5,7},{6,4},{7,5},{8,10},{9,11},{10,... | collective-permute-start | bytes 1572872 | tf_op jit(solution)/shard_map/ppermute | solution.py:34
  36.1 2.5 %collective-permute-start.3 = (bf16[128,2048]{1,0:T(8,128)(2,1)S(1)}, bf16[128,2048]{1,0:T(8,128)(2,1)S(1)}, u32[]{:S(2)}, u32[]{:S(2)}) collective-permute-start(bf16[128,2048]{1,0:T(8,128)(2,1)S(1)} %bitcast.7), channel_id=1, source_target_pairs={{0,1},{1,2},{2,3},{3,0},{4,5},{5,6},{6,7},{7,4},{8,9},{9,10},{10,1... | collective-permute-start | bytes 1572872 | tf_op jit(solution)/shard_map/ppermute | solution.py:26
  38.6 4.6 %collective-permute-start.1 = (bf16[128,2048]{1,0:T(8,128)(2,1)S(1)}, bf16[128,2048]{1,0:T(8,128)(2,1)S(1)}, u32[]{:S(2)}, u32[]{:S(2)}) collective-permute-start(bf16[128,2048]{1,0:T(8,128)(2,1)S(1)} %bitcast.8), channel_id=1, source_target_pairs={{0,3},{1,0},{2,1},{3,2},{4,7},{5,4},{6,5},{7,6},{8,11},{9,8},{10,9... | collective-permute-start | bytes 1572872 | tf_op jit(solution)/shard_map/ppermute | solution.py:30
  44.1 1.1 %pack_heads.1 = bf16[8,288,256]{2,1,0:T(8,128)(2,1)} custom-call(bf16[32,2048]{1,0:T(8,128)(2,1)S(1)} %copy-done, bf16[2,32,2048]{2,1,0:T(8,128)(2,1)S(1)} %get-tuple-element.7.own_ref, bf16[2,32,2048]{2,1,0:T(8,128)(2,1)S(1)} %collective-permute-done.7.left_ref, bf16[2,32,2048]{2,1,0:T(8,128)(2,1)S(1)} %collective-permute-done.8.right_ref, ...), custom_call_target="tpu_custom_call" | custom-call | flops 20000000000 | bytes 2400000 | tf_op jit(solution)/shard_map/pack_heads/pallas_call | solution.py:196
  45.2 8.2 %all-to-all-start.1 = ((bf16[8,288,256]{2,1,0:T(8,128)(2,1)}), bf16[8,288,256]{2,1,0:T(8,128)(2,1)}, u32[]{:S(2)}, u32[]{:S(2)}) async-start(bf16[8,288,256]{2,1,0:T(8,128)(2,1)} %pack_heads.1), calls=%async_computation.1 | async-start | bytes 2359296 | tf_op jit(solution)/shard_map/all_to_all | solution.py:38
  53.4 3.5 %experts.7 = bf16[128,2048]{1,0:T(8,128)(2,1)} custom-call(bf16[128,2048]{1,0:T(8,128)(2,1)S(1)} %collective-permute-done.5.rows_ref, bf16[2048,512]{1,0:T(8,128)(2,1)} %up_ref.7, bf16[512,2048]{1,0:T(8,128)(2,1)} %down_ref.7), custom_call_target="tpu_custom_call" | custom-call | flops 53687091200 | bytes 5242880 | tf_op jit(solution)/shard_map/experts/pallas_call | solution.py:307
  56.9 1.9 %collective-permute-start.6 = (bf16[128,2048]{1,0:T(8,128)(2,1)}, bf16[128,2048]{1,0:T(8,128)(2,1)}, u32[]{:S(2)}, u32[]{:S(2)}) collective-permute-start(bf16[128,2048]{1,0:T(8,128)(2,1)} %experts.7), channel_id=1, source_target_pairs={{0,2},{1,3},{2,0},{3,1},{4,6},{5,7},{6,4},{7,5},{8,10},{9,11},{10,... | collective-permute-start | bytes 1572872 | tf_op jit(solution)/shard_map/ppermute | solution.py:34
  58.8 1.7 %collective-permute-done.3.rows_ref = bf16[128,2048]{1,0:T(8,128)(2,1)S(1)} collective-permute-done((bf16[128,2048]{1,0:T(8,128)(2,1)S(1)}, bf16[128,2048]{1,0:T(8,128)(2,1)S(1)}, u32[]{:S(2)}, u32[]{:S(2)}) %collective-permute-start.3) | collective-permute-done | bytes 524320 | tf_op jit(solution)/shard_map/ppermute | solution.py:26
  60.5 2.7 %experts.6 = bf16[128,2048]{1,0:T(8,128)(2,1)S(1)} custom-call(bf16[128,2048]{1,0:T(8,128)(2,1)S(1)} %collective-permute-done.3.rows_ref, bf16[2048,512]{1,0:T(8,128)(2,1)} %up_ref.7, bf16[512,2048]{1,0:T(8,128)(2,1)} %down_ref.7), custom_call_target="tpu_custom_call" | custom-call | flops 53687091200 | bytes 5242880 | tf_op jit(solution)/shard_map/experts/pallas_call | solution.py:307
  63.2 2.6 %collective-permute-start.4 = (bf16[128,2048]{1,0:T(8,128)(2,1)S(1)}, bf16[128,2048]{1,0:T(8,128)(2,1)S(1)}, u32[]{:S(2)}, u32[]{:S(2)}) collective-permute-start(bf16[128,2048]{1,0:T(8,128)(2,1)S(1)} %experts.6), channel_id=1, source_target_pairs={{0,3},{1,0},{2,1},{3,2},{4,7},{5,4},{6,5},{7,6},{8,11},{9,8},{10,9... | collective-permute-start | bytes 1572872 | tf_op jit(solution)/shard_map/ppermute | solution.py:30
  65.8 2.7 %experts.5 = bf16[128,2048]{1,0:T(8,128)(2,1)S(1)} custom-call(bf16[128,2048]{1,0:T(8,128)(2,1)S(1)} %collective-permute-done.1.rows_ref, bf16[2048,512]{1,0:T(8,128)(2,1)} %up_ref.7, bf16[512,2048]{1,0:T(8,128)(2,1)} %down_ref.7), custom_call_target="tpu_custom_call" | custom-call | flops 53687091200 | bytes 5242880 | tf_op jit(solution)/shard_map/experts/pallas_call | solution.py:307
  68.4 3.3 %collective-permute-start.2 = (bf16[128,2048]{1,0:T(8,128)(2,1)S(1)}, bf16[128,2048]{1,0:T(8,128)(2,1)S(1)}, u32[]{:S(2)}, u32[]{:S(2)}) collective-permute-start(bf16[128,2048]{1,0:T(8,128)(2,1)S(1)} %experts.5), channel_id=1, source_target_pairs={{0,1},{1,2},{2,3},{3,0},{4,5},{5,6},{6,7},{7,4},{8,9},{9,10},{10,1... | collective-permute-start | bytes 1572872 | tf_op jit(solution)/shard_map/ppermute | solution.py:26
  71.7 2.7 %experts.4.own_ref = bf16[128,2048]{1,0:T(8,128)(2,1)S(1)} custom-call(bf16[128,2048]{1,0:T(8,128)(2,1)S(1)} %bitcast.9, bf16[2048,512]{1,0:T(8,128)(2,1)} %up_ref.7, bf16[512,2048]{1,0:T(8,128)(2,1)} %down_ref.7), custom_call_target="tpu_custom_call" | custom-call | flops 53687091200 | bytes 5242880 | tf_op jit(solution)/shard_map/experts/pallas_call | solution.py:307
  74.4 6.3 %all-to-all-done.1.got_ref = bf16[8,288,256]{2,1,0:T(8,128)(2,1)} async-done(((bf16[8,288,256]{2,1,0:T(8,128)(2,1)}), bf16[8,288,256]{2,1,0:T(8,128)(2,1)}, u32[]{:S(2)}, u32[]{:S(2)}) %all-to-all-start.1) | async-done | bytes 1179680 | tf_op jit(solution)/shard_map/all_to_all | solution.py:38
  80.7 4.9 %attend.1.mixed_ref = bf16[8,32,256]{2,1,0:T(8,128)(2,1)S(1)} custom-call(s32[32]{0:T(128)S(1)} %copy-done.3, bf16[8,288,256]{2,1,0:T(8,128)(2,1)} %all-to-all-done.1.got_ref, s32[4,32]{1,0:T(4,128)} %counts_ref.1), custom_call_target="tpu_custom_call" | custom-call | flops 300000000 | bytes 1400000 | tf_op jit(solution)/shard_map/attend/pallas_call | solution.py:264
  85.6 1.3 %finish.1 = bf16[8,160,256]{2,1,0:T(8,128)(2,1)S(1)} custom-call(bf16[128,2048]{1,0:T(8,128)(2,1)S(1)} %experts.4.own_ref, bf16[128,2048]{1,0:T(8,128)(2,1)S(1)} %collective-permute-done.2.left_ref, bf16[128,2048]{1,0:T(8,128)(2,1)S(1)} %collective-permute-done.4.right_ref, bf16[128,2048]{1,0:T(8,128)(2,1)} %collective-permute-done.6.far_ref, ...), custom_call_target="tpu_custom_call" | custom-call | flops 1000000 | bytes 2900000 | tf_op jit(solution)/shard_map/finish/pallas_call | solution.py:121
  86.9 21.5 %all_to_all.15.ret_ref = bf16[8,160,256]{2,1,0:T(8,128)(2,1)S(1)} all-to-all(bf16[8,160,256]{2,1,0:T(8,128)(2,1)S(1)} %finish.1), channel_id=1, replica_groups={{0,4,8,12,16,20,24,28},{1,5,9,13,17,21,25,29},{2,6,10,14,18,22,26,30},{..., dimensions={0} | all-to-all | bytes 1310720 | tf_op jit(solution)/shard_map/all_to_all | solution.py:38
  108.4 1.3 %combine.1 = (bf16[32,2048]{1,0:T(8,128)(2,1)}, bf16[32,2048]{1,0:T(8,128)(2,1)}) custom-call(bf16[8,160,256]{2,1,0:T(8,128)(2,1)S(1)} %all_to_all.15.ret_ref, s32[2,32]{1,0:T(2,128)S(1)} %bitcast.11, f32[2,32]{1,0:T(2,128)S(1)} %bitcast.12), custom_call_target="tpu_custom_call" | custom-call | flops 25000000 | bytes 1000000 | tf_op jit(solution)/shard_map/combine/pallas_call | solution.py:168
  (16 shorter events, 1.3 us)
Async XLA Ops:
  3.3 27.8 %all-to-all-start = ((bf16[8,16,2048]{2,1,0:T(8,128)(2,1)}), bf16[8,16,2048]{2,1,0:T(8,128)(2,1)S(1)}, u32[]{:S(2)}, u32[]{:S(2)}) async-start(bf16[8,16,2048]{2,1,0:T(8,128)(2,1)} %get-tuple-element.6), calls=%async_computation | async-start | bytes 1048576 | tf_op jit(solution)/shard_map/all_to_all | solution.py:38
  13.7 11.2 %collective-permute-start = (bf16[2,32,2048]{2,1,0:T(8,128)(2,1)S(1)}, bf16[2,32,2048]{2,1,0:T(8,128)(2,1)S(1)}, u32[]{:S(2)}, u32[]{:S(2)}) collective-permute-start(bf16[2,32,2048]{2,1,0:T(8,128)(2,1)S(1)} %get-tuple-element.7.own_ref), channel_id=1, source_target_pairs={{0,2},{1,3},{2,0},{3,1},{4,6},{5,7},{6,4},{7,5},{8,10},{9,11},{10,... | collective-permute-start | bytes 786440 | tf_op jit(solution)/shard_map/ppermute | solution.py:34
  18.6 24.6 %collective-permute-start.8 = (bf16[2,32,2048]{2,1,0:T(8,128)(2,1)S(1)}, bf16[2,32,2048]{2,1,0:T(8,128)(2,1)S(1)}, u32[]{:S(2)}, u32[]{:S(2)}) collective-permute-start(bf16[2,32,2048]{2,1,0:T(8,128)(2,1)S(1)} %get-tuple-element.7.own_ref), channel_id=1, source_target_pairs={{0,3},{1,0},{2,1},{3,2},{4,7},{5,4},{6,5},{7,6},{8,11},{9,8},{10,9... | collective-permute-start | bytes 786440 | tf_op jit(solution)/shard_map/ppermute | solution.py:30
  21.6 21.5 %collective-permute-start.7 = (bf16[2,32,2048]{2,1,0:T(8,128)(2,1)S(1)}, bf16[2,32,2048]{2,1,0:T(8,128)(2,1)S(1)}, u32[]{:S(2)}, u32[]{:S(2)}) collective-permute-start(bf16[2,32,2048]{2,1,0:T(8,128)(2,1)S(1)} %get-tuple-element.7.own_ref), channel_id=1, source_target_pairs={{0,1},{1,2},{2,3},{3,0},{4,5},{5,6},{6,7},{7,4},{8,9},{9,10},{10,1... | collective-permute-start | bytes 786440 | tf_op jit(solution)/shard_map/ppermute | solution.py:26
  31.2 22.2 %collective-permute-start.5 = (bf16[128,2048]{1,0:T(8,128)(2,1)S(1)}, bf16[128,2048]{1,0:T(8,128)(2,1)S(1)}, u32[]{:S(2)}, u32[]{:S(2)}) collective-permute-start(bf16[128,2048]{1,0:T(8,128)(2,1)S(1)} %bitcast.6), channel_id=1, source_target_pairs={{0,2},{1,3},{2,0},{3,1},{4,6},{5,7},{6,4},{7,5},{8,10},{9,11},{10,... | collective-permute-start | bytes 1572872 | tf_op jit(solution)/shard_map/ppermute | solution.py:34
  36.1 24.4 %collective-permute-start.3 = (bf16[128,2048]{1,0:T(8,128)(2,1)S(1)}, bf16[128,2048]{1,0:T(8,128)(2,1)S(1)}, u32[]{:S(2)}, u32[]{:S(2)}) collective-permute-start(bf16[128,2048]{1,0:T(8,128)(2,1)S(1)} %bitcast.7), channel_id=1, source_target_pairs={{0,1},{1,2},{2,3},{3,0},{4,5},{5,6},{6,7},{7,4},{8,9},{9,10},{10,1... | collective-permute-start | bytes 1572872 | tf_op jit(solution)/shard_map/ppermute | solution.py:26
  38.6 27.2 %collective-permute-start.1 = (bf16[128,2048]{1,0:T(8,128)(2,1)S(1)}, bf16[128,2048]{1,0:T(8,128)(2,1)S(1)}, u32[]{:S(2)}, u32[]{:S(2)}) collective-permute-start(bf16[128,2048]{1,0:T(8,128)(2,1)S(1)} %bitcast.8), channel_id=1, source_target_pairs={{0,3},{1,0},{2,1},{3,2},{4,7},{5,4},{6,5},{7,6},{8,11},{9,8},{10,9... | collective-permute-start | bytes 1572872 | tf_op jit(solution)/shard_map/ppermute | solution.py:30
  43.2 0.9 copy-start
  45.2 35.5 %all-to-all-start.1 = ((bf16[8,288,256]{2,1,0:T(8,128)(2,1)}), bf16[8,288,256]{2,1,0:T(8,128)(2,1)}, u32[]{:S(2)}, u32[]{:S(2)}) async-start(bf16[8,288,256]{2,1,0:T(8,128)(2,1)} %pack_heads.1), calls=%async_computation.1 | async-start | bytes 2359296 | tf_op jit(solution)/shard_map/all_to_all | solution.py:38
  56.9 28.7 %collective-permute-start.6 = (bf16[128,2048]{1,0:T(8,128)(2,1)}, bf16[128,2048]{1,0:T(8,128)(2,1)}, u32[]{:S(2)}, u32[]{:S(2)}) collective-permute-start(bf16[128,2048]{1,0:T(8,128)(2,1)} %experts.7), channel_id=1, source_target_pairs={{0,2},{1,3},{2,0},{3,1},{4,6},{5,7},{6,4},{7,5},{8,10},{9,11},{10,... | collective-permute-start | bytes 1572872 | tf_op jit(solution)/shard_map/ppermute | solution.py:34
  63.2 22.4 %collective-permute-start.4 = (bf16[128,2048]{1,0:T(8,128)(2,1)S(1)}, bf16[128,2048]{1,0:T(8,128)(2,1)S(1)}, u32[]{:S(2)}, u32[]{:S(2)}) collective-permute-start(bf16[128,2048]{1,0:T(8,128)(2,1)S(1)} %experts.6), channel_id=1, source_target_pairs={{0,3},{1,0},{2,1},{3,2},{4,7},{5,4},{6,5},{7,6},{8,11},{9,8},{10,9... | collective-permute-start | bytes 1572872 | tf_op jit(solution)/shard_map/ppermute | solution.py:30
  68.4 12.2 %copy-start.3 = (s32[32]{0:T(128)S(1)}, s32[32]{0:T(128)}, u32[]{:S(2)}) copy-start(s32[32]{0:T(128)} %owner_ref.1) | copy-start | bytes 388
  68.4 17.2 %collective-permute-start.2 = (bf16[128,2048]{1,0:T(8,128)(2,1)S(1)}, bf16[128,2048]{1,0:T(8,128)(2,1)S(1)}, u32[]{:S(2)}, u32[]{:S(2)}) collective-permute-start(bf16[128,2048]{1,0:T(8,128)(2,1)S(1)} %experts.5), channel_id=1, source_target_pairs={{0,1},{1,2},{2,3},{3,0},{4,5},{5,6},{6,7},{7,4},{8,9},{9,10},{10,1... | collective-permute-start | bytes 1572872 | tf_op jit(solution)/shard_map/ppermute | solution.py:26
  85.6 22.9 %copy-start.1 = (s32[32,2]{0,1:T(2,128)S(1)}, s32[32,2]{0,1:T(2,128)}, u32[]{:S(2)}) copy-start(s32[32,2]{0,1:T(2,128)} %param.15) | copy-start | bytes 772
  85.6 22.9 %copy-start.2 = (f32[32,2]{0,1:T(2,128)S(1)}, f32[32,2]{0,1:T(2,128)}, u32[]{:S(2)}) copy-start(f32[32,2]{0,1:T(2,128)} %param.16) | copy-start | bytes 772

commit v3 on v2

--- a/solution.py
+++ b/solution.py
@@ -16,7 +16,8 @@
 BF = jnp.bfloat16
 F32 = jnp.float32
 
-Z_RINGS = [[z * NX + x for z in range(NZ)] for x in range(NX)]
+FIRST = list(range(NZ))
+LAST = list(range(NZ))[::-1]
 RIGHT = [(z * NX + x, z * NX + (x + 1) % NX) for z in range(NZ) for x in range(NX)]
 FAR = [(z * NX + x, z * NX + (x + 2) % NX) for z in range(NZ) for x in range(NX)]
 LEFT = [(z * NX + x, z * NX + (x - 1) % NX) for z in range(NZ) for x in range(NX)]
@@ -34,9 +35,10 @@
     return lax.ppermute(a, "dev", FAR)
 
 
-def along_z(a):
+def along_z(a, order=tuple(range(NZ))):
+    rings = [[z * NX + x for z in order] for x in range(NX)]
     return lax.all_to_all(
-        a, "dev", split_axis=0, concat_axis=0, axis_index_groups=Z_RINGS, tiled=True
+        a, "dev", split_axis=0, concat_axis=0, axis_index_groups=rings, tiled=True
     )
 
 
@@ -51,15 +53,7 @@
     return jnp.sum(jnp.where(at == to, row, 0.0), axis=1, keepdims=True)
 
 
-def pack_rows_kernel(
-    queries_ref, routes_ref, gain_ref, keys_ref, values_ref, out_ref, both_ref, sems
-):
-    copies = [
-        pltpu.make_async_copy(ref, both_ref.at[at], sems.at[at])
-        for at, ref in enumerate((keys_ref, values_ref))
-    ]
-    for copy in copies:
-        copy.start()
+def pack_rows_kernel(queries_ref, routes_ref, gain_ref, out_ref):
     rows = queries_ref[...].astype(F32)
     mean_sq = jnp.mean(rows * rows, axis=-1, keepdims=True)
     normed = (rows * lax.rsqrt(mean_sq + 1e-06) * gain_ref[...]).astype(BF)
@@ -73,46 +67,36 @@
         slot = jnp.sum(jnp.where(at < to, turn(mine), 0.0), axis=0, keepdims=True)
         picker = jnp.where((place == slot) & (mine > 0.5), 1.0, 0.0).astype(BF)
         packed = jnp.dot(picker, normed, preferred_element_type=F32).astype(BF)
-        for z in range(HALF):
-            out_ref[expert * HALF + z] = packed
-    for copy in copies:
-        copy.wait()
-
-
-def pack_rows(queries, routes, gain, keys, values):
+        for z in range(expert * HALF, (expert + 1) * HALF):
+            out_ref[FIRST.index(z)] = packed
+
+
+def pack_rows(queries, routes, gain):
     width = queries.shape[1]
-    args = (queries, routes, gain.reshape(1, width), keys, values)
-    args = in_hbm(*args)
     return pl.pallas_call(
         pack_rows_kernel,
-        in_specs=[pl.BlockSpec(memory_space=pltpu.VMEM)] * 3
-        + [pl.BlockSpec(memory_space=pl.ANY)] * 2,
-        out_specs=[
-            pl.BlockSpec(memory_space=pltpu.VMEM),
-            pl.BlockSpec(memory_space=pl.ANY),
-        ],
-        out_shape=[
-            jax.ShapeDtypeStruct((NZ, CAP, width), BF),
-            jax.ShapeDtypeStruct((2, *keys.shape), BF),
-        ],
-        scratch_shapes=[pltpu.SemaphoreType.DMA((2,))],
-        cost_estimate=pl.CostEstimate(
-            flops=4_000_000, bytes_accessed=1_200_000, transcendentals=32
+        out_shape=jax.ShapeDtypeStruct((NZ, CAP, width), BF),
+        cost_estimate=pl.CostEstimate(
+            flops=4_000_000, bytes_accessed=700_000, transcendentals=32
         ),
         compiler_params=pltpu.CompilerParams(vmem_limit_bytes=4 * 2**20),
         name="pack_rows",
-    )(*args)
+    )(*in_hbm(queries, routes, gain.reshape(1, width)))
 
 
 def finish_kernel(own_ref, left_ref, right_ref, far_ref, mixed_ref, out_ref):
     span = out_ref.shape[2]
     pieces = own_ref.shape[1] // span
-    for piece in range(pieces):
-        cols = slice(piece * span, (piece + 1) * span)
-        total = own_ref[:, cols].astype(F32) + left_ref[:, cols].astype(F32)
-        total = total + right_ref[:, cols].astype(F32) + far_ref[:, cols].astype(F32)
-        out_ref[:, piece * CAP : (piece + 1) * CAP, :] = total.astype(BF).reshape(NZ, CAP, span)
-    out_ref[:, pieces * CAP :, :] = mixed_ref[...]
+    for z in range(NZ):
+        rows = slice(FIRST.index(z) * CAP, (FIRST.index(z) + 1) * CAP)
+        place = LAST.index(z)
+        total = own_ref[rows].astype(F32) + left_ref[rows].astype(F32)
+        total = total + right_ref[rows].astype(F32) + far_ref[rows].astype(F32)
+        total = total.astype(BF)
+        for piece in range(pieces):
+            cols = slice(piece * span, (piece + 1) * span)
+            out_ref[place, piece * CAP : (piece + 1) * CAP, :] = total[:, cols]
+        out_ref[place, pieces * CAP :, :] = mixed_ref[z]
 
 
 def finish(own, left, right, far, mixed):
@@ -148,9 +132,10 @@
         rows = slice(piece * CAP, (piece + 1) * CAP)
         total = None
         for expert in range(EXPF):
-            summed = ret_ref[expert * HALF, rows, :].astype(F32)
-            for z in range(1, HALF):
-                summed = summed + ret_ref[expert * HALF + z, rows, :].astype(F32)
+            summed = None
+            for z in range(expert * HALF, (expert + 1) * HALF):
+                term = ret_ref[LAST.index(z), rows, :].astype(F32)
+                summed = term if summed is None else summed + term
             part = jnp.dot(
                 spread[expert],
                 summed,
@@ -160,7 +145,7 @@
             total = part if total is None else total + part
         routed_ref[:, piece * span : (piece + 1) * span] = total.astype(BF)
     for z in range(NZ):
-        context_ref[:, z * span : (z + 1) * span] = ret_ref[z, pieces * CAP :, :]
+        context_ref[:, z * span : (z + 1) * span] = ret_ref[LAST.index(z), pieces * CAP :, :]
 
 
 def combine(ret, routes, gate, beams, width):
@@ -262,7 +247,7 @@
 def attend(got, counts, owner, beams):
     span = got.shape[2]
     return pl.pallas_call(
-        functools.partial(attend_kernel, beams=beams, group=2),
+        functools.partial(attend_kernel, beams=beams, group=8),
         in_specs=[
             pl.BlockSpec(memory_space=pltpu.SMEM),
             pl.BlockSpec(memory_space=pltpu.VMEM),
@@ -277,38 +262,49 @@
     )(owner, got, *in_hbm(counts))
 
 
-def experts_kernel(rows_ref, up_ref, down_ref, out_ref, up, down, sems):
+def experts_kernel(*refs):
+    *ins, up_ref, down_ref = refs[: len(refs) // 2]
+    *outs, up, down, sems = refs[len(refs) // 2 :]
+    parts = 2
     copies = []
     for which, (source, target) in enumerate(((up_ref, up), (down_ref, down))):
-        size = target.shape[0] // 2
-        for half in range(2):
-            own = slice(half * size, (half + 1) * size)
+        size = target.shape[0] // parts
+        for part in range(parts):
+            own = slice(part * size, (part + 1) * size)
             copies.append(
-                pltpu.make_async_copy(source.at[own], target.at[own], sems.at[which, half])
+                pltpu.make_async_copy(source.at[own], target.at[own], sems.at[which, part])
             )
-            copies[-1].start()
-    value = rows_ref[...]
+    ahead = 4
+    for copy in copies[:ahead]:
+        copy.start()
+    value = jnp.concatenate([ref[...] for ref in ins], axis=0)
     for which, weight in enumerate((up, down)):
-        size = weight.shape[0] // 2
+        size = weight.shape[0] // parts
         total = None
-        for half in range(2):
-            own = slice(half * size, (half + 1) * size)
-            copies[which * 2 + half].wait()
-            part = jnp.dot(value[:, own], weight[own, :], preferred_element_type=F32)
-            total = part if total is None else total + part
+        for part in range(parts):
+            own = slice(part * size, (part + 1) * size)
+            index = which * parts + part
+            copies[index].wait()
+            if index + ahead < len(copies):
+                copies[index + ahead].start()
+            term = jnp.dot(value[:, own], weight[own, :], preferred_element_type=F32)
+            total = term if total is None else total + term
         if which == 0:
             value = (total / (1.0 + jnp.exp(-total))).astype(BF)
-    out_ref[...] = total.astype(BF)
-
-
-def experts(rows, up, down):
-    size = rows.shape[0]
+    size = ins[0].shape[0]
+    for index, out_ref in enumerate(outs):
+        out_ref[...] = total[index * size : (index + 1) * size].astype(BF)
+
+
+def experts(blocks, up, down):
+    count = len(blocks)
+    size = count * blocks[0].shape[0]
     width, hidden = up.shape
     return pl.pallas_call(
         experts_kernel,
-        in_specs=[pl.BlockSpec(memory_space=pltpu.VMEM)]
+        in_specs=[pl.BlockSpec(memory_space=pltpu.VMEM)] * count
         + [pl.BlockSpec(memory_space=pl.ANY)] * 2,
-        out_shape=jax.ShapeDtypeStruct(rows.shape, BF),
+        out_shape=[jax.ShapeDtypeStruct(block.shape, BF) for block in blocks],
         scratch_shapes=[
             pltpu.VMEM(up.shape, up.dtype),
             pltpu.VMEM(down.shape, down.dtype),
@@ -319,9 +315,9 @@
             bytes_accessed=4 * width * hidden + 4 * size * width,
             transcendentals=size * hidden,
         ),
-        compiler_params=pltpu.CompilerParams(vmem_limit_bytes=10 * 2**20),
+        compiler_params=pltpu.CompilerParams(vmem_limit_bytes=14 * 2**20),
         name="experts",
-    )(rows, *in_hbm(up, down))
+    )(*blocks, *in_hbm(up, down))
 
 
 def on_device(
@@ -335,25 +331,22 @@
     routes, route_gate = routes.T, route_gate.T
 
     size = NZ * CAP
-    packed, own = pack_rows(
-        queries, routes, norm_gain, keys.reshape(shard, width), values.reshape(shard, width)
-    )
+    packed = pack_rows(queries, routes, norm_gain)
+    own = jnp.stack([keys.reshape(shard, width), values.reshape(shard, width)])
     left, right, far = to_right(own), to_left(own), to_far(own)
-    block = along_z(packed).reshape(size, width)
+    block = along_z(packed, FIRST).reshape(size, width)
     block, far = lax.optimization_barrier((block, far))
     block_f, block_l, block_r = to_far(block), to_right(block), to_left(block)
-    part = experts(block, w_up, w_down)
+    (part,) = experts([block], w_up, w_down)
 
     got = along_z(pack_heads(queries, own, left, right, far))
     mixed = attend(got, kv_count, beam_user, beams)
 
-    part_l = experts(block_l, w_up, w_down)
-    from_r = to_left(part_l)
-    part_r = experts(block_r, w_up, w_down)
-    from_l = to_right(part_r)
-    part_f = experts(block_f, w_up, w_down)
+    part_l, part_r = experts([block_l, block_r], w_up, w_down)
+    from_r, from_l = to_left(part_l), to_right(part_r)
+    (part_f,) = experts([block_f], w_up, w_down)
     from_f = to_far(part_f)
-    ret = along_z(finish(part, from_l, from_r, from_f, mixed))
+    ret = along_z(finish(part, from_l, from_r, from_f, mixed), LAST)
     context, routed = combine(ret, routes, route_gate, beams, width)
     return (context, routed)
 

time: 110 us -> 105 us (0.955)
  the two profiles are of different devices: /device:TPU:32 before, /device:TPU:52 now
where the time goes in v3:
time: 105 us
  starting transfers between devices  43.8 us (42%)
  waiting for transfers between devices  20.9 us (20%)
  blocking collectives  20.6 us (20%)
  Pallas kernels  17.7 us (17%)
    all_to_all x1, blocking collectives, along_z(): lax.all_to_all(a, 'dev', split_axis=0, concat_axis=0, axis_index_groups=r...  20.6 us
    all_to_all x2, starting transfers between devices, along_z(): lax.all_to_all(a, 'dev', split_axis=0, concat_axis=0, axis_index_groups=r...  14.6 us
    ppermute x3, starting transfers between devices, to_far(): return lax.ppermute(a, 'dev', FAR)  11.4 us
    ppermute x3, starting transfers between devices, to_left(): return lax.ppermute(a, 'dev', LEFT)  10.9 us
    all_to_all x2, waiting for transfers between devices, along_z(): lax.all_to_all(a, 'dev', split_axis=0, concat_axis=0, axis_index_groups=r...  9.33 us
    pallas_call x3, Pallas kernels, experts(): pl.pallas_call(experts_kernel, in_specs=[pl.BlockSpec(memory_space=pltpu....  9.26 us
    ppermute x3, waiting for transfers between devices, to_far(): return lax.ppermute(a, 'dev', FAR)  7.39 us
    ppermute x3, starting transfers between devices, to_right(): return lax.ppermute(a, 'dev', RIGHT)  6.95 us
  transfers between devices with their start and end apart: 11, of which 8 were waited for; matrix products, arithmetic and copies ran while one was open for 1% of the time, Pallas kernels for 12%

profile of v3, /device:TPU:52, one launch (start us, length us, event | category | flops | bytes accessed | tf_op | source)
XLA Modules:
  0.0 104.8 jit_solution(2565826874087096075)
XLA Ops:
  0.6 2.0 %pack_rows.1 = bf16[8,16,2048]{2,1,0:T(8,128)(2,1)} custom-call(bf16[32,2048]{1,0:T(8,128)(2,1)} %q_ref.1, s32[2,32]{1,0:T(2,128)} %bitcast.10, f32[1,2048]{1,0:T(1,128)} %bitcast.15), custom_call_target="tpu_custom_call" | custom-call | flops 4000000 | bytes 700000 | tf_op jit(solution)/shard_map/pack_rows/pallas_call | solution.py:76
  2.7 10.3 %all-to-all-start = ((bf16[8,16,2048]{2,1,0:T(8,128)(2,1)}), bf16[8,16,2048]{2,1,0:T(8,128)(2,1)S(1)}, u32[]{:S(2)}, u32[]{:S(2)}) async-start(bf16[8,16,2048]{2,1,0:T(8,128)(2,1)} %pack_rows.1), calls=%async_computation | async-start | bytes 1048576 | tf_op jit(solution)/shard_map/all_to_all | solution.py:40
  14.0 2.4 %collective-permute-start = (bf16[2,32,2048]{2,1,0:T(8,128)(2,1)S(1)}, bf16[2,32,2048]{2,1,0:T(8,128)(2,1)S(1)}, u32[]{:S(2)}, u32[]{:S(2)}) collective-permute-start(bf16[2,32,2048]{2,1,0:T(8,128)(2,1)S(1)} %pad_maximum_fusion.own_ref), channel_id=1, source_target_pairs={{0,2},{1,3},{2,0},{3,1},{4,6},{5,7},{6,4},{7,5},{8,10},{9,11},{10,... | collective-permute-start | bytes 786440 | tf_op jit(solution)/shard_map/ppermute | solution.py:35
  16.4 4.1 %collective-permute-start.8 = (bf16[2,32,2048]{2,1,0:T(8,128)(2,1)S(1)}, bf16[2,32,2048]{2,1,0:T(8,128)(2,1)S(1)}, u32[]{:S(2)}, u32[]{:S(2)}) collective-permute-start(bf16[2,32,2048]{2,1,0:T(8,128)(2,1)S(1)} %pad_maximum_fusion.own_ref), channel_id=1, source_target_pairs={{0,3},{1,0},{2,1},{3,2},{4,7},{5,4},{6,5},{7,6},{8,11},{9,8},{10,9... | collective-permute-start | bytes 786440 | tf_op jit(solution)/shard_map/ppermute | solution.py:31
  20.5 1.9 %collective-permute-start.7 = (bf16[2,32,2048]{2,1,0:T(8,128)(2,1)S(1)}, bf16[2,32,2048]{2,1,0:T(8,128)(2,1)S(1)}, u32[]{:S(2)}, u32[]{:S(2)}) collective-permute-start(bf16[2,32,2048]{2,1,0:T(8,128)(2,1)S(1)} %pad_maximum_fusion.own_ref), channel_id=1, source_target_pairs={{0,1},{1,2},{2,3},{3,0},{4,5},{5,6},{6,7},{7,4},{8,9},{9,10},{10,1... | collective-permute-start | bytes 786440 | tf_op jit(solution)/shard_map/ppermute | solution.py:27
  22.4 3.0 %collective-permute-done.far_ref = bf16[2,32,2048]{2,1,0:T(8,128)(2,1)S(1)} collective-permute-done((bf16[2,32,2048]{2,1,0:T(8,128)(2,1)S(1)}, bf16[2,32,2048]{2,1,0:T(8,128)(2,1)S(1)}, u32[]{:S(2)}, u32[]{:S(2)}) %collective-permute-start) | collective-permute-done | bytes 262176 | tf_op jit(solution)/shard_map/ppermute | solution.py:35
  25.4 5.1 %all-to-all-done = bf16[8,16,2048]{2,1,0:T(8,128)(2,1)S(1)} async-done(((bf16[8,16,2048]{2,1,0:T(8,128)(2,1)}), bf16[8,16,2048]{2,1,0:T(8,128)(2,1)S(1)}, u32[]{:S(2)}, u32[]{:S(2)}) %all-to-all-start) | async-done | bytes 524320 | tf_op jit(solution)/shard_map/all_to_all | solution.py:40
  30.5 2.4 %collective-permute-start.5 = (bf16[128,2048]{1,0:T(8,128)(2,1)S(1)}, bf16[128,2048]{1,0:T(8,128)(2,1)S(1)}, u32[]{:S(2)}, u32[]{:S(2)}) collective-permute-start(bf16[128,2048]{1,0:T(8,128)(2,1)S(1)} %bitcast.6), channel_id=1, source_target_pairs={{0,2},{1,3},{2,0},{3,1},{4,6},{5,7},{6,4},{7,5},{8,10},{9,11},{10,... | collective-permute-start | bytes 1572872 | tf_op jit(solution)/shard_map/ppermute | solution.py:35
  32.9 4.1 %collective-permute-start.2 = (bf16[128,2048]{1,0:T(8,128)(2,1)S(1)}, bf16[128,2048]{1,0:T(8,128)(2,1)S(1)}, u32[]{:S(2)}, u32[]{:S(2)}) collective-permute-start(bf16[128,2048]{1,0:T(8,128)(2,1)S(1)} %bitcast.7), channel_id=1, source_target_pairs={{0,3},{1,0},{2,1},{3,2},{4,7},{5,4},{6,5},{7,6},{8,11},{9,8},{10,9... | collective-permute-start | bytes 1572872 | tf_op jit(solution)/shard_map/ppermute | solution.py:31
  37.0 1.9 %collective-permute-start.1 = (bf16[128,2048]{1,0:T(8,128)(2,1)S(1)}, bf16[128,2048]{1,0:T(8,128)(2,1)S(1)}, u32[]{:S(2)}, u32[]{:S(2)}) collective-permute-start(bf16[128,2048]{1,0:T(8,128)(2,1)S(1)} %bitcast.8), channel_id=1, source_target_pairs={{0,1},{1,2},{2,3},{3,0},{4,5},{5,6},{6,7},{7,4},{8,9},{9,10},{10,1... | collective-permute-start | bytes 1572872 | tf_op jit(solution)/shard_map/ppermute | solution.py:27
  40.0 4.3 %all-to-all-start.1 = ((bf16[8,288,256]{2,1,0:T(8,128)(2,1)}), bf16[8,288,256]{2,1,0:T(8,128)(2,1)}, u32[]{:S(2)}, u32[]{:S(2)}) async-start(bf16[8,288,256]{2,1,0:T(8,128)(2,1)} %pack_heads.1), calls=%async_computation.1 | async-start | bytes 2359296 | tf_op jit(solution)/shard_map/all_to_all | solution.py:40
  44.3 4.4 %collective-permute-done.5.refs_0_ = bf16[128,2048]{1,0:T(8,128)(2,1)S(1)} collective-permute-done((bf16[128,2048]{1,0:T(8,128)(2,1)S(1)}, bf16[128,2048]{1,0:T(8,128)(2,1)S(1)}, u32[]{:S(2)}, u32[]{:S(2)}) %collective-permute-start.5) | collective-permute-done | bytes 524320 | tf_op jit(solution)/shard_map/ppermute | solution.py:35
  48.7 3.5 %experts.5 = bf16[128,2048]{1,0:T(8,128)(2,1)} custom-call(bf16[128,2048]{1,0:T(8,128)(2,1)S(1)} %collective-permute-done.5.refs_0_, bf16[2048,512]{1,0:T(8,128)(2,1)} %refs_1_.3, bf16[512,2048]{1,0:T(8,128)(2,1)} %refs_2_.5), custom_call_target="tpu_custom_call" | custom-call | flops 53687091200 | bytes 5242880 | tf_op jit(solution)/shard_map/experts/pallas_call | solution.py:303
  52.2 6.5 %collective-permute-start.6 = (bf16[128,2048]{1,0:T(8,128)(2,1)}, bf16[128,2048]{1,0:T(8,128)(2,1)}, u32[]{:S(2)}, u32[]{:S(2)}) collective-permute-start(bf16[128,2048]{1,0:T(8,128)(2,1)} %experts.5), channel_id=1, source_target_pairs={{0,2},{1,3},{2,0},{3,1},{4,6},{5,7},{6,4},{7,5},{8,10},{9,11},{10,... | collective-permute-start | bytes 1572872 | tf_op jit(solution)/shard_map/ppermute | solution.py:35
  59.9 3.1 %experts.4 = (bf16[128,2048]{1,0:T(8,128)(2,1)S(1)}, bf16[128,2048]{1,0:T(8,128)(2,1)S(1)}) custom-call(bf16[128,2048]{1,0:T(8,128)(2,1)S(1)} %collective-permute-done.1.refs_0_, bf16[128,2048]{1,0:T(8,128)(2,1)S(1)} %collective-permute-done.2.refs_1_, bf16[2048,512]{1,0:T(8,128)(2,1)} %refs_1_.3, bf16[512,2048]{1,0:T(8,128)(2,1)} %refs_2_.5), custom_call_target="tpu_custom_call" | custom-call | flops 107374182400 | bytes 6291456 | tf_op jit(solution)/shard_map/experts/pallas_call | solution.py:303
  63.0 3.1 %collective-permute-start.3 = (bf16[128,2048]{1,0:T(8,128)(2,1)S(1)}, bf16[128,2048]{1,0:T(8,128)(2,1)S(1)}, u32[]{:S(2)}, u32[]{:S(2)}) collective-permute-start(bf16[128,2048]{1,0:T(8,128)(2,1)S(1)} %get-tuple-element.7), channel_id=1, source_target_pairs={{0,1},{1,2},{2,3},{3,0},{4,5},{5,6},{6,7},{7,4},{8,9},{9,10},{10,1... | collective-permute-start | bytes 1572872 | tf_op jit(solution)/shard_map/ppermute | solution.py:27
  66.1 2.7 %collective-permute-start.4 = (bf16[128,2048]{1,0:T(8,128)(2,1)S(1)}, bf16[128,2048]{1,0:T(8,128)(2,1)S(1)}, u32[]{:S(2)}, u32[]{:S(2)}) collective-permute-start(bf16[128,2048]{1,0:T(8,128)(2,1)S(1)} %get-tuple-element.8), channel_id=1, source_target_pairs={{0,3},{1,0},{2,1},{3,2},{4,7},{5,4},{6,5},{7,6},{8,11},{9,8},{10,9... | collective-permute-start | bytes 1572872 | tf_op jit(solution)/shard_map/ppermute | solution.py:31
  68.9 2.7 %experts.3.own_ref = bf16[128,2048]{1,0:T(8,128)(2,1)S(1)} custom-call(bf16[128,2048]{1,0:T(8,128)(2,1)S(1)} %bitcast.9, bf16[2048,512]{1,0:T(8,128)(2,1)} %refs_1_.3, bf16[512,2048]{1,0:T(8,128)(2,1)} %refs_2_.5), custom_call_target="tpu_custom_call" | custom-call | flops 53687091200 | bytes 5242880 | tf_op jit(solution)/shard_map/experts/pallas_call | solution.py:303
  71.5 4.3 %all-to-all-done.1.got_ref = bf16[8,288,256]{2,1,0:T(8,128)(2,1)} async-done(((bf16[8,288,256]{2,1,0:T(8,128)(2,1)}), bf16[8,288,256]{2,1,0:T(8,128)(2,1)}, u32[]{:S(2)}, u32[]{:S(2)}) %all-to-all-start.1) | async-done | bytes 1179680 | tf_op jit(solution)/shard_map/all_to_all | solution.py:40
  75.8 2.7 %attend.1.mixed_ref = bf16[8,32,256]{2,1,0:T(8,128)(2,1)S(1)} custom-call(s32[32]{0:T(128)S(1)} %copy-done.3, bf16[8,288,256]{2,1,0:T(8,128)(2,1)} %all-to-all-done.1.got_ref, s32[4,32]{1,0:T(4,128)} %counts_ref.1), custom_call_target="tpu_custom_call" | custom-call | flops 300000000 | bytes 1400000 | tf_op jit(solution)/shard_map/attend/pallas_call | solution.py:249
  78.6 2.9 %collective-permute-done.3.left_ref = bf16[128,2048]{1,0:T(8,128)(2,1)S(1)} collective-permute-done((bf16[128,2048]{1,0:T(8,128)(2,1)S(1)}, bf16[128,2048]{1,0:T(8,128)(2,1)S(1)}, u32[]{:S(2)}, u32[]{:S(2)}) %collective-permute-start.3) | collective-permute-done | bytes 524320 | tf_op jit(solution)/shard_map/ppermute | solution.py:27
  81.6 1.3 %finish.1 = bf16[8,160,256]{2,1,0:T(8,128)(2,1)S(1)} custom-call(bf16[128,2048]{1,0:T(8,128)(2,1)S(1)} %experts.3.own_ref, bf16[128,2048]{1,0:T(8,128)(2,1)S(1)} %collective-permute-done.3.left_ref, bf16[128,2048]{1,0:T(8,128)(2,1)S(1)} %collective-permute-done.4.right_ref, bf16[128,2048]{1,0:T(8,128)(2,1)} %collective-permute-done.6.far_ref, ...), custom_call_target="tpu_custom_call" | custom-call | flops 1000000 | bytes 2900000 | tf_op jit(solution)/shard_map/finish/pallas_call | solution.py:105
  82.9 20.6 %all_to_all.15.ret_ref = bf16[8,160,256]{2,1,0:T(8,128)(2,1)S(1)} all-to-all(bf16[8,160,256]{2,1,0:T(8,128)(2,1)S(1)} %finish.1), channel_id=1, replica_groups={{28,24,20,16,12,8,4,0},{29,25,21,17,13,9,5,1},{30,26,22,18,14,10,6,2},{..., dimensions={0} | all-to-all | bytes 1310720 | tf_op jit(solution)/shard_map/all_to_all | solution.py:40
  103.5 1.3 %combine.1 = (bf16[32,2048]{1,0:T(8,128)(2,1)}, bf16[32,2048]{1,0:T(8,128)(2,1)}) custom-call(bf16[8,160,256]{2,1,0:T(8,128)(2,1)S(1)} %all_to_all.15.ret_ref, s32[2,32]{1,0:T(2,128)S(1)} %bitcast.11, f32[2,32]{1,0:T(2,128)S(1)} %bitcast.12), custom_call_target="tpu_custom_call" | custom-call | flops 25000000 | bytes 1000000 | tf_op jit(solution)/shard_map/combine/pallas_call | solution.py:153
  (16 shorter events, 3.4 us)
Async XLA Ops:
  0.6 38.3 %copy-start = (bf16[32,2048]{1,0:T(8,128)(2,1)S(1)}, bf16[32,2048]{1,0:T(8,128)(2,1)}, u32[]{:S(2)}) copy-start(bf16[32,2048]{1,0:T(8,128)(2,1)} %q_ref.1) | copy-start | bytes 393220
  2.7 27.8 %all-to-all-start = ((bf16[8,16,2048]{2,1,0:T(8,128)(2,1)}), bf16[8,16,2048]{2,1,0:T(8,128)(2,1)S(1)}, u32[]{:S(2)}, u32[]{:S(2)}) async-start(bf16[8,16,2048]{2,1,0:T(8,128)(2,1)} %pack_rows.1), calls=%async_computation | async-start | bytes 1048576 | tf_op jit(solution)/shard_map/all_to_all | solution.py:40
  14.0 11.4 %collective-permute-start = (bf16[2,32,2048]{2,1,0:T(8,128)(2,1)S(1)}, bf16[2,32,2048]{2,1,0:T(8,128)(2,1)S(1)}, u32[]{:S(2)}, u32[]{:S(2)}) collective-permute-start(bf16[2,32,2048]{2,1,0:T(8,128)(2,1)S(1)} %pad_maximum_fusion.own_ref), channel_id=1, source_target_pairs={{0,2},{1,3},{2,0},{3,1},{4,6},{5,7},{6,4},{7,5},{8,10},{9,11},{10,... | collective-permute-start | bytes 786440 | tf_op jit(solution)/shard_map/ppermute | solution.py:35
  16.4 22.5 %collective-permute-start.8 = (bf16[2,32,2048]{2,1,0:T(8,128)(2,1)S(1)}, bf16[2,32,2048]{2,1,0:T(8,128)(2,1)S(1)}, u32[]{:S(2)}, u32[]{:S(2)}) collective-permute-start(bf16[2,32,2048]{2,1,0:T(8,128)(2,1)S(1)} %pad_maximum_fusion.own_ref), channel_id=1, source_target_pairs={{0,3},{1,0},{2,1},{3,2},{4,7},{5,4},{6,5},{7,6},{8,11},{9,8},{10,9... | collective-permute-start | bytes 786440 | tf_op jit(solution)/shard_map/ppermute | solution.py:31
  20.5 18.4 %collective-permute-start.7 = (bf16[2,32,2048]{2,1,0:T(8,128)(2,1)S(1)}, bf16[2,32,2048]{2,1,0:T(8,128)(2,1)S(1)}, u32[]{:S(2)}, u32[]{:S(2)}) collective-permute-start(bf16[2,32,2048]{2,1,0:T(8,128)(2,1)S(1)} %pad_maximum_fusion.own_ref), channel_id=1, source_target_pairs={{0,1},{1,2},{2,3},{3,0},{4,5},{5,6},{6,7},{7,4},{8,9},{9,10},{10,1... | collective-permute-start | bytes 786440 | tf_op jit(solution)/shard_map/ppermute | solution.py:27
  30.5 18.2 %collective-permute-start.5 = (bf16[128,2048]{1,0:T(8,128)(2,1)S(1)}, bf16[128,2048]{1,0:T(8,128)(2,1)S(1)}, u32[]{:S(2)}, u32[]{:S(2)}) collective-permute-start(bf16[128,2048]{1,0:T(8,128)(2,1)S(1)} %bitcast.6), channel_id=1, source_target_pairs={{0,2},{1,3},{2,0},{3,1},{4,6},{5,7},{6,4},{7,5},{8,10},{9,11},{10,... | collective-permute-start | bytes 1572872 | tf_op jit(solution)/shard_map/ppermute | solution.py:35
  32.9 26.1 %collective-permute-start.2 = (bf16[128,2048]{1,0:T(8,128)(2,1)S(1)}, bf16[128,2048]{1,0:T(8,128)(2,1)S(1)}, u32[]{:S(2)}, u32[]{:S(2)}) collective-permute-start(bf16[128,2048]{1,0:T(8,128)(2,1)S(1)} %bitcast.7), channel_id=1, source_target_pairs={{0,3},{1,0},{2,1},{3,2},{4,7},{5,4},{6,5},{7,6},{8,11},{9,8},{10,9... | collective-permute-start | bytes 1572872 | tf_op jit(solution)/shard_map/ppermute | solution.py:31
  37.0 22.9 %collective-permute-start.1 = (bf16[128,2048]{1,0:T(8,128)(2,1)S(1)}, bf16[128,2048]{1,0:T(8,128)(2,1)S(1)}, u32[]{:S(2)}, u32[]{:S(2)}) collective-permute-start(bf16[128,2048]{1,0:T(8,128)(2,1)S(1)} %bitcast.8), channel_id=1, source_target_pairs={{0,1},{1,2},{2,3},{3,0},{4,5},{5,6},{6,7},{7,4},{8,9},{9,10},{10,1... | collective-permute-start | bytes 1572872 | tf_op jit(solution)/shard_map/ppermute | solution.py:27
  40.0 35.8 %all-to-all-start.1 = ((bf16[8,288,256]{2,1,0:T(8,128)(2,1)}), bf16[8,288,256]{2,1,0:T(8,128)(2,1)}, u32[]{:S(2)}, u32[]{:S(2)}) async-start(bf16[8,288,256]{2,1,0:T(8,128)(2,1)} %pack_heads.1), calls=%async_computation.1 | async-start | bytes 2359296 | tf_op jit(solution)/shard_map/all_to_all | solution.py:40
  52.2 26.4 %collective-permute-start.6 = (bf16[128,2048]{1,0:T(8,128)(2,1)}, bf16[128,2048]{1,0:T(8,128)(2,1)}, u32[]{:S(2)}, u32[]{:S(2)}) collective-permute-start(bf16[128,2048]{1,0:T(8,128)(2,1)} %experts.5), channel_id=1, source_target_pairs={{0,2},{1,3},{2,0},{3,1},{4,6},{5,7},{6,4},{7,5},{8,10},{9,11},{10,... | collective-permute-start | bytes 1572872 | tf_op jit(solution)/shard_map/ppermute | solution.py:35
  63.0 18.5 %collective-permute-start.3 = (bf16[128,2048]{1,0:T(8,128)(2,1)S(1)}, bf16[128,2048]{1,0:T(8,128)(2,1)S(1)}, u32[]{:S(2)}, u32[]{:S(2)}) collective-permute-start(bf16[128,2048]{1,0:T(8,128)(2,1)S(1)} %get-tuple-element.7), channel_id=1, source_target_pairs={{0,1},{1,2},{2,3},{3,0},{4,5},{5,6},{6,7},{7,4},{8,9},{9,10},{10,1... | collective-permute-start | bytes 1572872 | tf_op jit(solution)/shard_map/ppermute | solution.py:27
  66.1 9.7 %copy-start.3 = (s32[32]{0:T(128)S(1)}, s32[32]{0:T(128)}, u32[]{:S(2)}) copy-start(s32[32]{0:T(128)} %owner_ref.1) | copy-start | bytes 388
  66.1 15.5 %collective-permute-start.4 = (bf16[128,2048]{1,0:T(8,128)(2,1)S(1)}, bf16[128,2048]{1,0:T(8,128)(2,1)S(1)}, u32[]{:S(2)}, u32[]{:S(2)}) collective-permute-start(bf16[128,2048]{1,0:T(8,128)(2,1)S(1)} %get-tuple-element.8), channel_id=1, source_target_pairs={{0,3},{1,0},{2,1},{3,2},{4,7},{5,4},{6,5},{7,6},{8,11},{9,8},{10,9... | collective-permute-start | bytes 1572872 | tf_op jit(solution)/shard_map/ppermute | solution.py:31
  78.5 25.0 %copy-start.1 = (s32[32,2]{0,1:T(2,128)S(1)}, s32[32,2]{0,1:T(2,128)}, u32[]{:S(2)}) copy-start(s32[32,2]{0,1:T(2,128)} %param.15) | copy-start | bytes 772
  78.5 25.0 %copy-start.2 = (f32[32,2]{0,1:T(2,128)S(1)}, f32[32,2]{0,1:T(2,128)}, u32[]{:S(2)}) copy-start(f32[32,2]{0,1:T(2,128)} %param.16) | copy-start | bytes 772

commit v4 on v3

--- a/solution.py
+++ b/solution.py
@@ -16,7 +16,7 @@
 BF = jnp.bfloat16
 F32 = jnp.float32
 
-FIRST = list(range(NZ))
+FIRST = [0, 4, 1, 5, 2, 6, 3, 7]
 LAST = list(range(NZ))[::-1]
 RIGHT = [(z * NX + x, z * NX + (x + 1) % NX) for z in range(NZ) for x in range(NX)]
 FAR = [(z * NX + x, z * NX + (x + 2) % NX) for z in range(NZ) for x in range(NX)]
@@ -84,71 +84,62 @@
     )(*in_hbm(queries, routes, gain.reshape(1, width)))
 
 
-def finish_kernel(own_ref, left_ref, right_ref, far_ref, mixed_ref, out_ref):
-    span = out_ref.shape[2]
-    pieces = own_ref.shape[1] // span
+def finish_kernel(own_ref, left_ref, right_ref, far_ref, out_ref):
     for z in range(NZ):
         rows = slice(FIRST.index(z) * CAP, (FIRST.index(z) + 1) * CAP)
-        place = LAST.index(z)
         total = own_ref[rows].astype(F32) + left_ref[rows].astype(F32)
         total = total + right_ref[rows].astype(F32) + far_ref[rows].astype(F32)
-        total = total.astype(BF)
-        for piece in range(pieces):
-            cols = slice(piece * span, (piece + 1) * span)
-            out_ref[place, piece * CAP : (piece + 1) * CAP, :] = total[:, cols]
-        out_ref[place, pieces * CAP :, :] = mixed_ref[z]
-
-
-def finish(own, left, right, far, mixed):
-    beams, span = mixed.shape[1:]
-    pieces = own.shape[1] // span
+        out_ref[LAST.index(z)] = total.astype(BF)
+
+
+def finish(own, left, right, far):
     return pl.pallas_call(
         finish_kernel,
-        out_shape=jax.ShapeDtypeStruct((NZ, pieces * CAP + beams, span), BF),
-        cost_estimate=pl.CostEstimate(
-            flops=1_000_000, bytes_accessed=2_900_000, transcendentals=0
+        out_shape=jax.ShapeDtypeStruct((NZ, CAP, own.shape[1]), BF),
+        cost_estimate=pl.CostEstimate(
+            flops=1_000_000, bytes_accessed=2_600_000, transcendentals=0
         ),
         compiler_params=pltpu.CompilerParams(vmem_limit_bytes=8 * 2**20),
         name="finish",
-    )(own, left, right, far, mixed)
-
-
-def combine_kernel(ret_ref, routes_ref, gate_ref, context_ref, routed_ref):
+    )(own, left, right, far)
+
+
+def combine_kernel(
+    ret_ref, mixed_ref, other_ref, routes_ref, gate_ref, context_ref, routed_ref
+):
     routes = routes_ref[...]
     gate = gate_ref[...]
     beams = routes.shape[1]
-    span = ret_ref.shape[2]
-    pieces = routed_ref.shape[1] // span
     at = lax.broadcasted_iota(jnp.int32, (beams, beams), 0)
     to = lax.broadcasted_iota(jnp.int32, (beams, beams), 1)
     place = lax.broadcasted_iota(jnp.int32, (beams, CAP), 1).astype(F32)
     spread = []
+    summed = []
     for expert in range(EXPF):
         mine = jnp.sum((routes == expert).astype(F32), axis=0, keepdims=True)
         slot = jnp.sum(jnp.where(to < at, mine, 0.0), axis=1, keepdims=True)
         weight = jnp.sum(jnp.where(routes == expert, gate, 0.0), axis=0, keepdims=True)
         spread.append(jnp.where((place == slot) & (turn(mine) > 0.5), turn(weight), 0.0))
-    for piece in range(pieces):
-        rows = slice(piece * CAP, (piece + 1) * CAP)
         total = None
-        for expert in range(EXPF):
-            summed = None
-            for z in range(expert * HALF, (expert + 1) * HALF):
-                term = ret_ref[LAST.index(z), rows, :].astype(F32)
-                summed = term if summed is None else summed + term
-            part = jnp.dot(
-                spread[expert],
-                summed,
-                precision=lax.Precision.HIGHEST,
-                preferred_element_type=F32,
-            )
-            total = part if total is None else total + part
-        routed_ref[:, piece * span : (piece + 1) * span] = total.astype(BF)
+        for z in range(expert * HALF, (expert + 1) * HALF):
+            term = ret_ref[LAST.index(z)].astype(F32)
+            total = term if total is None else total + term
+        summed.append(total)
+    routed_ref[...] = jnp.dot(
+        jnp.concatenate(spread, axis=1),
+        jnp.concatenate(summed, axis=0),
+        precision=lax.Precision.HIGHEST,
+        preferred_element_type=F32,
+    ).astype(BF)
+    odd = parity() == 1
     for z in range(NZ):
-        context_ref[:, z * span : (z + 1) * span] = ret_ref[LAST.index(z), pieces * CAP :, :]
-
-
-def combine(ret, routes, gate, beams, width):
+        mine, other = mixed_ref[z, :beams, :], other_ref[z, beams:, :]
+        first = 2 * z * HEAD
+        context_ref[:, first : first + HEAD] = jnp.where(odd, other, mine)
+        context_ref[:, first + HEAD : first + 2 * HEAD] = jnp.where(odd, mine, other)
+
+
+def combine(ret, mixed, other, routes, gate, beams, width):
     shape = jax.ShapeDtypeStruct((beams, width), BF)
     return pl.pallas_call(
         combine_kernel,
@@ -158,35 +149,73 @@
         ),
         compiler_params=pltpu.CompilerParams(vmem_limit_bytes=6 * 2**20),
         name="combine",
-    )(ret, routes, gate)
-
-
-def pack_heads_kernel(q_ref, own_ref, left_ref, right_ref, far_ref, out_ref):
-    rows = q_ref.shape[0]
-    shard = own_ref.shape[1]
-    span = out_ref.shape[2]
+    )(ret, mixed, other, routes, gate)
+
+
+def parity():
+    return lax.axis_index("dev") % 2
+
+
+def split_heads_kernel(
+    queries_ref, keys_ref, values_ref, right_ref, left_ref, far_ref, mine_ref
+):
+    odd = parity() == 1
+    rows = queries_ref.shape[0]
+    for at, ref in enumerate((keys_ref, values_ref, queries_ref)):
+        place = slice(at * rows, (at + 1) * rows)
+        for z in range(NZ):
+            first = ref[:, 2 * z * HEAD : (2 * z + 1) * HEAD]
+            second = ref[:, (2 * z + 1) * HEAD : (2 * z + 2) * HEAD]
+            same = jnp.where(odd, second, first)
+            other = jnp.where(odd, first, second)
+            cols = slice(z * HEAD, (z + 1) * HEAD)
+            mine_ref[place, cols] = same
+            right_ref[place, cols] = other
+            if at < 2:
+                far_ref[place, cols] = same
+                left_ref[place, cols] = other
+
+
+def split_heads(queries, keys, values):
+    rows, width = queries.shape
+    three = jax.ShapeDtypeStruct((3 * rows, width // 2), BF)
+    two = jax.ShapeDtypeStruct((2 * rows, width // 2), BF)
+    return pl.pallas_call(
+        split_heads_kernel,
+        out_shape=[three, two, two, three],
+        cost_estimate=pl.CostEstimate(
+            flops=200_000, bytes_accessed=1_700_000, transcendentals=0
+        ),
+        compiler_params=pltpu.CompilerParams(vmem_limit_bytes=6 * 2**20),
+        name="split_heads",
+    )(*in_hbm(queries, keys, values))
+
+
+def pack_heads_kernel(mine_ref, left_ref, right_ref, far_ref, out_ref):
+    rows = mine_ref.shape[0] // 3
     for z in range(NZ):
-        cols = slice(z * span, (z + 1) * span)
+        cols = slice(z * HEAD, (z + 1) * HEAD)
         at = 0
         for which in (0, 1):
-            for ref in (own_ref, left_ref, right_ref, far_ref):
-                out_ref[z, at : at + shard, :] = ref[which, :, cols]
-                at += shard
-        out_ref[z, at : at + rows, :] = q_ref[:, cols]
-
-
-def pack_heads(queries, own, left, right, far):
-    rows, width = queries.shape
-    shard = own.shape[1]
+            for ref in (mine_ref, left_ref, right_ref, far_ref):
+                out_ref[z, at : at + rows, :] = ref[which * rows : (which + 1) * rows, cols]
+                at += rows
+        for ref in (mine_ref, left_ref):
+            out_ref[z, at : at + rows, :] = ref[2 * rows :, cols]
+            at += rows
+
+
+def pack_heads(mine, left, right, far):
+    rows = mine.shape[0] // 3
     return pl.pallas_call(
         pack_heads_kernel,
-        out_shape=jax.ShapeDtypeStruct((NZ, 2 * NX * shard + rows, width // NZ), BF),
-        cost_estimate=pl.CostEstimate(
-            flops=20_000_000_000, bytes_accessed=2_400_000, transcendentals=0
-        ),
-        compiler_params=pltpu.CompilerParams(vmem_limit_bytes=8 * 2**20),
+        out_shape=jax.ShapeDtypeStruct((NZ, 2 * (NX + 1) * rows, HEAD), BF),
+        cost_estimate=pl.CostEstimate(
+            flops=20_000_000_000, bytes_accessed=1_300_000, transcendentals=0
+        ),
+        compiler_params=pltpu.CompilerParams(vmem_limit_bytes=6 * 2**20),
         name="pack_heads",
-    )(queries, own, left, right, far)
+    )(mine, left, right, far)
 
 
 def valid_positions(counts, shard):
@@ -208,54 +237,45 @@
     return user[:1], (at[:1] % offsets).astype(F32) < limit - 0.5
 
 
-def attend_kernel(owner_ref, got_ref, counts_ref, out_ref, *, beams, group):
-    span = got_ref.shape[2]
-    memory = (got_ref.shape[1] - beams) // 2
+def attend_kernel(owner_ref, got_ref, counts_ref, out_ref):
+    beams = out_ref.shape[1] // 2
+    memory = (got_ref.shape[1] - 2 * beams) // 2
     count = NZ * memory
     user, valid = valid_positions(counts_ref[...], memory // NX)
     x = lax.axis_index("dev") % NX
-    biases = []
-    for src in range(NZ):
-        mine = user == owner_ref[src * NX + x]
-        biases.append(jnp.where(mine & valid, 0.0, -1e30))
-    for head in range(span // HEAD):
-        cols = slice(head * HEAD, (head + 1) * HEAD)
-        keys = got_ref[:, 0:memory, cols].reshape(count, HEAD)
-        values = got_ref[:, memory : 2 * memory, cols].reshape(count, HEAD)
-        for src in range(0, NZ, group):
-            own = slice(src, src + group)
-            rows = got_ref[own, 2 * memory : 2 * memory + beams, cols]
-            rows = rows.reshape(group * beams, HEAD)
-            scores = lax.dot_general(
-                rows, keys, (((1,), (1,)), ((), ())), preferred_element_type=F32
-            )
-            scores = jnp.concatenate(
-                [
-                    scores[at * beams : (at + 1) * beams] * HEAD ** (-0.5) + biases[src + at]
-                    for at in range(group)
-                ],
-                axis=0,
-            )
-            top = jnp.max(scores, axis=-1, keepdims=True)
-            expo = jnp.exp(scores - top)
-            total = jnp.sum(expo, axis=-1, keepdims=True)
-            weights = (expo * (1.0 / total)).astype(BF)
-            mixed = jnp.dot(weights, values, preferred_element_type=F32).astype(BF)
-            out_ref[own, :, cols] = mixed.reshape(group, beams, HEAD)
+    keys = got_ref[:, 0:memory, :].reshape(count, HEAD)
+    values = got_ref[:, memory : 2 * memory, :].reshape(count, HEAD)
+    for at, column in enumerate((x, (x + NX - 1) % NX)):
+        first = 2 * memory + at * beams
+        rows = got_ref[:, first : first + beams, :].reshape(NZ * beams, HEAD)
+        scores = lax.dot_general(
+            rows, keys, (((1,), (1,)), ((), ())), preferred_element_type=F32
+        )
+        masked = []
+        for src in range(NZ):
+            mine = user == owner_ref[src * NX + column]
+            bias = jnp.where(mine & valid, 0.0, -1e30)
+            masked.append(scores[src * beams : (src + 1) * beams] * HEAD ** (-0.5) + bias)
+        scores = jnp.concatenate(masked, axis=0)
+        top = jnp.max(scores, axis=-1, keepdims=True)
+        expo = jnp.exp(scores - top)
+        total = jnp.sum(expo, axis=-1, keepdims=True)
+        weights = (expo * (1.0 / total)).astype(BF)
+        mixed = jnp.dot(weights, values, preferred_element_type=F32).astype(BF)
+        out_ref[:, at * beams : (at + 1) * beams, :] = mixed.reshape(NZ, beams, HEAD)
 
 
 def attend(got, counts, owner, beams):
-    span = got.shape[2]
-    return pl.pallas_call(
-        functools.partial(attend_kernel, beams=beams, group=8),
+    return pl.pallas_call(
+        attend_kernel,
         in_specs=[
             pl.BlockSpec(memory_space=pltpu.SMEM),
             pl.BlockSpec(memory_space=pltpu.VMEM),
             pl.BlockSpec(memory_space=pltpu.VMEM),
         ],
-        out_shape=jax.ShapeDtypeStruct((NZ, beams, span), BF),
-        cost_estimate=pl.CostEstimate(
-            flops=300_000_000, bytes_accessed=1_400_000, transcendentals=600_000
+        out_shape=jax.ShapeDtypeStruct((NZ, 2 * beams, HEAD), BF),
+        cost_estimate=pl.CostEstimate(
+            flops=300_000_000, bytes_accessed=1_000_000, transcendentals=600_000
         ),
         compiler_params=pltpu.CompilerParams(vmem_limit_bytes=12 * 2**20),
         name="attend",
@@ -326,28 +346,31 @@
     beams, width = queries.shape
     users, shard_len, _ = keys.shape
     shard = users * shard_len
-    x = lax.rem(lax.axis_index("dev"), NX)
 
     routes, route_gate = routes.T, route_gate.T
 
     size = NZ * CAP
     packed = pack_rows(queries, routes, norm_gain)
-    own = jnp.stack([keys.reshape(shard, width), values.reshape(shard, width)])
-    left, right, far = to_right(own), to_left(own), to_far(own)
+    for_right, for_left, for_far, mine = split_heads(
+        queries, keys.reshape(shard, width), values.reshape(shard, width)
+    )
+    left, right, far = to_right(for_right), to_left(for_left), to_far(for_far)
     block = along_z(packed, FIRST).reshape(size, width)
     block, far = lax.optimization_barrier((block, far))
     block_f, block_l, block_r = to_far(block), to_right(block), to_left(block)
     (part,) = experts([block], w_up, w_down)
 
-    got = along_z(pack_heads(queries, own, left, right, far))
-    mixed = attend(got, kv_count, beam_user, beams)
-
+    got = along_z(pack_heads(mine, left, right, far))
+    mixed = along_z(attend(got, kv_count, beam_user, beams))
+    other = to_left(mixed)
+
+    (part_f,) = experts([block_f], w_up, w_down)
+    from_f = to_far(part_f)
+    block_l, block_r, part, _ = lax.optimization_barrier((block_l, block_r, part, part_f))
     part_l, part_r = experts([block_l, block_r], w_up, w_down)
     from_r, from_l = to_left(part_l), to_right(part_r)
-    (part_f,) = experts([block_f], w_up, w_down)
-    from_f = to_far(part_f)
-    ret = along_z(finish(part, from_l, from_r, from_f, mixed), LAST)
-    context, routed = combine(ret, routes, route_gate, beams, width)
+    ret = along_z(finish(part, from_l, from_r, from_f), LAST)
+    context, routed = combine(ret, mixed, other, routes, route_gate, beams, width)
     return (context, routed)
 
 

time: 105 us -> 103 us (0.981)
  the two profiles are of different devices: /device:TPU:52 before, /device:TPU:104 now
where the time goes in v4:
time: 103 us; the launch traced here: 102 us
  starting transfers between devices  60.8 us (59%)
  waiting for transfers between devices  21.4 us (21%)
  Pallas kernels  18.9 us (18%)
    all_to_all x4, starting transfers between devices, along_z(): lax.all_to_all(a, 'dev', split_axis=0, concat_axis=0, axis_index_groups=r...  25 us
    ppermute x4, starting transfers between devices, to_left(): return lax.ppermute(a, 'dev', LEFT)  13.4 us
    ppermute x3, starting transfers between devices, to_far(): return lax.ppermute(a, 'dev', FAR)  12.9 us
    ppermute x3, starting transfers between devices, to_right(): return lax.ppermute(a, 'dev', RIGHT)  9.53 us
    pallas_call x3, Pallas kernels, experts(): pl.pallas_call(experts_kernel, in_specs=[pl.BlockSpec(memory_space=pltpu....  9.41 us
    ppermute x4, waiting for transfers between devices, to_left(): return lax.ppermute(a, 'dev', LEFT)  8.75 us
    all_to_all x4, waiting for transfers between devices, along_z(): lax.all_to_all(a, 'dev', split_axis=0, concat_axis=0, axis_index_groups=r...  8.17 us
    pallas_call x1, Pallas kernels, attend(): pl.pallas_call(attend_kernel, in_specs=[pl.BlockSpec(memory_space=pltpu.S...  3.18 us
  transfers between devices with their start and end apart: 14, of which 8 were waited for; matrix products, arithmetic and copies ran while one was open for 0% of the time, Pallas kernels for 15%

profile of v4, /device:TPU:104, one launch (start us, length us, event | category | flops | bytes accessed | tf_op | source)
XLA Modules:
  0.0 102.0 jit_solution(1721073723392829214)
XLA Ops:
  0.6 2.0 %pack_rows.1 = bf16[8,16,2048]{2,1,0:T(8,128)(2,1)} custom-call(bf16[32,2048]{1,0:T(8,128)(2,1)} %queries_ref.3, s32[2,32]{1,0:T(2,128)} %bitcast.10, f32[1,2048]{1,0:T(1,128)} %bitcast.15), custom_call_target="tpu_custom_call" | custom-call | flops 4000000 | bytes 700000 | tf_op jit(solution)/shard_map/pack_rows/pallas_call | solution.py:76
  2.6 10.0 %all-to-all-start = ((bf16[8,16,2048]{2,1,0:T(8,128)(2,1)}), bf16[8,16,2048]{2,1,0:T(8,128)(2,1)S(1)}, u32[]{:S(2)}, u32[]{:S(2)}) async-start(bf16[8,16,2048]{2,1,0:T(8,128)(2,1)} %pack_rows.1), calls=%async_computation | async-start | bytes 1048576 | tf_op jit(solution)/shard_map/all_to_all | solution.py:40
  13.8 3.4 %collective-permute-start.7 = (bf16[96,1024]{1,0:T(8,128)(2,1)S(1)}, bf16[96,1024]{1,0:T(8,128)(2,1)S(1)}, u32[]{:S(2)}, u32[]{:S(2)}) collective-permute-start(bf16[96,1024]{1,0:T(8,128)(2,1)S(1)} %get-tuple-element.21), channel_id=1, source_target_pairs={{0,1},{1,2},{2,3},{3,0},{4,5},{5,6},{6,7},{7,4},{8,9},{9,10},{10,1... | collective-permute-start | bytes 589832 | tf_op jit(solution)/shard_map/ppermute | solution.py:27
  17.2 4.6 %collective-permute-start = (bf16[64,1024]{1,0:T(8,128)(2,1)S(1)}, bf16[64,1024]{1,0:T(8,128)(2,1)S(1)}, u32[]{:S(2)}, u32[]{:S(2)}) collective-permute-start(bf16[64,1024]{1,0:T(8,128)(2,1)S(1)} %get-tuple-element.13), channel_id=1, source_target_pairs={{0,2},{1,3},{2,0},{3,1},{4,6},{5,7},{6,4},{7,5},{8,10},{9,11},{10,... | collective-permute-start | bytes 393224 | tf_op jit(solution)/shard_map/ppermute | solution.py:35
  21.8 3.3 %collective-permute-start.8 = (bf16[64,1024]{1,0:T(8,128)(2,1)S(1)}, bf16[64,1024]{1,0:T(8,128)(2,1)S(1)}, u32[]{:S(2)}, u32[]{:S(2)}) collective-permute-start(bf16[64,1024]{1,0:T(8,128)(2,1)S(1)} %get-tuple-element.22), channel_id=1, source_target_pairs={{0,3},{1,0},{2,1},{3,2},{4,7},{5,4},{6,5},{7,6},{8,11},{9,8},{10,9... | collective-permute-start | bytes 393224 | tf_op jit(solution)/shard_map/ppermute | solution.py:31
  27.9 4.9 %collective-permute-start.3 = (bf16[128,2048]{1,0:T(8,128)(2,1)S(1)}, bf16[128,2048]{1,0:T(8,128)(2,1)S(1)}, u32[]{:S(2)}, u32[]{:S(2)}) collective-permute-start(bf16[128,2048]{1,0:T(8,128)(2,1)S(1)} %bitcast.6), channel_id=1, source_target_pairs={{0,2},{1,3},{2,0},{3,1},{4,6},{5,7},{6,4},{7,5},{8,10},{9,11},{10,... | collective-permute-start | bytes 1572872 | tf_op jit(solution)/shard_map/ppermute | solution.py:35
  32.9 3.0 %collective-permute-start.2 = (bf16[128,2048]{1,0:T(8,128)(2,1)S(1)}, bf16[128,2048]{1,0:T(8,128)(2,1)S(1)}, u32[]{:S(2)}, u32[]{:S(2)}) collective-permute-start(bf16[128,2048]{1,0:T(8,128)(2,1)S(1)} %bitcast.7), channel_id=1, source_target_pairs={{0,3},{1,0},{2,1},{3,2},{4,7},{5,4},{6,5},{7,6},{8,11},{9,8},{10,9... | collective-permute-start | bytes 1572872 | tf_op jit(solution)/shard_map/ppermute | solution.py:31
  35.9 2.8 %collective-permute-start.1 = (bf16[128,2048]{1,0:T(8,128)(2,1)S(1)}, bf16[128,2048]{1,0:T(8,128)(2,1)S(1)}, u32[]{:S(2)}, u32[]{:S(2)}) collective-permute-start(bf16[128,2048]{1,0:T(8,128)(2,1)S(1)} %bitcast.8), channel_id=1, source_target_pairs={{0,1},{1,2},{2,3},{3,0},{4,5},{5,6},{6,7},{7,4},{8,9},{9,10},{10,1... | collective-permute-start | bytes 1572872 | tf_op jit(solution)/shard_map/ppermute | solution.py:27
  39.7 5.4 %all-to-all-start.2 = ((bf16[8,320,128]{2,1,0:T(8,128)(2,1)}), bf16[8,320,128]{2,1,0:T(8,128)(2,1)}, u32[]{:S(2)}, u32[]{:S(2)}) async-start(bf16[8,320,128]{2,1,0:T(8,128)(2,1)} %pack_heads.1), calls=%async_computation.2 | async-start | bytes 1310720 | tf_op jit(solution)/shard_map/all_to_all | solution.py:40
  45.1 2.7 %experts.3.own_ref = bf16[128,2048]{1,0:T(8,128)(2,1)S(1)} custom-call(bf16[128,2048]{1,0:T(8,128)(2,1)S(1)} %bitcast.9, bf16[2048,512]{1,0:T(8,128)(2,1)} %refs_2_.5, bf16[512,2048]{1,0:T(8,128)(2,1)} %refs_3_.1), custom_call_target="tpu_custom_call" | custom-call | flops 53687091200 | bytes 5242880 | tf_op jit(solution)/shard_map/experts/pallas_call | solution.py:323
  47.8 2.7 %experts.4 = bf16[128,2048]{1,0:T(8,128)(2,1)S(1)} custom-call(bf16[128,2048]{1,0:T(8,128)(2,1)S(1)} %collective-permute-done.3.refs_0_, bf16[2048,512]{1,0:T(8,128)(2,1)} %refs_2_.5, bf16[512,2048]{1,0:T(8,128)(2,1)} %refs_3_.1), custom_call_target="tpu_custom_call" | custom-call | flops 53687091200 | bytes 5242880 | tf_op jit(solution)/shard_map/experts/pallas_call | solution.py:323
  50.5 3.4 %collective-permute-start.6 = (bf16[128,2048]{1,0:T(8,128)(2,1)S(1)}, bf16[128,2048]{1,0:T(8,128)(2,1)S(1)}, u32[]{:S(2)}, u32[]{:S(2)}) collective-permute-start(bf16[128,2048]{1,0:T(8,128)(2,1)S(1)} %experts.4), channel_id=1, source_target_pairs={{0,2},{1,3},{2,0},{3,1},{4,6},{5,7},{6,4},{7,5},{8,10},{9,11},{10,... | collective-permute-start | bytes 1572872 | tf_op jit(solution)/shard_map/ppermute | solution.py:35
  53.8 3.6 %collective-permute-done.2.refs_1_ = bf16[128,2048]{1,0:T(8,128)(2,1)S(1)} collective-permute-done((bf16[128,2048]{1,0:T(8,128)(2,1)S(1)}, bf16[128,2048]{1,0:T(8,128)(2,1)S(1)}, u32[]{:S(2)}, u32[]{:S(2)}) %collective-permute-start.2) | collective-permute-done | bytes 524320 | tf_op jit(solution)/shard_map/ppermute | solution.py:31
  57.5 4.1 %experts.5 = (bf16[128,2048]{1,0:T(8,128)(2,1)}, bf16[128,2048]{1,0:T(8,128)(2,1)}) custom-call(bf16[128,2048]{1,0:T(8,128)(2,1)S(1)} %collective-permute-done.1.refs_0_, bf16[128,2048]{1,0:T(8,128)(2,1)S(1)} %collective-permute-done.2.refs_1_, bf16[2048,512]{1,0:T(8,128)(2,1)} %refs_2_.5, bf16[512,2048]{1,0:T(8,128)(2,1)} %refs_3_.1), custom_call_target="tpu_custom_call" | custom-call | flops 107374182400 | bytes 6291456 | tf_op jit(solution)/shard_map/experts/pallas_call | solution.py:323
  61.6 3.3 %collective-permute-start.4 = (bf16[128,2048]{1,0:T(8,128)(2,1)}, bf16[128,2048]{1,0:T(8,128)(2,1)S(1)}, u32[]{:S(2)}, u32[]{:S(2)}) collective-permute-start(bf16[128,2048]{1,0:T(8,128)(2,1)} %get-tuple-element.18), channel_id=1, source_target_pairs={{0,1},{1,2},{2,3},{3,0},{4,5},{5,6},{6,7},{7,4},{8,9},{9,10},{10,1... | collective-permute-start | bytes 1572872 | tf_op jit(solution)/shard_map/ppermute | solution.py:27
  64.9 3.7 %collective-permute-start.5 = (bf16[128,2048]{1,0:T(8,128)(2,1)}, bf16[128,2048]{1,0:T(8,128)(2,1)S(1)}, u32[]{:S(2)}, u32[]{:S(2)}) collective-permute-start(bf16[128,2048]{1,0:T(8,128)(2,1)} %get-tuple-element.19), channel_id=1, source_target_pairs={{0,3},{1,0},{2,1},{3,2},{4,7},{5,4},{6,5},{7,6},{8,11},{9,8},{10,9... | collective-permute-start | bytes 1572872 | tf_op jit(solution)/shard_map/ppermute | solution.py:31
  68.7 3.2 %attend.1 = bf16[8,64,128]{2,1,0:T(8,128)(2,1)} custom-call(s32[32]{0:T(128)S(1)} %copy-done.2, bf16[8,320,128]{2,1,0:T(8,128)(2,1)} %all-to-all-done.2.got_ref, s32[4,32]{1,0:T(4,128)} %counts_ref.1), custom_call_target="tpu_custom_call" | custom-call | flops 300000000 | bytes 1000000 | tf_op jit(solution)/shard_map/attend/pallas_call | solution.py:269
  71.9 4.2 %all-to-all-start.3 = ((bf16[8,64,128]{2,1,0:T(8,128)(2,1)}), bf16[8,64,128]{2,1,0:T(8,128)(2,1)S(1)}, u32[]{:S(2)}, u32[]{:S(2)}) async-start(bf16[8,64,128]{2,1,0:T(8,128)(2,1)} %attend.1), calls=%async_computation.3 | async-start | bytes 262144 | tf_op jit(solution)/shard_map/all_to_all | solution.py:40
  76.1 2.9 %collective-permute-done.4.left_ref = bf16[128,2048]{1,0:T(8,128)(2,1)S(1)} collective-permute-done((bf16[128,2048]{1,0:T(8,128)(2,1)}, bf16[128,2048]{1,0:T(8,128)(2,1)S(1)}, u32[]{:S(2)}, u32[]{:S(2)}) %collective-permute-start.4) | collective-permute-done | bytes 524320 | tf_op jit(solution)/shard_map/ppermute | solution.py:27
  81.6 2.1 %all-to-all-done.3.mixed_ref = bf16[8,64,128]{2,1,0:T(8,128)(2,1)S(1)} async-done(((bf16[8,64,128]{2,1,0:T(8,128)(2,1)}), bf16[8,64,128]{2,1,0:T(8,128)(2,1)S(1)}, u32[]{:S(2)}, u32[]{:S(2)}) %all-to-all-start.3) | async-done | bytes 131104 | tf_op jit(solution)/shard_map/all_to_all | solution.py:40
  83.7 5.4 %all-to-all-start.1 = ((bf16[8,16,2048]{2,1,0:T(8,128)(2,1)}), bf16[8,16,2048]{2,1,0:T(8,128)(2,1)S(1)}, u32[]{:S(2)}, u32[]{:S(2)}) async-start(bf16[8,16,2048]{2,1,0:T(8,128)(2,1)} %finish.1), calls=%async_computation.1 | async-start | bytes 1048576 | tf_op jit(solution)/shard_map/all_to_all | solution.py:40
  89.1 3.3 %collective-permute-start.9 = (bf16[8,64,128]{2,1,0:T(8,128)(2,1)S(1)}, bf16[8,64,128]{2,1,0:T(8,128)(2,1)S(1)}, u32[]{:S(2)}, u32[]{:S(2)}) collective-permute-start(bf16[8,64,128]{2,1,0:T(8,128)(2,1)S(1)} %all-to-all-done.3.mixed_ref), channel_id=1, source_target_pairs={{0,3},{1,0},{2,1},{3,2},{4,7},{5,4},{6,5},{7,6},{8,11},{9,8},{10,9... | collective-permute-start | bytes 393224 | tf_op jit(solution)/shard_map/ppermute | solution.py:31
  92.4 3.5 %collective-permute-done.9.other_ref = bf16[8,64,128]{2,1,0:T(8,128)(2,1)S(1)} collective-permute-done((bf16[8,64,128]{2,1,0:T(8,128)(2,1)S(1)}, bf16[8,64,128]{2,1,0:T(8,128)(2,1)S(1)}, u32[]{:S(2)}, u32[]{:S(2)}) %collective-permute-start.9) | collective-permute-done | bytes 131104 | tf_op jit(solution)/shard_map/ppermute | solution.py:31
  95.9 4.9 %all-to-all-done.1.ret_ref = bf16[8,16,2048]{2,1,0:T(8,128)(2,1)S(1)} async-done(((bf16[8,16,2048]{2,1,0:T(8,128)(2,1)}), bf16[8,16,2048]{2,1,0:T(8,128)(2,1)S(1)}, u32[]{:S(2)}, u32[]{:S(2)}) %all-to-all-start.1) | async-done | bytes 524320 | tf_op jit(solution)/shard_map/all_to_all | solution.py:40
  (19 shorter events, 8.7 us)
Async XLA Ops:
  2.6 25.3 %all-to-all-start = ((bf16[8,16,2048]{2,1,0:T(8,128)(2,1)}), bf16[8,16,2048]{2,1,0:T(8,128)(2,1)S(1)}, u32[]{:S(2)}, u32[]{:S(2)}) async-start(bf16[8,16,2048]{2,1,0:T(8,128)(2,1)} %pack_rows.1), calls=%async_computation | async-start | bytes 1048576 | tf_op jit(solution)/shard_map/all_to_all | solution.py:40
  13.8 25.0 %collective-permute-start.7 = (bf16[96,1024]{1,0:T(8,128)(2,1)S(1)}, bf16[96,1024]{1,0:T(8,128)(2,1)S(1)}, u32[]{:S(2)}, u32[]{:S(2)}) collective-permute-start(bf16[96,1024]{1,0:T(8,128)(2,1)S(1)} %get-tuple-element.21), channel_id=1, source_target_pairs={{0,1},{1,2},{2,3},{3,0},{4,5},{5,6},{6,7},{7,4},{8,9},{9,10},{10,1... | collective-permute-start | bytes 589832 | tf_op jit(solution)/shard_map/ppermute | solution.py:27
  17.2 9.6 %collective-permute-start = (bf16[64,1024]{1,0:T(8,128)(2,1)S(1)}, bf16[64,1024]{1,0:T(8,128)(2,1)S(1)}, u32[]{:S(2)}, u32[]{:S(2)}) collective-permute-start(bf16[64,1024]{1,0:T(8,128)(2,1)S(1)} %get-tuple-element.13), channel_id=1, source_target_pairs={{0,2},{1,3},{2,0},{3,1},{4,6},{5,7},{6,4},{7,5},{8,10},{9,11},{10,... | collective-permute-start | bytes 393224 | tf_op jit(solution)/shard_map/ppermute | solution.py:35
  21.8 16.9 %collective-permute-start.8 = (bf16[64,1024]{1,0:T(8,128)(2,1)S(1)}, bf16[64,1024]{1,0:T(8,128)(2,1)S(1)}, u32[]{:S(2)}, u32[]{:S(2)}) collective-permute-start(bf16[64,1024]{1,0:T(8,128)(2,1)S(1)} %get-tuple-element.22), channel_id=1, source_target_pairs={{0,3},{1,0},{2,1},{3,2},{4,7},{5,4},{6,5},{7,6},{8,11},{9,8},{10,9... | collective-permute-start | bytes 393224 | tf_op jit(solution)/shard_map/ppermute | solution.py:31
  27.9 19.8 %collective-permute-start.3 = (bf16[128,2048]{1,0:T(8,128)(2,1)S(1)}, bf16[128,2048]{1,0:T(8,128)(2,1)S(1)}, u32[]{:S(2)}, u32[]{:S(2)}) collective-permute-start(bf16[128,2048]{1,0:T(8,128)(2,1)S(1)} %bitcast.6), channel_id=1, source_target_pairs={{0,2},{1,3},{2,0},{3,1},{4,6},{5,7},{6,4},{7,5},{8,10},{9,11},{10,... | collective-permute-start | bytes 1572872 | tf_op jit(solution)/shard_map/ppermute | solution.py:35
  32.9 24.6 %collective-permute-start.2 = (bf16[128,2048]{1,0:T(8,128)(2,1)S(1)}, bf16[128,2048]{1,0:T(8,128)(2,1)S(1)}, u32[]{:S(2)}, u32[]{:S(2)}) collective-permute-start(bf16[128,2048]{1,0:T(8,128)(2,1)S(1)} %bitcast.7), channel_id=1, source_target_pairs={{0,3},{1,0},{2,1},{3,2},{4,7},{5,4},{6,5},{7,6},{8,11},{9,8},{10,9... | collective-permute-start | bytes 1572872 | tf_op jit(solution)/shard_map/ppermute | solution.py:31
  35.9 21.6 %collective-permute-start.1 = (bf16[128,2048]{1,0:T(8,128)(2,1)S(1)}, bf16[128,2048]{1,0:T(8,128)(2,1)S(1)}, u32[]{:S(2)}, u32[]{:S(2)}) collective-permute-start(bf16[128,2048]{1,0:T(8,128)(2,1)S(1)} %bitcast.8), channel_id=1, source_target_pairs={{0,1},{1,2},{2,3},{3,0},{4,5},{5,6},{6,7},{7,4},{8,9},{9,10},{10,1... | collective-permute-start | bytes 1572872 | tf_op jit(solution)/shard_map/ppermute | solution.py:27
  39.7 28.9 %all-to-all-start.2 = ((bf16[8,320,128]{2,1,0:T(8,128)(2,1)}), bf16[8,320,128]{2,1,0:T(8,128)(2,1)}, u32[]{:S(2)}, u32[]{:S(2)}) async-start(bf16[8,320,128]{2,1,0:T(8,128)(2,1)} %pack_heads.1), calls=%async_computation.2 | async-start | bytes 1310720 | tf_op jit(solution)/shard_map/all_to_all | solution.py:40
  50.5 18.2 %copy-start.2 = (s32[32]{0:T(128)S(1)}, s32[32]{0:T(128)}, u32[]{:S(2)}) copy-start(s32[32]{0:T(128)} %owner_ref.1) | copy-start | bytes 388
  50.5 25.6 %collective-permute-start.6 = (bf16[128,2048]{1,0:T(8,128)(2,1)S(1)}, bf16[128,2048]{1,0:T(8,128)(2,1)S(1)}, u32[]{:S(2)}, u32[]{:S(2)}) collective-permute-start(bf16[128,2048]{1,0:T(8,128)(2,1)S(1)} %experts.4), channel_id=1, source_target_pairs={{0,2},{1,3},{2,0},{3,1},{4,6},{5,7},{6,4},{7,5},{8,10},{9,11},{10,... | collective-permute-start | bytes 1572872 | tf_op jit(solution)/shard_map/ppermute | solution.py:35
  61.6 17.3 %collective-permute-start.4 = (bf16[128,2048]{1,0:T(8,128)(2,1)}, bf16[128,2048]{1,0:T(8,128)(2,1)S(1)}, u32[]{:S(2)}, u32[]{:S(2)}) collective-permute-start(bf16[128,2048]{1,0:T(8,128)(2,1)} %get-tuple-element.18), channel_id=1, source_target_pairs={{0,1},{1,2},{2,3},{3,0},{4,5},{5,6},{6,7},{7,4},{8,9},{9,10},{10,1... | collective-permute-start | bytes 1572872 | tf_op jit(solution)/shard_map/ppermute | solution.py:27
  64.9 15.6 %collective-permute-start.5 = (bf16[128,2048]{1,0:T(8,128)(2,1)}, bf16[128,2048]{1,0:T(8,128)(2,1)S(1)}, u32[]{:S(2)}, u32[]{:S(2)}) collective-permute-start(bf16[128,2048]{1,0:T(8,128)(2,1)} %get-tuple-element.19), channel_id=1, source_target_pairs={{0,3},{1,0},{2,1},{3,2},{4,7},{5,4},{6,5},{7,6},{8,11},{9,8},{10,9... | collective-permute-start | bytes 1572872 | tf_op jit(solution)/shard_map/ppermute | solution.py:31
  71.9 29.0 %copy-start = (s32[32,2]{0,1:T(2,128)S(1)}, s32[32,2]{0,1:T(2,128)}, u32[]{:S(2)}) copy-start(s32[32,2]{0,1:T(2,128)} %param.15) | copy-start | bytes 772
  71.9 29.0 %copy-start.1 = (f32[32,2]{0,1:T(2,128)S(1)}, f32[32,2]{0,1:T(2,128)}, u32[]{:S(2)}) copy-start(f32[32,2]{0,1:T(2,128)} %param.16) | copy-start | bytes 772
  71.9 11.8 %all-to-all-start.3 = ((bf16[8,64,128]{2,1,0:T(8,128)(2,1)}), bf16[8,64,128]{2,1,0:T(8,128)(2,1)S(1)}, u32[]{:S(2)}, u32[]{:S(2)}) async-start(bf16[8,64,128]{2,1,0:T(8,128)(2,1)} %attend.1), calls=%async_computation.3 | async-start | bytes 262144 | tf_op jit(solution)/shard_map/all_to_all | solution.py:40
  83.7 17.1 %all-to-all-start.1 = ((bf16[8,16,2048]{2,1,0:T(8,128)(2,1)}), bf16[8,16,2048]{2,1,0:T(8,128)(2,1)S(1)}, u32[]{:S(2)}, u32[]{:S(2)}) async-start(bf16[8,16,2048]{2,1,0:T(8,128)(2,1)} %finish.1), calls=%async_computation.1 | async-start | bytes 1048576 | tf_op jit(solution)/shard_map/all_to_all | solution.py:40
  89.1 6.8 %collective-permute-start.9 = (bf16[8,64,128]{2,1,0:T(8,128)(2,1)S(1)}, bf16[8,64,128]{2,1,0:T(8,128)(2,1)S(1)}, u32[]{:S(2)}, u32[]{:S(2)}) collective-permute-start(bf16[8,64,128]{2,1,0:T(8,128)(2,1)S(1)} %all-to-all-done.3.mixed_ref), channel_id=1, source_target_pairs={{0,3},{1,0},{2,1},{3,2},{4,7},{5,4},{6,5},{7,6},{8,11},{9,8},{10,9... | collective-permute-start | bytes 393224 | tf_op jit(solution)/shard_map/ppermute | solution.py:31

commit v5 on v4

--- a/solution.py
+++ b/solution.py
@@ -84,24 +84,39 @@
     )(*in_hbm(queries, routes, gain.reshape(1, width)))
 
 
-def finish_kernel(own_ref, left_ref, right_ref, far_ref, out_ref):
+def gather_kernel(own_ref, far_ref, out_ref):
+    out_ref[...] = own_ref[...].astype(F32) + far_ref[...].astype(F32)
+
+
+def own_and_far(own, far):
+    return pl.pallas_call(
+        gather_kernel,
+        out_shape=jax.ShapeDtypeStruct(own.shape, F32),
+        cost_estimate=pl.CostEstimate(
+            flops=20_000_000_000, bytes_accessed=2_000_000, transcendentals=0
+        ),
+        compiler_params=pltpu.CompilerParams(vmem_limit_bytes=8 * 2**20),
+        name="own_and_far",
+    )(own, far)
+
+
+def finish_kernel(sum_ref, left_ref, right_ref, out_ref):
     for z in range(NZ):
         rows = slice(FIRST.index(z) * CAP, (FIRST.index(z) + 1) * CAP)
-        total = own_ref[rows].astype(F32) + left_ref[rows].astype(F32)
-        total = total + right_ref[rows].astype(F32) + far_ref[rows].astype(F32)
+        total = sum_ref[rows] + left_ref[rows].astype(F32) + right_ref[rows].astype(F32)
         out_ref[LAST.index(z)] = total.astype(BF)
 
 
-def finish(own, left, right, far):
+def finish(partial, left, right):
     return pl.pallas_call(
         finish_kernel,
-        out_shape=jax.ShapeDtypeStruct((NZ, CAP, own.shape[1]), BF),
+        out_shape=jax.ShapeDtypeStruct((NZ, CAP, partial.shape[1]), BF),
         cost_estimate=pl.CostEstimate(
             flops=1_000_000, bytes_accessed=2_600_000, transcendentals=0
         ),
         compiler_params=pltpu.CompilerParams(vmem_limit_bytes=8 * 2**20),
         name="finish",
-    )(own, left, right, far)
+    )(partial, left, right)
 
 
 def combine_kernel(
@@ -282,38 +297,40 @@
     )(owner, got, *in_hbm(counts))
 
 
+def preload_kernel(up_ref, down_ref, up_out, down_out, sems):
+    copies = [
+        pltpu.make_async_copy(source, target, sems.at[at])
+        for at, (source, target) in enumerate(((up_ref, up_out), (down_ref, down_out)))
+    ]
+    for copy in copies:
+        copy.start()
+    for copy in copies:
+        copy.wait()
+
+
+def preload(up, down):
+    return pl.pallas_call(
+        preload_kernel,
+        in_specs=[pl.BlockSpec(memory_space=pl.ANY)] * 2,
+        out_specs=[pl.BlockSpec(memory_space=pltpu.VMEM)] * 2,
+        out_shape=[jax.ShapeDtypeStruct(a.shape, a.dtype) for a in (up, down)],
+        scratch_shapes=[pltpu.SemaphoreType.DMA((2,))],
+        cost_estimate=pl.CostEstimate(flops=0, bytes_accessed=8 * 2**20, transcendentals=0),
+        compiler_params=pltpu.CompilerParams(vmem_limit_bytes=6 * 2**20),
+        name="preload",
+    )(*in_hbm(up, down))
+
+
 def experts_kernel(*refs):
-    *ins, up_ref, down_ref = refs[: len(refs) // 2]
-    *outs, up, down, sems = refs[len(refs) // 2 :]
-    parts = 2
-    copies = []
-    for which, (source, target) in enumerate(((up_ref, up), (down_ref, down))):
-        size = target.shape[0] // parts
-        for part in range(parts):
-            own = slice(part * size, (part + 1) * size)
-            copies.append(
-                pltpu.make_async_copy(source.at[own], target.at[own], sems.at[which, part])
-            )
-    ahead = 4
-    for copy in copies[:ahead]:
-        copy.start()
-    value = jnp.concatenate([ref[...] for ref in ins], axis=0)
-    for which, weight in enumerate((up, down)):
-        size = weight.shape[0] // parts
-        total = None
-        for part in range(parts):
-            own = slice(part * size, (part + 1) * size)
-            index = which * parts + part
-            copies[index].wait()
-            if index + ahead < len(copies):
-                copies[index + ahead].start()
-            term = jnp.dot(value[:, own], weight[own, :], preferred_element_type=F32)
-            total = term if total is None else total + term
-        if which == 0:
-            value = (total / (1.0 + jnp.exp(-total))).astype(BF)
+    *ins, up_ref, down_ref = refs[: len(refs) // 2 + 1]
+    outs = refs[len(refs) // 2 + 1 :]
+    rows = jnp.concatenate([ref[...] for ref in ins], axis=0)
+    hidden = jnp.dot(rows, up_ref[...], preferred_element_type=F32)
+    hidden = (hidden / (1.0 + jnp.exp(-hidden))).astype(BF)
+    total = jnp.dot(hidden, down_ref[...], preferred_element_type=F32).astype(BF)
     size = ins[0].shape[0]
     for index, out_ref in enumerate(outs):
-        out_ref[...] = total[index * size : (index + 1) * size].astype(BF)
+        out_ref[...] = total[index * size : (index + 1) * size]
 
 
 def experts(blocks, up, down):
@@ -322,22 +339,16 @@
     width, hidden = up.shape
     return pl.pallas_call(
         experts_kernel,
-        in_specs=[pl.BlockSpec(memory_space=pltpu.VMEM)] * count
-        + [pl.BlockSpec(memory_space=pl.ANY)] * 2,
+        in_specs=[pl.BlockSpec(memory_space=pltpu.VMEM)] * (count + 2),
         out_shape=[jax.ShapeDtypeStruct(block.shape, BF) for block in blocks],
-        scratch_shapes=[
-            pltpu.VMEM(up.shape, up.dtype),
-            pltpu.VMEM(down.shape, down.dtype),
-            pltpu.SemaphoreType.DMA((2, 2)),
-        ],
         cost_estimate=pl.CostEstimate(
             flops=400 * size * width * hidden,
             bytes_accessed=4 * width * hidden + 4 * size * width,
             transcendentals=size * hidden,
         ),
-        compiler_params=pltpu.CompilerParams(vmem_limit_bytes=14 * 2**20),
+        compiler_params=pltpu.CompilerParams(vmem_limit_bytes=10 * 2**20),
         name="experts",
-    )(*blocks, *in_hbm(up, down))
+    )(*blocks, up, down)
 
 
 def on_device(
@@ -358,6 +369,8 @@
     block = along_z(packed, FIRST).reshape(size, width)
     block, far = lax.optimization_barrier((block, far))
     block_f, block_l, block_r = to_far(block), to_right(block), to_left(block)
+    w_up, w_down, _ = lax.optimization_barrier((w_up, w_down, block))
+    w_up, w_down = preload(w_up, w_down)
     (part,) = experts([block], w_up, w_down)
 
     got = along_z(pack_heads(mine, left, right, far))
@@ -369,7 +382,7 @@
     block_l, block_r, part, _ = lax.optimization_barrier((block_l, block_r, part, part_f))
     part_l, part_r = experts([block_l, block_r], w_up, w_down)
     from_r, from_l = to_left(part_l), to_right(part_r)
-    ret = along_z(finish(part, from_l, from_r, from_f), LAST)
+    ret = along_z(finish(own_and_far(part, from_f), from_l, from_r), LAST)
     context, routed = combine(ret, mixed, other, routes, route_gate, beams, width)
     return (context, routed)
 

time: 103 us -> 101 us (0.981)
  the two profiles are of different devices: /device:TPU:104 before, /device:TPU:120 now
where the time goes in v5:
time: 101 us; the launch traced here: 100 us
  starting transfers between devices  60.7 us (60%)
  waiting for transfers between devices  22 us (22%)
  Pallas kernels  15.8 us (16%)
  local copies, waits for them, and re-layouts  1.06 us (1%)
    all_to_all x4, starting transfers between devices, along_z(): lax.all_to_all(a, 'dev', split_axis=0, concat_axis=0, axis_index_groups=r...  24.9 us
    ppermute x4, starting transfers between devices, to_left(): return lax.ppermute(a, 'dev', LEFT)  13.4 us
    ppermute x3, starting transfers between devices, to_far(): return lax.ppermute(a, 'dev', FAR)  12.9 us
    ppermute x3, starting transfers between devices, to_right(): return lax.ppermute(a, 'dev', RIGHT)  9.52 us
    ppermute x4, waiting for transfers between devices, to_left(): return lax.ppermute(a, 'dev', LEFT)  8.56 us
    all_to_all x4, waiting for transfers between devices, along_z(): lax.all_to_all(a, 'dev', split_axis=0, concat_axis=0, axis_index_groups=r...  8.19 us
    pallas_call x3, Pallas kernels, experts(): pl.pallas_call(experts_kernel, in_specs=[pl.BlockSpec(memory_space=pltpu....  4 us
    ppermute x3, waiting for transfers between devices, to_right(): return lax.ppermute(a, 'dev', RIGHT)  3.65 us
  transfers between devices with their start and end apart: 14, of which 8 were waited for; matrix products, arithmetic and copies ran while one was open for 0% of the time, Pallas kernels for 13%

profile of v5, /device:TPU:120, one launch (start us, length us, event | category | flops | bytes accessed | tf_op | source)
XLA Modules:
  0.0 100.4 jit_solution(10868202586455919095)
XLA Ops:
  0.6 2.0 %pack_rows.1 = bf16[8,16,2048]{2,1,0:T(8,128)(2,1)} custom-call(bf16[32,2048]{1,0:T(8,128)(2,1)} %queries_ref.3, s32[2,32]{1,0:T(2,128)} %bitcast.10, f32[1,2048]{1,0:T(1,128)} %bitcast.15), custom_call_target="tpu_custom_call" | custom-call | flops 4000000 | bytes 700000 | tf_op jit(solution)/shard_map/pack_rows/pallas_call | solution.py:76
  2.6 10.0 %all-to-all-start = ((bf16[8,16,2048]{2,1,0:T(8,128)(2,1)}), bf16[8,16,2048]{2,1,0:T(8,128)(2,1)S(1)}, u32[]{:S(2)}, u32[]{:S(2)}) async-start(bf16[8,16,2048]{2,1,0:T(8,128)(2,1)} %pack_rows.1), calls=%async_computation | async-start | bytes 1048576 | tf_op jit(solution)/shard_map/all_to_all | solution.py:40
  13.8 3.4 %collective-permute-start.7 = (bf16[96,1024]{1,0:T(8,128)(2,1)S(1)}, bf16[96,1024]{1,0:T(8,128)(2,1)S(1)}, u32[]{:S(2)}, u32[]{:S(2)}) collective-permute-start(bf16[96,1024]{1,0:T(8,128)(2,1)S(1)} %get-tuple-element.29), channel_id=1, source_target_pairs={{0,1},{1,2},{2,3},{3,0},{4,5},{5,6},{6,7},{7,4},{8,9},{9,10},{10,1... | collective-permute-start | bytes 589832 | tf_op jit(solution)/shard_map/ppermute | solution.py:27
  17.2 4.6 %collective-permute-start = (bf16[64,1024]{1,0:T(8,128)(2,1)S(1)}, bf16[64,1024]{1,0:T(8,128)(2,1)S(1)}, u32[]{:S(2)}, u32[]{:S(2)}) collective-permute-start(bf16[64,1024]{1,0:T(8,128)(2,1)S(1)} %get-tuple-element.17), channel_id=1, source_target_pairs={{0,2},{1,3},{2,0},{3,1},{4,6},{5,7},{6,4},{7,5},{8,10},{9,11},{10,... | collective-permute-start | bytes 393224 | tf_op jit(solution)/shard_map/ppermute | solution.py:35
  21.8 3.3 %collective-permute-start.8 = (bf16[64,1024]{1,0:T(8,128)(2,1)S(1)}, bf16[64,1024]{1,0:T(8,128)(2,1)S(1)}, u32[]{:S(2)}, u32[]{:S(2)}) collective-permute-start(bf16[64,1024]{1,0:T(8,128)(2,1)S(1)} %get-tuple-element.30), channel_id=1, source_target_pairs={{0,3},{1,0},{2,1},{3,2},{4,7},{5,4},{6,5},{7,6},{8,11},{9,8},{10,9... | collective-permute-start | bytes 393224 | tf_op jit(solution)/shard_map/ppermute | solution.py:31
  25.2 1.6 %collective-permute-done.far_ref = bf16[64,1024]{1,0:T(8,128)(2,1)S(1)} collective-permute-done((bf16[64,1024]{1,0:T(8,128)(2,1)S(1)}, bf16[64,1024]{1,0:T(8,128)(2,1)S(1)}, u32[]{:S(2)}, u32[]{:S(2)}) %collective-permute-start) | collective-permute-done | bytes 131104 | tf_op jit(solution)/shard_map/ppermute | solution.py:35
  27.9 4.9 %collective-permute-start.3 = (bf16[128,2048]{1,0:T(8,128)(2,1)S(1)}, bf16[128,2048]{1,0:T(8,128)(2,1)S(1)}, u32[]{:S(2)}, u32[]{:S(2)}) collective-permute-start(bf16[128,2048]{1,0:T(8,128)(2,1)S(1)} %bitcast.6), channel_id=1, source_target_pairs={{0,2},{1,3},{2,0},{3,1},{4,6},{5,7},{6,4},{7,5},{8,10},{9,11},{10,... | collective-permute-start | bytes 1572872 | tf_op jit(solution)/shard_map/ppermute | solution.py:35
  32.9 3.0 %collective-permute-start.2 = (bf16[128,2048]{1,0:T(8,128)(2,1)S(1)}, bf16[128,2048]{1,0:T(8,128)(2,1)S(1)}, u32[]{:S(2)}, u32[]{:S(2)}) collective-permute-start(bf16[128,2048]{1,0:T(8,128)(2,1)S(1)} %bitcast.7), channel_id=1, source_target_pairs={{0,3},{1,0},{2,1},{3,2},{4,7},{5,4},{6,5},{7,6},{8,11},{9,8},{10,9... | collective-permute-start | bytes 1572872 | tf_op jit(solution)/shard_map/ppermute | solution.py:31
  35.9 2.8 %collective-permute-start.1 = (bf16[128,2048]{1,0:T(8,128)(2,1)S(1)}, bf16[128,2048]{1,0:T(8,128)(2,1)S(1)}, u32[]{:S(2)}, u32[]{:S(2)}) collective-permute-start(bf16[128,2048]{1,0:T(8,128)(2,1)S(1)} %bitcast.8), channel_id=1, source_target_pairs={{0,1},{1,2},{2,3},{3,0},{4,5},{5,6},{6,7},{7,4},{8,9},{9,10},{10,1... | collective-permute-start | bytes 1572872 | tf_op jit(solution)/shard_map/ppermute | solution.py:27
  39.7 5.4 %all-to-all-start.2 = ((bf16[8,320,128]{2,1,0:T(8,128)(2,1)}), bf16[8,320,128]{2,1,0:T(8,128)(2,1)}, u32[]{:S(2)}, u32[]{:S(2)}) async-start(bf16[8,320,128]{2,1,0:T(8,128)(2,1)} %pack_heads.1), calls=%async_computation.2 | async-start | bytes 1310720 | tf_op jit(solution)/shard_map/all_to_all | solution.py:40
  45.1 2.2 %preload.1 = (bf16[2048,512]{1,0:T(8,128)(2,1)S(1)}, bf16[512,2048]{1,0:T(8,128)(2,1)S(1)}) custom-call(bf16[2048,512]{1,0:T(8,128)(2,1)} %up_ref, bf16[512,2048]{1,0:T(8,128)(2,1)} %down_ref), custom_call_target="tpu_custom_call" | custom-call | bytes 8388608 | tf_op jit(solution)/shard_map/preload/pallas_call | solution.py:312
  49.2 3.4 %collective-permute-start.4 = (bf16[128,2048]{1,0:T(8,128)(2,1)S(1)}, bf16[128,2048]{1,0:T(8,128)(2,1)S(1)}, u32[]{:S(2)}, u32[]{:S(2)}) collective-permute-start(bf16[128,2048]{1,0:T(8,128)(2,1)S(1)} %experts.4), channel_id=1, source_target_pairs={{0,2},{1,3},{2,0},{3,1},{4,6},{5,7},{6,4},{7,5},{8,10},{9,11},{10,... | collective-permute-start | bytes 1572872 | tf_op jit(solution)/shard_map/ppermute | solution.py:35
  52.6 4.9 %collective-permute-done.2.refs_1_ = bf16[128,2048]{1,0:T(8,128)(2,1)S(1)} collective-permute-done((bf16[128,2048]{1,0:T(8,128)(2,1)S(1)}, bf16[128,2048]{1,0:T(8,128)(2,1)S(1)}, u32[]{:S(2)}, u32[]{:S(2)}) %collective-permute-start.2) | collective-permute-done | bytes 524320 | tf_op jit(solution)/shard_map/ppermute | solution.py:31
  57.5 2.2 %experts.5 = (bf16[128,2048]{1,0:T(8,128)(2,1)S(1)}, bf16[128,2048]{1,0:T(8,128)(2,1)}) custom-call(bf16[128,2048]{1,0:T(8,128)(2,1)S(1)} %collective-permute-done.1.refs_0_, bf16[128,2048]{1,0:T(8,128)(2,1)S(1)} %collective-permute-done.2.refs_1_, bf16[2048,512]{1,0:T(8,128)(2,1)S(1)} %get-tuple-element.21.refs_1_.refs_2_, ...), custom_call_target="tpu_custom_call" | custom-call | flops 107374182400 | bytes 6291456 | tf_op jit(solution)/shard_map/experts/pallas_call | solution.py:340
  59.7 3.3 %collective-permute-start.5 = (bf16[128,2048]{1,0:T(8,128)(2,1)}, bf16[128,2048]{1,0:T(8,128)(2,1)S(1)}, u32[]{:S(2)}, u32[]{:S(2)}) collective-permute-start(bf16[128,2048]{1,0:T(8,128)(2,1)} %get-tuple-element.26), channel_id=1, source_target_pairs={{0,1},{1,2},{2,3},{3,0},{4,5},{5,6},{6,7},{7,4},{8,9},{9,10},{10,1... | collective-permute-start | bytes 1572872 | tf_op jit(solution)/shard_map/ppermute | solution.py:27
  63.0 3.7 %collective-permute-start.6 = (bf16[128,2048]{1,0:T(8,128)(2,1)S(1)}, bf16[128,2048]{1,0:T(8,128)(2,1)S(1)}, u32[]{:S(2)}, u32[]{:S(2)}) collective-permute-start(bf16[128,2048]{1,0:T(8,128)(2,1)S(1)} %get-tuple-element.27), channel_id=1, source_target_pairs={{0,3},{1,0},{2,1},{3,2},{4,7},{5,4},{6,5},{7,6},{8,11},{9,8},{10,9... | collective-permute-start | bytes 1572872 | tf_op jit(solution)/shard_map/ppermute | solution.py:31
  66.8 3.2 %attend.1 = bf16[8,64,128]{2,1,0:T(8,128)(2,1)} custom-call(s32[32]{0:T(128)S(1)} %copy-done.2, bf16[8,320,128]{2,1,0:T(8,128)(2,1)} %all-to-all-done.2.got_ref, s32[4,32]{1,0:T(4,128)} %counts_ref.1), custom_call_target="tpu_custom_call" | custom-call | flops 300000000 | bytes 1000000 | tf_op jit(solution)/shard_map/attend/pallas_call | solution.py:284
  69.9 4.2 %all-to-all-start.3 = ((bf16[8,64,128]{2,1,0:T(8,128)(2,1)}), bf16[8,64,128]{2,1,0:T(8,128)(2,1)S(1)}, u32[]{:S(2)}, u32[]{:S(2)}) async-start(bf16[8,64,128]{2,1,0:T(8,128)(2,1)} %attend.1), calls=%async_computation.3 | async-start | bytes 262144 | tf_op jit(solution)/shard_map/all_to_all | solution.py:40
  75.3 3.6 %collective-permute-done.5.left_ref = bf16[128,2048]{1,0:T(8,128)(2,1)S(1)} collective-permute-done((bf16[128,2048]{1,0:T(8,128)(2,1)}, bf16[128,2048]{1,0:T(8,128)(2,1)S(1)}, u32[]{:S(2)}, u32[]{:S(2)}) %collective-permute-start.5) | collective-permute-done | bytes 524320 | tf_op jit(solution)/shard_map/ppermute | solution.py:27
  80.0 1.8 %all-to-all-done.3.mixed_ref = bf16[8,64,128]{2,1,0:T(8,128)(2,1)S(1)} async-done(((bf16[8,64,128]{2,1,0:T(8,128)(2,1)}), bf16[8,64,128]{2,1,0:T(8,128)(2,1)S(1)}, u32[]{:S(2)}, u32[]{:S(2)}) %all-to-all-start.3) | async-done | bytes 131104 | tf_op jit(solution)/shard_map/all_to_all | solution.py:40
  81.7 5.4 %all-to-all-start.1 = ((bf16[8,16,2048]{2,1,0:T(8,128)(2,1)}), bf16[8,16,2048]{2,1,0:T(8,128)(2,1)S(1)}, u32[]{:S(2)}, u32[]{:S(2)}) async-start(bf16[8,16,2048]{2,1,0:T(8,128)(2,1)} %finish.1), calls=%async_computation.1 | async-start | bytes 1048576 | tf_op jit(solution)/shard_map/all_to_all | solution.py:40
  87.1 3.3 %collective-permute-start.9 = (bf16[8,64,128]{2,1,0:T(8,128)(2,1)S(1)}, bf16[8,64,128]{2,1,0:T(8,128)(2,1)S(1)}, u32[]{:S(2)}, u32[]{:S(2)}) collective-permute-start(bf16[8,64,128]{2,1,0:T(8,128)(2,1)S(1)} %all-to-all-done.3.mixed_ref), channel_id=1, source_target_pairs={{0,3},{1,0},{2,1},{3,2},{4,7},{5,4},{6,5},{7,6},{8,11},{9,8},{10,9... | collective-permute-start | bytes 393224 | tf_op jit(solution)/shard_map/ppermute | solution.py:31
  90.4 3.6 %collective-permute-done.9.other_ref = bf16[8,64,128]{2,1,0:T(8,128)(2,1)S(1)} collective-permute-done((bf16[8,64,128]{2,1,0:T(8,128)(2,1)S(1)}, bf16[8,64,128]{2,1,0:T(8,128)(2,1)S(1)}, u32[]{:S(2)}, u32[]{:S(2)}) %collective-permute-start.9) | collective-permute-done | bytes 131104 | tf_op jit(solution)/shard_map/ppermute | solution.py:31
  94.0 5.2 %all-to-all-done.1.ret_ref = bf16[8,16,2048]{2,1,0:T(8,128)(2,1)S(1)} async-done(((bf16[8,16,2048]{2,1,0:T(8,128)(2,1)}), bf16[8,16,2048]{2,1,0:T(8,128)(2,1)S(1)}, u32[]{:S(2)}, u32[]{:S(2)}) %all-to-all-start.1) | async-done | bytes 524320 | tf_op jit(solution)/shard_map/all_to_all | solution.py:40
  (25 shorter events, 8.5 us)
Async XLA Ops:
  2.6 25.3 %all-to-all-start = ((bf16[8,16,2048]{2,1,0:T(8,128)(2,1)}), bf16[8,16,2048]{2,1,0:T(8,128)(2,1)S(1)}, u32[]{:S(2)}, u32[]{:S(2)}) async-start(bf16[8,16,2048]{2,1,0:T(8,128)(2,1)} %pack_rows.1), calls=%async_computation | async-start | bytes 1048576 | tf_op jit(solution)/shard_map/all_to_all | solution.py:40
  13.8 25.0 %collective-permute-start.7 = (bf16[96,1024]{1,0:T(8,128)(2,1)S(1)}, bf16[96,1024]{1,0:T(8,128)(2,1)S(1)}, u32[]{:S(2)}, u32[]{:S(2)}) collective-permute-start(bf16[96,1024]{1,0:T(8,128)(2,1)S(1)} %get-tuple-element.29), channel_id=1, source_target_pairs={{0,1},{1,2},{2,3},{3,0},{4,5},{5,6},{6,7},{7,4},{8,9},{9,10},{10,1... | collective-permute-start | bytes 589832 | tf_op jit(solution)/shard_map/ppermute | solution.py:27
  17.2 9.6 %collective-permute-start = (bf16[64,1024]{1,0:T(8,128)(2,1)S(1)}, bf16[64,1024]{1,0:T(8,128)(2,1)S(1)}, u32[]{:S(2)}, u32[]{:S(2)}) collective-permute-start(bf16[64,1024]{1,0:T(8,128)(2,1)S(1)} %get-tuple-element.17), channel_id=1, source_target_pairs={{0,2},{1,3},{2,0},{3,1},{4,6},{5,7},{6,4},{7,5},{8,10},{9,11},{10,... | collective-permute-start | bytes 393224 | tf_op jit(solution)/shard_map/ppermute | solution.py:35
  21.8 16.9 %collective-permute-start.8 = (bf16[64,1024]{1,0:T(8,128)(2,1)S(1)}, bf16[64,1024]{1,0:T(8,128)(2,1)S(1)}, u32[]{:S(2)}, u32[]{:S(2)}) collective-permute-start(bf16[64,1024]{1,0:T(8,128)(2,1)S(1)} %get-tuple-element.30), channel_id=1, source_target_pairs={{0,3},{1,0},{2,1},{3,2},{4,7},{5,4},{6,5},{7,6},{8,11},{9,8},{10,9... | collective-permute-start | bytes 393224 | tf_op jit(solution)/shard_map/ppermute | solution.py:31
  27.9 20.3 %collective-permute-start.3 = (bf16[128,2048]{1,0:T(8,128)(2,1)S(1)}, bf16[128,2048]{1,0:T(8,128)(2,1)S(1)}, u32[]{:S(2)}, u32[]{:S(2)}) collective-permute-start(bf16[128,2048]{1,0:T(8,128)(2,1)S(1)} %bitcast.6), channel_id=1, source_target_pairs={{0,2},{1,3},{2,0},{3,1},{4,6},{5,7},{6,4},{7,5},{8,10},{9,11},{10,... | collective-permute-start | bytes 1572872 | tf_op jit(solution)/shard_map/ppermute | solution.py:35
  32.9 24.6 %collective-permute-start.2 = (bf16[128,2048]{1,0:T(8,128)(2,1)S(1)}, bf16[128,2048]{1,0:T(8,128)(2,1)S(1)}, u32[]{:S(2)}, u32[]{:S(2)}) collective-permute-start(bf16[128,2048]{1,0:T(8,128)(2,1)S(1)} %bitcast.7), channel_id=1, source_target_pairs={{0,3},{1,0},{2,1},{3,2},{4,7},{5,4},{6,5},{7,6},{8,11},{9,8},{10,9... | collective-permute-start | bytes 1572872 | tf_op jit(solution)/shard_map/ppermute | solution.py:31
  35.9 21.6 %collective-permute-start.1 = (bf16[128,2048]{1,0:T(8,128)(2,1)S(1)}, bf16[128,2048]{1,0:T(8,128)(2,1)S(1)}, u32[]{:S(2)}, u32[]{:S(2)}) collective-permute-start(bf16[128,2048]{1,0:T(8,128)(2,1)S(1)} %bitcast.8), channel_id=1, source_target_pairs={{0,1},{1,2},{2,3},{3,0},{4,5},{5,6},{6,7},{7,4},{8,9},{9,10},{10,1... | collective-permute-start | bytes 1572872 | tf_op jit(solution)/shard_map/ppermute | solution.py:27
  39.7 27.0 %all-to-all-start.2 = ((bf16[8,320,128]{2,1,0:T(8,128)(2,1)}), bf16[8,320,128]{2,1,0:T(8,128)(2,1)}, u32[]{:S(2)}, u32[]{:S(2)}) async-start(bf16[8,320,128]{2,1,0:T(8,128)(2,1)} %pack_heads.1), calls=%async_computation.2 | async-start | bytes 1310720 | tf_op jit(solution)/shard_map/all_to_all | solution.py:40
  48.3 0.9 copy-start.3
  49.2 17.6 %copy-start.2 = (s32[32]{0:T(128)S(1)}, s32[32]{0:T(128)}, u32[]{:S(2)}) copy-start(s32[32]{0:T(128)} %owner_ref.1) | copy-start | bytes 388
  49.2 24.9 %collective-permute-start.4 = (bf16[128,2048]{1,0:T(8,128)(2,1)S(1)}, bf16[128,2048]{1,0:T(8,128)(2,1)S(1)}, u32[]{:S(2)}, u32[]{:S(2)}) collective-permute-start(bf16[128,2048]{1,0:T(8,128)(2,1)S(1)} %experts.4), channel_id=1, source_target_pairs={{0,2},{1,3},{2,0},{3,1},{4,6},{5,7},{6,4},{7,5},{8,10},{9,11},{10,... | collective-permute-start | bytes 1572872 | tf_op jit(solution)/shard_map/ppermute | solution.py:35
  59.7 19.2 %collective-permute-start.5 = (bf16[128,2048]{1,0:T(8,128)(2,1)}, bf16[128,2048]{1,0:T(8,128)(2,1)S(1)}, u32[]{:S(2)}, u32[]{:S(2)}) collective-permute-start(bf16[128,2048]{1,0:T(8,128)(2,1)} %get-tuple-element.26), channel_id=1, source_target_pairs={{0,1},{1,2},{2,3},{3,0},{4,5},{5,6},{6,7},{7,4},{8,9},{9,10},{10,1... | collective-permute-start | bytes 1572872 | tf_op jit(solution)/shard_map/ppermute | solution.py:27
  63.0 16.0 %collective-permute-start.6 = (bf16[128,2048]{1,0:T(8,128)(2,1)S(1)}, bf16[128,2048]{1,0:T(8,128)(2,1)S(1)}, u32[]{:S(2)}, u32[]{:S(2)}) collective-permute-start(bf16[128,2048]{1,0:T(8,128)(2,1)S(1)} %get-tuple-element.27), channel_id=1, source_target_pairs={{0,3},{1,0},{2,1},{3,2},{4,7},{5,4},{6,5},{7,6},{8,11},{9,8},{10,9... | collective-permute-start | bytes 1572872 | tf_op jit(solution)/shard_map/ppermute | solution.py:31
  69.9 11.8 %all-to-all-start.3 = ((bf16[8,64,128]{2,1,0:T(8,128)(2,1)}), bf16[8,64,128]{2,1,0:T(8,128)(2,1)S(1)}, u32[]{:S(2)}, u32[]{:S(2)}) async-start(bf16[8,64,128]{2,1,0:T(8,128)(2,1)} %attend.1), calls=%async_computation.3 | async-start | bytes 262144 | tf_op jit(solution)/shard_map/all_to_all | solution.py:40
  74.1 1.0 %copy-start.4 = (bf16[128,2048]{1,0:T(8,128)(2,1)S(1)}, bf16[128,2048]{1,0:T(8,128)(2,1)}, u32[]{:S(2)}) copy-start(bf16[128,2048]{1,0:T(8,128)(2,1)} %copy-done.3) | copy-start | bytes 1572868
  75.2 24.0 %copy-start = (s32[32,2]{0,1:T(2,128)S(1)}, s32[32,2]{0,1:T(2,128)}, u32[]{:S(2)}) copy-start(s32[32,2]{0,1:T(2,128)} %param.15) | copy-start | bytes 772
  75.3 24.0 %copy-start.1 = (f32[32,2]{0,1:T(2,128)S(1)}, f32[32,2]{0,1:T(2,128)}, u32[]{:S(2)}) copy-start(f32[32,2]{0,1:T(2,128)} %param.16) | copy-start | bytes 772
  81.7 17.5 %all-to-all-start.1 = ((bf16[8,16,2048]{2,1,0:T(8,128)(2,1)}), bf16[8,16,2048]{2,1,0:T(8,128)(2,1)S(1)}, u32[]{:S(2)}, u32[]{:S(2)}) async-start(bf16[8,16,2048]{2,1,0:T(8,128)(2,1)} %finish.1), calls=%async_computation.1 | async-start | bytes 1048576 | tf_op jit(solution)/shard_map/all_to_all | solution.py:40
  87.1 6.8 %collective-permute-start.9 = (bf16[8,64,128]{2,1,0:T(8,128)(2,1)S(1)}, bf16[8,64,128]{2,1,0:T(8,128)(2,1)S(1)}, u32[]{:S(2)}, u32[]{:S(2)}) collective-permute-start(bf16[8,64,128]{2,1,0:T(8,128)(2,1)S(1)} %all-to-all-done.3.mixed_ref), channel_id=1, source_target_pairs={{0,3},{1,0},{2,1},{3,2},{4,7},{5,4},{6,5},{7,6},{8,11},{9,8},{10,9... | collective-permute-start | bytes 393224 | tf_op jit(solution)/shard_map/ppermute | solution.py:31

commit v6 on v5

--- a/solution.py
+++ b/solution.py
@@ -119,9 +119,7 @@
     )(partial, left, right)
 
 
-def combine_kernel(
-    ret_ref, mixed_ref, other_ref, routes_ref, gate_ref, context_ref, routed_ref
-):
+def prepare_kernel(mixed_ref, other_ref, routes_ref, gate_ref, context_ref, spread_ref):
     routes = routes_ref[...]
     gate = gate_ref[...]
     beams = routes.shape[1]
@@ -129,42 +127,61 @@
     to = lax.broadcasted_iota(jnp.int32, (beams, beams), 1)
     place = lax.broadcasted_iota(jnp.int32, (beams, CAP), 1).astype(F32)
     spread = []
-    summed = []
     for expert in range(EXPF):
         mine = jnp.sum((routes == expert).astype(F32), axis=0, keepdims=True)
         slot = jnp.sum(jnp.where(to < at, mine, 0.0), axis=1, keepdims=True)
         weight = jnp.sum(jnp.where(routes == expert, gate, 0.0), axis=0, keepdims=True)
         spread.append(jnp.where((place == slot) & (turn(mine) > 0.5), turn(weight), 0.0))
+    spread_ref[...] = jnp.concatenate(spread, axis=1)
+    odd = parity() == 1
+    for z in range(NZ):
+        mine, other = mixed_ref[z, :beams, :], other_ref[z, beams:, :]
+        first = 2 * z * HEAD
+        context_ref[:, first : first + HEAD] = jnp.where(odd, other, mine)
+        context_ref[:, first + HEAD : first + 2 * HEAD] = jnp.where(odd, mine, other)
+
+
+def prepare(mixed, other, routes, gate, beams, width):
+    return pl.pallas_call(
+        prepare_kernel,
+        out_shape=[
+            jax.ShapeDtypeStruct((beams, width), BF),
+            jax.ShapeDtypeStruct((beams, EXPF * CAP), F32),
+        ],
+        cost_estimate=pl.CostEstimate(
+            flops=100_000, bytes_accessed=400_000, transcendentals=0
+        ),
+        compiler_params=pltpu.CompilerParams(vmem_limit_bytes=4 * 2**20),
+        name="prepare",
+    )(mixed, other, routes, gate)
+
+
+def combine_kernel(ret_ref, spread_ref, routed_ref):
+    summed = []
+    for expert in range(EXPF):
         total = None
         for z in range(expert * HALF, (expert + 1) * HALF):
             term = ret_ref[LAST.index(z)].astype(F32)
             total = term if total is None else total + term
         summed.append(total)
     routed_ref[...] = jnp.dot(
-        jnp.concatenate(spread, axis=1),
+        spread_ref[...],
         jnp.concatenate(summed, axis=0),
         precision=lax.Precision.HIGHEST,
         preferred_element_type=F32,
     ).astype(BF)
-    odd = parity() == 1
-    for z in range(NZ):
-        mine, other = mixed_ref[z, :beams, :], other_ref[z, beams:, :]
-        first = 2 * z * HEAD
-        context_ref[:, first : first + HEAD] = jnp.where(odd, other, mine)
-        context_ref[:, first + HEAD : first + 2 * HEAD] = jnp.where(odd, mine, other)
-
-
-def combine(ret, mixed, other, routes, gate, beams, width):
-    shape = jax.ShapeDtypeStruct((beams, width), BF)
+
+
+def combine(ret, spread, beams, width):
     return pl.pallas_call(
         combine_kernel,
-        out_shape=[shape, shape],
+        out_shape=jax.ShapeDtypeStruct((beams, width), BF),
         cost_estimate=pl.CostEstimate(
             flops=25_000_000, bytes_accessed=1_000_000, transcendentals=0
         ),
         compiler_params=pltpu.CompilerParams(vmem_limit_bytes=6 * 2**20),
         name="combine",
-    )(ret, mixed, other, routes, gate)
+    )(ret, spread)
 
 
 def parity():
@@ -383,7 +400,8 @@
     part_l, part_r = experts([block_l, block_r], w_up, w_down)
     from_r, from_l = to_left(part_l), to_right(part_r)
     ret = along_z(finish(own_and_far(part, from_f), from_l, from_r), LAST)
-    context, routed = combine(ret, mixed, other, routes, route_gate, beams, width)
+    context, spread = prepare(mixed, other, routes, route_gate, beams, width)
+    routed = combine(ret, spread, beams, width)
     return (context, routed)
 
 

time: 101 us -> 101 us (level)
  the two profiles are of different devices: /device:TPU:120 before, /device:TPU:112 now
where the time goes in v6:
time: 101 us; the launch traced here: 100 us
  starting transfers between devices  60.7 us (60%)
  waiting for transfers between devices  21.2 us (21%)
  Pallas kernels  16.4 us (16%)
  local copies, waits for them, and re-layouts  1.06 us (1%)
    all_to_all x4, starting transfers between devices, along_z(): lax.all_to_all(a, 'dev', split_axis=0, concat_axis=0, axis_index_groups=r...  24.9 us
    ppermute x4, starting transfers between devices, to_left(): return lax.ppermute(a, 'dev', LEFT)  13.4 us
    ppermute x3, starting transfers between devices, to_far(): return lax.ppermute(a, 'dev', FAR)  12.9 us
    ppermute x3, starting transfers between devices, to_right(): return lax.ppermute(a, 'dev', RIGHT)  9.52 us
    ppermute x4, waiting for transfers between devices, to_left(): return lax.ppermute(a, 'dev', LEFT)  8.54 us
    all_to_all x4, waiting for transfers between devices, along_z(): lax.all_to_all(a, 'dev', split_axis=0, concat_axis=0, axis_index_groups=r...  7.43 us
    pallas_call x3, Pallas kernels, experts(): pl.pallas_call(experts_kernel, in_specs=[pl.BlockSpec(memory_space=pltpu....  4 us
    ppermute x3, waiting for transfers between devices, to_right(): return lax.ppermute(a, 'dev', RIGHT)  3.67 us
  transfers between devices with their start and end apart: 14, of which 8 were waited for; matrix products, arithmetic and copies ran while one was open for 0% of the time, Pallas kernels for 13%

profile of v6, /device:TPU:112, one launch (start us, length us, event | category | flops | bytes accessed | tf_op | source)
XLA Modules:
  0.0 100.2 jit_solution(13752913695584029055)
XLA Ops:
  0.6 2.0 %pack_rows.1 = bf16[8,16,2048]{2,1,0:T(8,128)(2,1)} custom-call(bf16[32,2048]{1,0:T(8,128)(2,1)} %queries_ref.3, s32[2,32]{1,0:T(2,128)} %bitcast.10, f32[1,2048]{1,0:T(1,128)} %bitcast.15), custom_call_target="tpu_custom_call" | custom-call | flops 4000000 | bytes 700000 | tf_op jit(solution)/shard_map/pack_rows/pallas_call | solution.py:76
  2.6 10.0 %all-to-all-start = ((bf16[8,16,2048]{2,1,0:T(8,128)(2,1)}), bf16[8,16,2048]{2,1,0:T(8,128)(2,1)S(1)}, u32[]{:S(2)}, u32[]{:S(2)}) async-start(bf16[8,16,2048]{2,1,0:T(8,128)(2,1)} %pack_rows.1), calls=%async_computation | async-start | bytes 1048576 | tf_op jit(solution)/shard_map/all_to_all | solution.py:40
  13.8 3.4 %collective-permute-start = (bf16[96,1024]{1,0:T(8,128)(2,1)S(1)}, bf16[96,1024]{1,0:T(8,128)(2,1)S(1)}, u32[]{:S(2)}, u32[]{:S(2)}) collective-permute-start(bf16[96,1024]{1,0:T(8,128)(2,1)S(1)} %get-tuple-element.20), channel_id=1, source_target_pairs={{0,1},{1,2},{2,3},{3,0},{4,5},{5,6},{6,7},{7,4},{8,9},{9,10},{10,1... | collective-permute-start | bytes 589832 | tf_op jit(solution)/shard_map/ppermute | solution.py:27
  17.2 4.6 %collective-permute-start.2 = (bf16[64,1024]{1,0:T(8,128)(2,1)S(1)}, bf16[64,1024]{1,0:T(8,128)(2,1)S(1)}, u32[]{:S(2)}, u32[]{:S(2)}) collective-permute-start(bf16[64,1024]{1,0:T(8,128)(2,1)S(1)} %get-tuple-element.22), channel_id=1, source_target_pairs={{0,2},{1,3},{2,0},{3,1},{4,6},{5,7},{6,4},{7,5},{8,10},{9,11},{10,... | collective-permute-start | bytes 393224 | tf_op jit(solution)/shard_map/ppermute | solution.py:35
  21.8 3.3 %collective-permute-start.1 = (bf16[64,1024]{1,0:T(8,128)(2,1)S(1)}, bf16[64,1024]{1,0:T(8,128)(2,1)S(1)}, u32[]{:S(2)}, u32[]{:S(2)}) collective-permute-start(bf16[64,1024]{1,0:T(8,128)(2,1)S(1)} %get-tuple-element.21), channel_id=1, source_target_pairs={{0,3},{1,0},{2,1},{3,2},{4,7},{5,4},{6,5},{7,6},{8,11},{9,8},{10,9... | collective-permute-start | bytes 393224 | tf_op jit(solution)/shard_map/ppermute | solution.py:31
  25.2 1.6 %collective-permute-done.2.far_ref = bf16[64,1024]{1,0:T(8,128)(2,1)S(1)} collective-permute-done((bf16[64,1024]{1,0:T(8,128)(2,1)S(1)}, bf16[64,1024]{1,0:T(8,128)(2,1)S(1)}, u32[]{:S(2)}, u32[]{:S(2)}) %collective-permute-start.2) | collective-permute-done | bytes 131104 | tf_op jit(solution)/shard_map/ppermute | solution.py:35
  27.9 4.9 %collective-permute-start.6 = (bf16[128,2048]{1,0:T(8,128)(2,1)S(1)}, bf16[128,2048]{1,0:T(8,128)(2,1)S(1)}, u32[]{:S(2)}, u32[]{:S(2)}) collective-permute-start(bf16[128,2048]{1,0:T(8,128)(2,1)S(1)} %bitcast.6), channel_id=1, source_target_pairs={{0,2},{1,3},{2,0},{3,1},{4,6},{5,7},{6,4},{7,5},{8,10},{9,11},{10,... | collective-permute-start | bytes 1572872 | tf_op jit(solution)/shard_map/ppermute | solution.py:35
  32.9 3.0 %collective-permute-start.5 = (bf16[128,2048]{1,0:T(8,128)(2,1)S(1)}, bf16[128,2048]{1,0:T(8,128)(2,1)S(1)}, u32[]{:S(2)}, u32[]{:S(2)}) collective-permute-start(bf16[128,2048]{1,0:T(8,128)(2,1)S(1)} %bitcast.7), channel_id=1, source_target_pairs={{0,3},{1,0},{2,1},{3,2},{4,7},{5,4},{6,5},{7,6},{8,11},{9,8},{10,9... | collective-permute-start | bytes 1572872 | tf_op jit(solution)/shard_map/ppermute | solution.py:31
  35.9 2.8 %collective-permute-start.4 = (bf16[128,2048]{1,0:T(8,128)(2,1)S(1)}, bf16[128,2048]{1,0:T(8,128)(2,1)S(1)}, u32[]{:S(2)}, u32[]{:S(2)}) collective-permute-start(bf16[128,2048]{1,0:T(8,128)(2,1)S(1)} %bitcast.8), channel_id=1, source_target_pairs={{0,1},{1,2},{2,3},{3,0},{4,5},{5,6},{6,7},{7,4},{8,9},{9,10},{10,1... | collective-permute-start | bytes 1572872 | tf_op jit(solution)/shard_map/ppermute | solution.py:27
  39.7 5.4 %all-to-all-start.1 = ((bf16[8,320,128]{2,1,0:T(8,128)(2,1)}), bf16[8,320,128]{2,1,0:T(8,128)(2,1)}, u32[]{:S(2)}, u32[]{:S(2)}) async-start(bf16[8,320,128]{2,1,0:T(8,128)(2,1)} %pack_heads.1), calls=%async_computation.1 | async-start | bytes 1310720 | tf_op jit(solution)/shard_map/all_to_all | solution.py:40
  45.1 2.2 %preload.1 = (bf16[2048,512]{1,0:T(8,128)(2,1)S(1)}, bf16[512,2048]{1,0:T(8,128)(2,1)S(1)}) custom-call(bf16[2048,512]{1,0:T(8,128)(2,1)} %up_ref, bf16[512,2048]{1,0:T(8,128)(2,1)} %down_ref), custom_call_target="tpu_custom_call" | custom-call | bytes 8388608 | tf_op jit(solution)/shard_map/preload/pallas_call | solution.py:329
  49.2 3.4 %collective-permute-start.7 = (bf16[128,2048]{1,0:T(8,128)(2,1)S(1)}, bf16[128,2048]{1,0:T(8,128)(2,1)S(1)}, u32[]{:S(2)}, u32[]{:S(2)}) collective-permute-start(bf16[128,2048]{1,0:T(8,128)(2,1)S(1)} %experts.4), channel_id=1, source_target_pairs={{0,2},{1,3},{2,0},{3,1},{4,6},{5,7},{6,4},{7,5},{8,10},{9,11},{10,... | collective-permute-start | bytes 1572872 | tf_op jit(solution)/shard_map/ppermute | solution.py:35
  52.6 4.9 %collective-permute-done.5.refs_1_ = bf16[128,2048]{1,0:T(8,128)(2,1)S(1)} collective-permute-done((bf16[128,2048]{1,0:T(8,128)(2,1)S(1)}, bf16[128,2048]{1,0:T(8,128)(2,1)S(1)}, u32[]{:S(2)}, u32[]{:S(2)}) %collective-permute-start.5) | collective-permute-done | bytes 524320 | tf_op jit(solution)/shard_map/ppermute | solution.py:31
  57.5 2.2 %experts.5 = (bf16[128,2048]{1,0:T(8,128)(2,1)S(1)}, bf16[128,2048]{1,0:T(8,128)(2,1)}) custom-call(bf16[128,2048]{1,0:T(8,128)(2,1)S(1)} %collective-permute-done.4.refs_0_, bf16[128,2048]{1,0:T(8,128)(2,1)S(1)} %collective-permute-done.5.refs_1_, bf16[2048,512]{1,0:T(8,128)(2,1)S(1)} %get-tuple-element.28.refs_1_.refs_2_, ...), custom_call_target="tpu_custom_call" | custom-call | flops 107374182400 | bytes 6291456 | tf_op jit(solution)/shard_map/experts/pallas_call | solution.py:357
  59.7 3.3 %collective-permute-start.8 = (bf16[128,2048]{1,0:T(8,128)(2,1)}, bf16[128,2048]{1,0:T(8,128)(2,1)S(1)}, u32[]{:S(2)}, u32[]{:S(2)}) collective-permute-start(bf16[128,2048]{1,0:T(8,128)(2,1)} %get-tuple-element.33), channel_id=1, source_target_pairs={{0,1},{1,2},{2,3},{3,0},{4,5},{5,6},{6,7},{7,4},{8,9},{9,10},{10,1... | collective-permute-start | bytes 1572872 | tf_op jit(solution)/shard_map/ppermute | solution.py:27
  63.0 3.7 %collective-permute-start.9 = (bf16[128,2048]{1,0:T(8,128)(2,1)S(1)}, bf16[128,2048]{1,0:T(8,128)(2,1)S(1)}, u32[]{:S(2)}, u32[]{:S(2)}) collective-permute-start(bf16[128,2048]{1,0:T(8,128)(2,1)S(1)} %get-tuple-element.34), channel_id=1, source_target_pairs={{0,3},{1,0},{2,1},{3,2},{4,7},{5,4},{6,5},{7,6},{8,11},{9,8},{10,9... | collective-permute-start | bytes 1572872 | tf_op jit(solution)/shard_map/ppermute | solution.py:31
  66.8 3.2 %attend.1 = bf16[8,64,128]{2,1,0:T(8,128)(2,1)} custom-call(s32[32]{0:T(128)S(1)} %copy-done.2, bf16[8,320,128]{2,1,0:T(8,128)(2,1)} %all-to-all-done.1.got_ref, s32[4,32]{1,0:T(4,128)} %counts_ref.1), custom_call_target="tpu_custom_call" | custom-call | flops 300000000 | bytes 1000000 | tf_op jit(solution)/shard_map/attend/pallas_call | solution.py:301
  70.0 4.1 %all-to-all-start.2 = ((bf16[8,64,128]{2,1,0:T(8,128)(2,1)}), bf16[8,64,128]{2,1,0:T(8,128)(2,1)S(1)}, u32[]{:S(2)}, u32[]{:S(2)}) async-start(bf16[8,64,128]{2,1,0:T(8,128)(2,1)} %attend.1), calls=%async_computation.2 | async-start | bytes 262144 | tf_op jit(solution)/shard_map/all_to_all | solution.py:40
  75.2 3.7 %collective-permute-done.8.left_ref = bf16[128,2048]{1,0:T(8,128)(2,1)S(1)} collective-permute-done((bf16[128,2048]{1,0:T(8,128)(2,1)}, bf16[128,2048]{1,0:T(8,128)(2,1)S(1)}, u32[]{:S(2)}, u32[]{:S(2)}) %collective-permute-start.8) | collective-permute-done | bytes 524320 | tf_op jit(solution)/shard_map/ppermute | solution.py:27
  80.0 1.7 %all-to-all-done.2.mixed_ref = bf16[8,64,128]{2,1,0:T(8,128)(2,1)S(1)} async-done(((bf16[8,64,128]{2,1,0:T(8,128)(2,1)}), bf16[8,64,128]{2,1,0:T(8,128)(2,1)S(1)}, u32[]{:S(2)}, u32[]{:S(2)}) %all-to-all-start.2) | async-done | bytes 131104 | tf_op jit(solution)/shard_map/all_to_all | solution.py:40
  81.7 5.4 %all-to-all-start.3 = ((bf16[8,16,2048]{2,1,0:T(8,128)(2,1)}), bf16[8,16,2048]{2,1,0:T(8,128)(2,1)S(1)}, u32[]{:S(2)}, u32[]{:S(2)}) async-start(bf16[8,16,2048]{2,1,0:T(8,128)(2,1)} %finish.1), calls=%async_computation.3 | async-start | bytes 1048576 | tf_op jit(solution)/shard_map/all_to_all | solution.py:40
  87.1 3.3 %collective-permute-start.3 = (bf16[8,64,128]{2,1,0:T(8,128)(2,1)S(1)}, bf16[8,64,128]{2,1,0:T(8,128)(2,1)S(1)}, u32[]{:S(2)}, u32[]{:S(2)}) collective-permute-start(bf16[8,64,128]{2,1,0:T(8,128)(2,1)S(1)} %all-to-all-done.2.mixed_ref), channel_id=1, source_target_pairs={{0,3},{1,0},{2,1},{3,2},{4,7},{5,4},{6,5},{7,6},{8,11},{9,8},{10,9... | collective-permute-start | bytes 393224 | tf_op jit(solution)/shard_map/ppermute | solution.py:31
  90.4 3.6 %collective-permute-done.3.other_ref = bf16[8,64,128]{2,1,0:T(8,128)(2,1)S(1)} collective-permute-done((bf16[8,64,128]{2,1,0:T(8,128)(2,1)S(1)}, bf16[8,64,128]{2,1,0:T(8,128)(2,1)S(1)}, u32[]{:S(2)}, u32[]{:S(2)}) %collective-permute-start.3) | collective-permute-done | bytes 131104 | tf_op jit(solution)/shard_map/ppermute | solution.py:31
  94.7 4.5 %all-to-all-done.3.ret_ref = bf16[8,16,2048]{2,1,0:T(8,128)(2,1)S(1)} async-done(((bf16[8,16,2048]{2,1,0:T(8,128)(2,1)}), bf16[8,16,2048]{2,1,0:T(8,128)(2,1)S(1)}, u32[]{:S(2)}, u32[]{:S(2)}) %all-to-all-start.3) | async-done | bytes 524320 | tf_op jit(solution)/shard_map/all_to_all | solution.py:40
  (26 shorter events, 9.1 us)
Async XLA Ops:
  2.6 25.3 %all-to-all-start = ((bf16[8,16,2048]{2,1,0:T(8,128)(2,1)}), bf16[8,16,2048]{2,1,0:T(8,128)(2,1)S(1)}, u32[]{:S(2)}, u32[]{:S(2)}) async-start(bf16[8,16,2048]{2,1,0:T(8,128)(2,1)} %pack_rows.1), calls=%async_computation | async-start | bytes 1048576 | tf_op jit(solution)/shard_map/all_to_all | solution.py:40
  13.8 25.0 %collective-permute-start = (bf16[96,1024]{1,0:T(8,128)(2,1)S(1)}, bf16[96,1024]{1,0:T(8,128)(2,1)S(1)}, u32[]{:S(2)}, u32[]{:S(2)}) collective-permute-start(bf16[96,1024]{1,0:T(8,128)(2,1)S(1)} %get-tuple-element.20), channel_id=1, source_target_pairs={{0,1},{1,2},{2,3},{3,0},{4,5},{5,6},{6,7},{7,4},{8,9},{9,10},{10,1... | collective-permute-start | bytes 589832 | tf_op jit(solution)/shard_map/ppermute | solution.py:27
  17.2 9.6 %collective-permute-start.2 = (bf16[64,1024]{1,0:T(8,128)(2,1)S(1)}, bf16[64,1024]{1,0:T(8,128)(2,1)S(1)}, u32[]{:S(2)}, u32[]{:S(2)}) collective-permute-start(bf16[64,1024]{1,0:T(8,128)(2,1)S(1)} %get-tuple-element.22), channel_id=1, source_target_pairs={{0,2},{1,3},{2,0},{3,1},{4,6},{5,7},{6,4},{7,5},{8,10},{9,11},{10,... | collective-permute-start | bytes 393224 | tf_op jit(solution)/shard_map/ppermute | solution.py:35
  21.8 16.9 %collective-permute-start.1 = (bf16[64,1024]{1,0:T(8,128)(2,1)S(1)}, bf16[64,1024]{1,0:T(8,128)(2,1)S(1)}, u32[]{:S(2)}, u32[]{:S(2)}) collective-permute-start(bf16[64,1024]{1,0:T(8,128)(2,1)S(1)} %get-tuple-element.21), channel_id=1, source_target_pairs={{0,3},{1,0},{2,1},{3,2},{4,7},{5,4},{6,5},{7,6},{8,11},{9,8},{10,9... | collective-permute-start | bytes 393224 | tf_op jit(solution)/shard_map/ppermute | solution.py:31
  27.9 20.4 %collective-permute-start.6 = (bf16[128,2048]{1,0:T(8,128)(2,1)S(1)}, bf16[128,2048]{1,0:T(8,128)(2,1)S(1)}, u32[]{:S(2)}, u32[]{:S(2)}) collective-permute-start(bf16[128,2048]{1,0:T(8,128)(2,1)S(1)} %bitcast.6), channel_id=1, source_target_pairs={{0,2},{1,3},{2,0},{3,1},{4,6},{5,7},{6,4},{7,5},{8,10},{9,11},{10,... | collective-permute-start | bytes 1572872 | tf_op jit(solution)/shard_map/ppermute | solution.py:35
  32.9 24.6 %collective-permute-start.5 = (bf16[128,2048]{1,0:T(8,128)(2,1)S(1)}, bf16[128,2048]{1,0:T(8,128)(2,1)S(1)}, u32[]{:S(2)}, u32[]{:S(2)}) collective-permute-start(bf16[128,2048]{1,0:T(8,128)(2,1)S(1)} %bitcast.7), channel_id=1, source_target_pairs={{0,3},{1,0},{2,1},{3,2},{4,7},{5,4},{6,5},{7,6},{8,11},{9,8},{10,9... | collective-permute-start | bytes 1572872 | tf_op jit(solution)/shard_map/ppermute | solution.py:31
  35.9 21.6 %collective-permute-start.4 = (bf16[128,2048]{1,0:T(8,128)(2,1)S(1)}, bf16[128,2048]{1,0:T(8,128)(2,1)S(1)}, u32[]{:S(2)}, u32[]{:S(2)}) collective-permute-start(bf16[128,2048]{1,0:T(8,128)(2,1)S(1)} %bitcast.8), channel_id=1, source_target_pairs={{0,1},{1,2},{2,3},{3,0},{4,5},{5,6},{6,7},{7,4},{8,9},{9,10},{10,1... | collective-permute-start | bytes 1572872 | tf_op jit(solution)/shard_map/ppermute | solution.py:27
  39.7 27.0 %all-to-all-start.1 = ((bf16[8,320,128]{2,1,0:T(8,128)(2,1)}), bf16[8,320,128]{2,1,0:T(8,128)(2,1)}, u32[]{:S(2)}, u32[]{:S(2)}) async-start(bf16[8,320,128]{2,1,0:T(8,128)(2,1)} %pack_heads.1), calls=%async_computation.1 | async-start | bytes 1310720 | tf_op jit(solution)/shard_map/all_to_all | solution.py:40
  48.3 0.9 copy-start.3
  49.2 17.6 %copy-start.2 = (s32[32]{0:T(128)S(1)}, s32[32]{0:T(128)}, u32[]{:S(2)}) copy-start(s32[32]{0:T(128)} %owner_ref.1) | copy-start | bytes 388
  49.2 24.9 %collective-permute-start.7 = (bf16[128,2048]{1,0:T(8,128)(2,1)S(1)}, bf16[128,2048]{1,0:T(8,128)(2,1)S(1)}, u32[]{:S(2)}, u32[]{:S(2)}) collective-permute-start(bf16[128,2048]{1,0:T(8,128)(2,1)S(1)} %experts.4), channel_id=1, source_target_pairs={{0,2},{1,3},{2,0},{3,1},{4,6},{5,7},{6,4},{7,5},{8,10},{9,11},{10,... | collective-permute-start | bytes 1572872 | tf_op jit(solution)/shard_map/ppermute | solution.py:35
  59.7 19.2 %collective-permute-start.8 = (bf16[128,2048]{1,0:T(8,128)(2,1)}, bf16[128,2048]{1,0:T(8,128)(2,1)S(1)}, u32[]{:S(2)}, u32[]{:S(2)}) collective-permute-start(bf16[128,2048]{1,0:T(8,128)(2,1)} %get-tuple-element.33), channel_id=1, source_target_pairs={{0,1},{1,2},{2,3},{3,0},{4,5},{5,6},{6,7},{7,4},{8,9},{9,10},{10,1... | collective-permute-start | bytes 1572872 | tf_op jit(solution)/shard_map/ppermute | solution.py:27
  63.0 16.0 %collective-permute-start.9 = (bf16[128,2048]{1,0:T(8,128)(2,1)S(1)}, bf16[128,2048]{1,0:T(8,128)(2,1)S(1)}, u32[]{:S(2)}, u32[]{:S(2)}) collective-permute-start(bf16[128,2048]{1,0:T(8,128)(2,1)S(1)} %get-tuple-element.34), channel_id=1, source_target_pairs={{0,3},{1,0},{2,1},{3,2},{4,7},{5,4},{6,5},{7,6},{8,11},{9,8},{10,9... | collective-permute-start | bytes 1572872 | tf_op jit(solution)/shard_map/ppermute | solution.py:31
  70.0 11.7 %all-to-all-start.2 = ((bf16[8,64,128]{2,1,0:T(8,128)(2,1)}), bf16[8,64,128]{2,1,0:T(8,128)(2,1)S(1)}, u32[]{:S(2)}, u32[]{:S(2)}) async-start(bf16[8,64,128]{2,1,0:T(8,128)(2,1)} %attend.1), calls=%async_computation.2 | async-start | bytes 262144 | tf_op jit(solution)/shard_map/all_to_all | solution.py:40
  74.1 1.0 %copy-start.4 = (bf16[128,2048]{1,0:T(8,128)(2,1)S(1)}, bf16[128,2048]{1,0:T(8,128)(2,1)}, u32[]{:S(2)}) copy-start(bf16[128,2048]{1,0:T(8,128)(2,1)} %copy-done.3) | copy-start | bytes 1572868
  75.2 18.7 %copy-start = (s32[32,2]{0,1:T(2,128)S(1)}, s32[32,2]{0,1:T(2,128)}, u32[]{:S(2)}) copy-start(s32[32,2]{0,1:T(2,128)} %param.15) | copy-start | bytes 772
  75.2 18.7 %copy-start.1 = (f32[32,2]{0,1:T(2,128)S(1)}, f32[32,2]{0,1:T(2,128)}, u32[]{:S(2)}) copy-start(f32[32,2]{0,1:T(2,128)} %param.16) | copy-start | bytes 772
  81.7 17.5 %all-to-all-start.3 = ((bf16[8,16,2048]{2,1,0:T(8,128)(2,1)}), bf16[8,16,2048]{2,1,0:T(8,128)(2,1)S(1)}, u32[]{:S(2)}, u32[]{:S(2)}) async-start(bf16[8,16,2048]{2,1,0:T(8,128)(2,1)} %finish.1), calls=%async_computation.3 | async-start | bytes 1048576 | tf_op jit(solution)/shard_map/all_to_all | solution.py:40
  87.1 6.8 %collective-permute-start.3 = (bf16[8,64,128]{2,1,0:T(8,128)(2,1)S(1)}, bf16[8,64,128]{2,1,0:T(8,128)(2,1)S(1)}, u32[]{:S(2)}, u32[]{:S(2)}) collective-permute-start(bf16[8,64,128]{2,1,0:T(8,128)(2,1)S(1)} %all-to-all-done.2.mixed_ref), channel_id=1, source_target_pairs={{0,3},{1,0},{2,1},{3,2},{4,7},{5,4},{6,5},{7,6},{8,11},{9,8},{10,9... | collective-permute-start | bytes 393224 | tf_op jit(solution)/shard_map/ppermute | solution.py:31

commit v7 on v5

--- a/solution.py
+++ b/solution.py
@@ -297,28 +297,23 @@
     )(owner, got, *in_hbm(counts))
 
 
-def preload_kernel(up_ref, down_ref, up_out, down_out, sems):
-    copies = [
-        pltpu.make_async_copy(source, target, sems.at[at])
-        for at, (source, target) in enumerate(((up_ref, up_out), (down_ref, down_out)))
-    ]
-    for copy in copies:
-        copy.start()
-    for copy in copies:
-        copy.wait()
-
-
-def preload(up, down):
+def preload_kernel(source_ref, target_ref, sem):
+    copy = pltpu.make_async_copy(source_ref, target_ref, sem)
+    copy.start()
+    copy.wait()
+
+
+def preload(weight):
     return pl.pallas_call(
         preload_kernel,
-        in_specs=[pl.BlockSpec(memory_space=pl.ANY)] * 2,
-        out_specs=[pl.BlockSpec(memory_space=pltpu.VMEM)] * 2,
-        out_shape=[jax.ShapeDtypeStruct(a.shape, a.dtype) for a in (up, down)],
-        scratch_shapes=[pltpu.SemaphoreType.DMA((2,))],
-        cost_estimate=pl.CostEstimate(flops=0, bytes_accessed=8 * 2**20, transcendentals=0),
-        compiler_params=pltpu.CompilerParams(vmem_limit_bytes=6 * 2**20),
+        in_specs=[pl.BlockSpec(memory_space=pl.ANY)],
+        out_specs=pl.BlockSpec(memory_space=pltpu.VMEM),
+        out_shape=jax.ShapeDtypeStruct(weight.shape, weight.dtype),
+        scratch_shapes=[pltpu.SemaphoreType.DMA],
+        cost_estimate=pl.CostEstimate(flops=0, bytes_accessed=4 * 2**20, transcendentals=0),
+        compiler_params=pltpu.CompilerParams(vmem_limit_bytes=4 * 2**20),
         name="preload",
-    )(*in_hbm(up, down))
+    )(*in_hbm(weight))
 
 
 def experts_kernel(*refs):
@@ -367,10 +362,12 @@
     )
     left, right, far = to_right(for_right), to_left(for_left), to_far(for_far)
     block = along_z(packed, FIRST).reshape(size, width)
-    block, far = lax.optimization_barrier((block, far))
+    w_up, _ = lax.optimization_barrier((w_up, for_far))
+    w_up = preload(w_up)
+    block, far, w_up = lax.optimization_barrier((block, far, w_up))
     block_f, block_l, block_r = to_far(block), to_right(block), to_left(block)
-    w_up, w_down, _ = lax.optimization_barrier((w_up, w_down, block))
-    w_up, w_down = preload(w_up, w_down)
+    w_down, _ = lax.optimization_barrier((w_down, block))
+    w_down = preload(w_down)
     (part,) = experts([block], w_up, w_down)
 
     got = along_z(pack_heads(mine, left, right, far))

time: 101 us -> 104 us (1.030)
  the two profiles are of different devices: /device:TPU:120 before, /device:TPU:32 now
where the time goes in v7:
time: 104 us; the launch traced here: 103 us
  starting transfers between devices  63 us (61%)
  Pallas kernels  22.4 us (22%)
  waiting for transfers between devices  14 us (13%)
  local copies, waits for them, and re-layouts  2.61 us (3%)
    all_to_all x4, starting transfers between devices, along_z(): lax.all_to_all(a, 'dev', split_axis=0, concat_axis=0, axis_index_groups=r...  29.5 us
    ppermute x4, starting transfers between devices, to_left(): return lax.ppermute(a, 'dev', LEFT)  12.6 us
    ppermute x3, starting transfers between devices, to_far(): return lax.ppermute(a, 'dev', FAR)  11.3 us
    ppermute x3, starting transfers between devices, to_right(): return lax.ppermute(a, 'dev', RIGHT)  9.73 us
    all_to_all x4, waiting for transfers between devices, along_z(): lax.all_to_all(a, 'dev', split_axis=0, concat_axis=0, axis_index_groups=r...  9.02 us
    pallas_call x3, Pallas kernels, experts(): pl.pallas_call(experts_kernel, in_specs=[pl.BlockSpec(memory_space=pltpu....  7.06 us
    ppermute x4, waiting for transfers between devices, to_left(): return lax.ppermute(a, 'dev', LEFT)  4.49 us
    pallas_call x2, Pallas kernels, preload(): pl.pallas_call(preload_kernel, in_specs=[pl.BlockSpec(memory_space=pl.ANY...  3.2 us
  transfers between devices with their start and end apart: 14, of which 4 were waited for; matrix products, arithmetic and copies ran while one was open for 0% of the time, Pallas kernels for 19%

profile of v7, /device:TPU:32, one launch (start us, length us, event | category | flops | bytes accessed | tf_op | source)
XLA Modules:
  0.0 102.9 jit_solution(150188848124615037)
XLA Ops:
  0.6 2.0 %pack_rows.1 = bf16[8,16,2048]{2,1,0:T(8,128)(2,1)} custom-call(bf16[32,2048]{1,0:T(8,128)(2,1)} %queries_ref.3, s32[2,32]{1,0:T(2,128)} %bitcast.10, f32[1,2048]{1,0:T(1,128)} %bitcast.15), custom_call_target="tpu_custom_call" | custom-call | flops 4000000 | bytes 700000 | tf_op jit(solution)/shard_map/pack_rows/pallas_call | solution.py:76
  2.6 10.3 %all-to-all-start = ((bf16[8,16,2048]{2,1,0:T(8,128)(2,1)}), bf16[8,16,2048]{2,1,0:T(8,128)(2,1)S(1)}, u32[]{:S(2)}, u32[]{:S(2)}) async-start(bf16[8,16,2048]{2,1,0:T(8,128)(2,1)} %pack_rows.1), calls=%async_computation | async-start | bytes 1048576 | tf_op jit(solution)/shard_map/all_to_all | solution.py:40
  13.0 1.9 %split_heads.1 = (bf16[96,1024]{1,0:T(8,128)(2,1)}, bf16[64,1024]{1,0:T(8,128)(2,1)}, bf16[64,1024]{1,0:T(8,128)(2,1)S(1)}, bf16[96,1024]{1,0:T(8,128)(2,1)S(1)}) custom-call(bf16[32,2048]{1,0:T(8,128)(2,1)} %queries_ref.3, bf16[32,2048]{1,0:T(8,128)(2,1)} %bitcast.13, bf16[32,2048]{1,0:T(8,128)(2,1)} %bitcast.14), custom_call_target="tpu_custom_call" | custom-call | flops 200000 | bytes 1700000 | tf_op jit(solution)/shard_map/split_heads/pallas_call | solution.py:198
  14.8 3.4 %collective-permute-start.7 = (bf16[96,1024]{1,0:T(8,128)(2,1)}, bf16[96,1024]{1,0:T(8,128)(2,1)S(1)}, u32[]{:S(2)}, u32[]{:S(2)}) collective-permute-start(bf16[96,1024]{1,0:T(8,128)(2,1)} %get-tuple-element.27), channel_id=1, source_target_pairs={{0,1},{1,2},{2,3},{3,0},{4,5},{5,6},{6,7},{7,4},{8,9},{9,10},{10,1... | collective-permute-start | bytes 589832 | tf_op jit(solution)/shard_map/ppermute | solution.py:27
  18.2 4.6 %collective-permute-start = (bf16[64,1024]{1,0:T(8,128)(2,1)S(1)}, bf16[64,1024]{1,0:T(8,128)(2,1)S(1)}, u32[]{:S(2)}, u32[]{:S(2)}) collective-permute-start(bf16[64,1024]{1,0:T(8,128)(2,1)S(1)} %get-tuple-element.16), channel_id=1, source_target_pairs={{0,2},{1,3},{2,0},{3,1},{4,6},{5,7},{6,4},{7,5},{8,10},{9,11},{10,... | collective-permute-start | bytes 393224 | tf_op jit(solution)/shard_map/ppermute | solution.py:35
  22.9 3.3 %collective-permute-start.8 = (bf16[64,1024]{1,0:T(8,128)(2,1)}, bf16[64,1024]{1,0:T(8,128)(2,1)}, u32[]{:S(2)}, u32[]{:S(2)}) collective-permute-start(bf16[64,1024]{1,0:T(8,128)(2,1)} %get-tuple-element.28), channel_id=1, source_target_pairs={{0,3},{1,0},{2,1},{3,2},{4,7},{5,4},{6,5},{7,6},{8,11},{9,8},{10,9... | collective-permute-start | bytes 393224 | tf_op jit(solution)/shard_map/ppermute | solution.py:31
  26.2 1.6 %preload.2.refs_1_.refs_2_ = bf16[2048,512]{1,0:T(8,128)(2,1)S(1)} custom-call(bf16[2048,512]{1,0:T(8,128)(2,1)} %source_ref), custom_call_target="tpu_custom_call" | custom-call | bytes 4194304 | tf_op jit(solution)/shard_map/preload/pallas_call | solution.py:307
  28.9 3.0 %collective-permute-start.3 = (bf16[128,2048]{1,0:T(8,128)(2,1)S(1)}, bf16[128,2048]{1,0:T(8,128)(2,1)}, u32[]{:S(2)}, u32[]{:S(2)}) collective-permute-start(bf16[128,2048]{1,0:T(8,128)(2,1)S(1)} %bitcast.6), channel_id=1, source_target_pairs={{0,2},{1,3},{2,0},{3,1},{4,6},{5,7},{6,4},{7,5},{8,10},{9,11},{10,... | collective-permute-start | bytes 1572872 | tf_op jit(solution)/shard_map/ppermute | solution.py:35
  32.0 4.3 %collective-permute-start.2 = (bf16[128,2048]{1,0:T(8,128)(2,1)S(1)}, bf16[128,2048]{1,0:T(8,128)(2,1)S(1)}, u32[]{:S(2)}, u32[]{:S(2)}) collective-permute-start(bf16[128,2048]{1,0:T(8,128)(2,1)S(1)} %bitcast.7), channel_id=1, source_target_pairs={{0,3},{1,0},{2,1},{3,2},{4,7},{5,4},{6,5},{7,6},{8,11},{9,8},{10,9... | collective-permute-start | bytes 1572872 | tf_op jit(solution)/shard_map/ppermute | solution.py:31
  36.3 1.9 %collective-permute-start.1 = (bf16[128,2048]{1,0:T(8,128)(2,1)S(1)}, bf16[128,2048]{1,0:T(8,128)(2,1)}, u32[]{:S(2)}, u32[]{:S(2)}) collective-permute-start(bf16[128,2048]{1,0:T(8,128)(2,1)S(1)} %bitcast.8), channel_id=1, source_target_pairs={{0,1},{1,2},{2,3},{3,0},{4,5},{5,6},{6,7},{7,4},{8,9},{9,10},{10,1... | collective-permute-start | bytes 1572872 | tf_op jit(solution)/shard_map/ppermute | solution.py:27
  39.1 1.9 %pack_heads.1 = bf16[8,320,128]{2,1,0:T(8,128)(2,1)} custom-call(bf16[96,1024]{1,0:T(8,128)(2,1)S(1)} %get-tuple-element.26.mine_ref, bf16[96,1024]{1,0:T(8,128)(2,1)S(1)} %collective-permute-done.7.left_ref, bf16[64,1024]{1,0:T(8,128)(2,1)} %collective-permute-done.8.right_ref, bf16[64,1024]{1,0:T(8,128)(2,1)S(1)} %copy-done.3), custom_call_target="tpu_custom_call" | custom-call | flops 20000000000 | bytes 1300000 | tf_op jit(solution)/shard_map/pack_heads/pallas_call | solution.py:225
  41.0 7.4 %all-to-all-start.2 = ((bf16[8,320,128]{2,1,0:T(8,128)(2,1)}), bf16[8,320,128]{2,1,0:T(8,128)(2,1)}, u32[]{:S(2)}, u32[]{:S(2)}) async-start(bf16[8,320,128]{2,1,0:T(8,128)(2,1)} %pack_heads.1), calls=%async_computation.2 | async-start | bytes 1310720 | tf_op jit(solution)/shard_map/all_to_all | solution.py:40
  50.9 2.9 %experts.4 = bf16[128,2048]{1,0:T(8,128)(2,1)} custom-call(bf16[128,2048]{1,0:T(8,128)(2,1)} %collective-permute-done.3.refs_0_, bf16[2048,512]{1,0:T(8,128)(2,1)S(1)} %preload.2.refs_1_.refs_2_, bf16[512,2048]{1,0:T(8,128)(2,1)S(1)} %preload.3.refs_2_.refs_3_), custom_call_target="tpu_custom_call" | custom-call | flops 53687091200 | bytes 5242880 | tf_op jit(solution)/shard_map/experts/pallas_call | solution.py:335
  53.9 3.6 %collective-permute-start.4 = (bf16[128,2048]{1,0:T(8,128)(2,1)}, bf16[128,2048]{1,0:T(8,128)(2,1)}, u32[]{:S(2)}, u32[]{:S(2)}) collective-permute-start(bf16[128,2048]{1,0:T(8,128)(2,1)} %experts.4), channel_id=1, source_target_pairs={{0,2},{1,3},{2,0},{3,1},{4,6},{5,7},{6,4},{7,5},{8,10},{9,11},{10,... | collective-permute-start | bytes 1572872 | tf_op jit(solution)/shard_map/ppermute | solution.py:35
  57.5 3.2 %experts.5 = (bf16[128,2048]{1,0:T(8,128)(2,1)S(1)}, bf16[128,2048]{1,0:T(8,128)(2,1)}) custom-call(bf16[128,2048]{1,0:T(8,128)(2,1)} %collective-permute-done.1.refs_0_, bf16[128,2048]{1,0:T(8,128)(2,1)S(1)} %collective-permute-done.2.refs_1_, bf16[2048,512]{1,0:T(8,128)(2,1)S(1)} %preload.2.refs_1_.refs_2_, bf16[512,2048]{1,0:T(8,128)(2,1)S(1)} %preload.3.refs_2_.refs_3_), custom_call_target="tpu_custom_call" | custom-call | flops 107374182400 | bytes 6291456 | tf_op jit(solution)/shard_map/experts/pallas_call | solution.py:335
  60.7 4.4 %collective-permute-start.5 = (bf16[128,2048]{1,0:T(8,128)(2,1)}, bf16[128,2048]{1,0:T(8,128)(2,1)S(1)}, u32[]{:S(2)}, u32[]{:S(2)}) collective-permute-start(bf16[128,2048]{1,0:T(8,128)(2,1)} %get-tuple-element.24), channel_id=1, source_target_pairs={{0,1},{1,2},{2,3},{3,0},{4,5},{5,6},{6,7},{7,4},{8,9},{9,10},{10,1... | collective-permute-start | bytes 1572872 | tf_op jit(solution)/shard_map/ppermute | solution.py:27
  65.1 2.6 %collective-permute-start.6 = (bf16[128,2048]{1,0:T(8,128)(2,1)S(1)}, bf16[128,2048]{1,0:T(8,128)(2,1)S(1)}, u32[]{:S(2)}, u32[]{:S(2)}) collective-permute-start(bf16[128,2048]{1,0:T(8,128)(2,1)S(1)} %get-tuple-element.25), channel_id=1, source_target_pairs={{0,3},{1,0},{2,1},{3,2},{4,7},{5,4},{6,5},{7,6},{8,11},{9,8},{10,9... | collective-permute-start | bytes 1572872 | tf_op jit(solution)/shard_map/ppermute | solution.py:31
  67.8 3.2 %attend.1 = bf16[8,64,128]{2,1,0:T(8,128)(2,1)} custom-call(s32[32]{0:T(128)S(1)} %copy-done.4, bf16[8,320,128]{2,1,0:T(8,128)(2,1)} %all-to-all-done.2.got_ref, s32[4,32]{1,0:T(4,128)} %counts_ref.1), custom_call_target="tpu_custom_call" | custom-call | flops 300000000 | bytes 1000000 | tf_op jit(solution)/shard_map/attend/pallas_call | solution.py:284
  70.9 7.2 %all-to-all-start.3 = ((bf16[8,64,128]{2,1,0:T(8,128)(2,1)}), bf16[8,64,128]{2,1,0:T(8,128)(2,1)S(1)}, u32[]{:S(2)}, u32[]{:S(2)}) async-start(bf16[8,64,128]{2,1,0:T(8,128)(2,1)} %attend.1), calls=%async_computation.3 | async-start | bytes 262144 | tf_op jit(solution)/shard_map/all_to_all | solution.py:40
  81.4 5.9 %all-to-all-done.3.mixed_ref = bf16[8,64,128]{2,1,0:T(8,128)(2,1)S(1)} async-done(((bf16[8,64,128]{2,1,0:T(8,128)(2,1)}), bf16[8,64,128]{2,1,0:T(8,128)(2,1)S(1)}, u32[]{:S(2)}, u32[]{:S(2)}) %all-to-all-start.3) | async-done | bytes 131104 | tf_op jit(solution)/shard_map/all_to_all | solution.py:40
  87.3 4.5 %all-to-all-start.1 = ((bf16[8,16,2048]{2,1,0:T(8,128)(2,1)}), bf16[8,16,2048]{2,1,0:T(8,128)(2,1)S(1)}, u32[]{:S(2)}, u32[]{:S(2)}) async-start(bf16[8,16,2048]{2,1,0:T(8,128)(2,1)} %finish.1), calls=%async_computation.1 | async-start | bytes 1048576 | tf_op jit(solution)/shard_map/all_to_all | solution.py:40
  91.8 2.4 %collective-permute-start.9 = (bf16[8,64,128]{2,1,0:T(8,128)(2,1)S(1)}, bf16[8,64,128]{2,1,0:T(8,128)(2,1)S(1)}, u32[]{:S(2)}, u32[]{:S(2)}) collective-permute-start(bf16[8,64,128]{2,1,0:T(8,128)(2,1)S(1)} %all-to-all-done.3.mixed_ref), channel_id=1, source_target_pairs={{0,3},{1,0},{2,1},{3,2},{4,7},{5,4},{6,5},{7,6},{8,11},{9,8},{10,9... | collective-permute-start | bytes 393224 | tf_op jit(solution)/shard_map/ppermute | solution.py:31
  94.1 4.5 %collective-permute-done.9.other_ref = bf16[8,64,128]{2,1,0:T(8,128)(2,1)S(1)} collective-permute-done((bf16[8,64,128]{2,1,0:T(8,128)(2,1)S(1)}, bf16[8,64,128]{2,1,0:T(8,128)(2,1)S(1)}, u32[]{:S(2)}, u32[]{:S(2)}) %collective-permute-start.9) | collective-permute-done | bytes 131104 | tf_op jit(solution)/shard_map/ppermute | solution.py:31
  98.6 3.1 %all-to-all-done.1.ret_ref = bf16[8,16,2048]{2,1,0:T(8,128)(2,1)S(1)} async-done(((bf16[8,16,2048]{2,1,0:T(8,128)(2,1)}), bf16[8,16,2048]{2,1,0:T(8,128)(2,1)S(1)}, u32[]{:S(2)}, u32[]{:S(2)}) %all-to-all-start.1) | async-done | bytes 524320 | tf_op jit(solution)/shard_map/all_to_all | solution.py:40
  (30 shorter events, 8.8 us)
Async XLA Ops:
  2.6 26.3 %all-to-all-start = ((bf16[8,16,2048]{2,1,0:T(8,128)(2,1)}), bf16[8,16,2048]{2,1,0:T(8,128)(2,1)S(1)}, u32[]{:S(2)}, u32[]{:S(2)}) async-start(bf16[8,16,2048]{2,1,0:T(8,128)(2,1)} %pack_rows.1), calls=%async_computation | async-start | bytes 1048576 | tf_op jit(solution)/shard_map/all_to_all | solution.py:40
  14.8 23.4 %collective-permute-start.7 = (bf16[96,1024]{1,0:T(8,128)(2,1)}, bf16[96,1024]{1,0:T(8,128)(2,1)S(1)}, u32[]{:S(2)}, u32[]{:S(2)}) collective-permute-start(bf16[96,1024]{1,0:T(8,128)(2,1)} %get-tuple-element.27), channel_id=1, source_target_pairs={{0,1},{1,2},{2,3},{3,0},{4,5},{5,6},{6,7},{7,4},{8,9},{9,10},{10,1... | collective-permute-start | bytes 589832 | tf_op jit(solution)/shard_map/ppermute | solution.py:27
  18.2 10.1 %collective-permute-start = (bf16[64,1024]{1,0:T(8,128)(2,1)S(1)}, bf16[64,1024]{1,0:T(8,128)(2,1)S(1)}, u32[]{:S(2)}, u32[]{:S(2)}) collective-permute-start(bf16[64,1024]{1,0:T(8,128)(2,1)S(1)} %get-tuple-element.16), channel_id=1, source_target_pairs={{0,2},{1,3},{2,0},{3,1},{4,6},{5,7},{6,4},{7,5},{8,10},{9,11},{10,... | collective-permute-start | bytes 393224 | tf_op jit(solution)/shard_map/ppermute | solution.py:35
  22.9 15.3 %collective-permute-start.8 = (bf16[64,1024]{1,0:T(8,128)(2,1)}, bf16[64,1024]{1,0:T(8,128)(2,1)}, u32[]{:S(2)}, u32[]{:S(2)}) collective-permute-start(bf16[64,1024]{1,0:T(8,128)(2,1)} %get-tuple-element.28), channel_id=1, source_target_pairs={{0,3},{1,0},{2,1},{3,2},{4,7},{5,4},{6,5},{7,6},{8,11},{9,8},{10,9... | collective-permute-start | bytes 393224 | tf_op jit(solution)/shard_map/ppermute | solution.py:31
  28.3 0.7 copy-start.2
  28.9 22.0 %collective-permute-start.3 = (bf16[128,2048]{1,0:T(8,128)(2,1)S(1)}, bf16[128,2048]{1,0:T(8,128)(2,1)}, u32[]{:S(2)}, u32[]{:S(2)}) collective-permute-start(bf16[128,2048]{1,0:T(8,128)(2,1)S(1)} %bitcast.6), channel_id=1, source_target_pairs={{0,2},{1,3},{2,0},{3,1},{4,6},{5,7},{6,4},{7,5},{8,10},{9,11},{10,... | collective-permute-start | bytes 1572872 | tf_op jit(solution)/shard_map/ppermute | solution.py:35
  32.0 25.5 %collective-permute-start.2 = (bf16[128,2048]{1,0:T(8,128)(2,1)S(1)}, bf16[128,2048]{1,0:T(8,128)(2,1)S(1)}, u32[]{:S(2)}, u32[]{:S(2)}) collective-permute-start(bf16[128,2048]{1,0:T(8,128)(2,1)S(1)} %bitcast.7), channel_id=1, source_target_pairs={{0,3},{1,0},{2,1},{3,2},{4,7},{5,4},{6,5},{7,6},{8,11},{9,8},{10,9... | collective-permute-start | bytes 1572872 | tf_op jit(solution)/shard_map/ppermute | solution.py:31
  36.3 21.2 %collective-permute-start.1 = (bf16[128,2048]{1,0:T(8,128)(2,1)S(1)}, bf16[128,2048]{1,0:T(8,128)(2,1)}, u32[]{:S(2)}, u32[]{:S(2)}) collective-permute-start(bf16[128,2048]{1,0:T(8,128)(2,1)S(1)} %bitcast.8), channel_id=1, source_target_pairs={{0,1},{1,2},{2,3},{3,0},{4,5},{5,6},{6,7},{7,4},{8,9},{9,10},{10,1... | collective-permute-start | bytes 1572872 | tf_op jit(solution)/shard_map/ppermute | solution.py:27
  38.2 0.9 copy-start.3
  41.0 26.8 %all-to-all-start.2 = ((bf16[8,320,128]{2,1,0:T(8,128)(2,1)}), bf16[8,320,128]{2,1,0:T(8,128)(2,1)}, u32[]{:S(2)}, u32[]{:S(2)}) async-start(bf16[8,320,128]{2,1,0:T(8,128)(2,1)} %pack_heads.1), calls=%async_computation.2 | async-start | bytes 1310720 | tf_op jit(solution)/shard_map/all_to_all | solution.py:40
  50.9 3.0 %copy-start.5 = (bf16[128,2048]{1,0:T(8,128)(2,1)}, bf16[128,2048]{1,0:T(8,128)(2,1)S(1)}, u32[]{:S(2)}) copy-start(bf16[128,2048]{1,0:T(8,128)(2,1)S(1)} %experts.3.own_ref) | copy-start | bytes 1572868
  53.9 13.9 %copy-start.4 = (s32[32]{0:T(128)S(1)}, s32[32]{0:T(128)}, u32[]{:S(2)}) copy-start(s32[32]{0:T(128)} %owner_ref.1) | copy-start | bytes 388
  53.9 24.3 %collective-permute-start.4 = (bf16[128,2048]{1,0:T(8,128)(2,1)}, bf16[128,2048]{1,0:T(8,128)(2,1)}, u32[]{:S(2)}, u32[]{:S(2)}) collective-permute-start(bf16[128,2048]{1,0:T(8,128)(2,1)} %experts.4), channel_id=1, source_target_pairs={{0,2},{1,3},{2,0},{3,1},{4,6},{5,7},{6,4},{7,5},{8,10},{9,11},{10,... | collective-permute-start | bytes 1572872 | tf_op jit(solution)/shard_map/ppermute | solution.py:35
  60.7 19.7 %collective-permute-start.5 = (bf16[128,2048]{1,0:T(8,128)(2,1)}, bf16[128,2048]{1,0:T(8,128)(2,1)S(1)}, u32[]{:S(2)}, u32[]{:S(2)}) collective-permute-start(bf16[128,2048]{1,0:T(8,128)(2,1)} %get-tuple-element.24), channel_id=1, source_target_pairs={{0,1},{1,2},{2,3},{3,0},{4,5},{5,6},{6,7},{7,4},{8,9},{9,10},{10,1... | collective-permute-start | bytes 1572872 | tf_op jit(solution)/shard_map/ppermute | solution.py:27
  65.1 15.3 %collective-permute-start.6 = (bf16[128,2048]{1,0:T(8,128)(2,1)S(1)}, bf16[128,2048]{1,0:T(8,128)(2,1)S(1)}, u32[]{:S(2)}, u32[]{:S(2)}) collective-permute-start(bf16[128,2048]{1,0:T(8,128)(2,1)S(1)} %get-tuple-element.25), channel_id=1, source_target_pairs={{0,3},{1,0},{2,1},{3,2},{4,7},{5,4},{6,5},{7,6},{8,11},{9,8},{10,9... | collective-permute-start | bytes 1572872 | tf_op jit(solution)/shard_map/ppermute | solution.py:31
  70.9 16.3 %all-to-all-start.3 = ((bf16[8,64,128]{2,1,0:T(8,128)(2,1)}), bf16[8,64,128]{2,1,0:T(8,128)(2,1)S(1)}, u32[]{:S(2)}, u32[]{:S(2)}) async-start(bf16[8,64,128]{2,1,0:T(8,128)(2,1)} %attend.1), calls=%async_computation.3 | async-start | bytes 262144 | tf_op jit(solution)/shard_map/all_to_all | solution.py:40
  78.2 1.0 %copy-start.6 = (bf16[128,2048]{1,0:T(8,128)(2,1)S(1)}, bf16[128,2048]{1,0:T(8,128)(2,1)}, u32[]{:S(2)}) copy-start(bf16[128,2048]{1,0:T(8,128)(2,1)} %copy-done.5) | copy-start | bytes 1572868
  80.4 21.4 %copy-start = (s32[32,2]{0,1:T(2,128)S(1)}, s32[32,2]{0,1:T(2,128)}, u32[]{:S(2)}) copy-start(s32[32,2]{0,1:T(2,128)} %param.15) | copy-start | bytes 772
  80.4 21.4 %copy-start.1 = (f32[32,2]{0,1:T(2,128)S(1)}, f32[32,2]{0,1:T(2,128)}, u32[]{:S(2)}) copy-start(f32[32,2]{0,1:T(2,128)} %param.16) | copy-start | bytes 772
  87.3 14.5 %all-to-all-start.1 = ((bf16[8,16,2048]{2,1,0:T(8,128)(2,1)}), bf16[8,16,2048]{2,1,0:T(8,128)(2,1)S(1)}, u32[]{:S(2)}, u32[]{:S(2)}) async-start(bf16[8,16,2048]{2,1,0:T(8,128)(2,1)} %finish.1), calls=%async_computation.1 | async-start | bytes 1048576 | tf_op jit(solution)/shard_map/all_to_all | solution.py:40
  91.8 6.8 %collective-permute-start.9 = (bf16[8,64,128]{2,1,0:T(8,128)(2,1)S(1)}, bf16[8,64,128]{2,1,0:T(8,128)(2,1)S(1)}, u32[]{:S(2)}, u32[]{:S(2)}) collective-permute-start(bf16[8,64,128]{2,1,0:T(8,128)(2,1)S(1)} %all-to-all-done.3.mixed_ref), channel_id=1, source_target_pairs={{0,3},{1,0},{2,1},{3,2},{4,7},{5,4},{6,5},{7,6},{8,11},{9,8},{10,9... | collective-permute-start | bytes 393224 | tf_op jit(solution)/shard_map/ppermute | solution.py:31
